TPU v7x, 512 devices: a whole 4x4x16 slice. The times are simulated.
512 devices in a mesh: gx: 8 (over y, z_hi), gy: 8 (over x, core), gz: 8 (over z_lo).
Axes of the slice: x: 4, y: 4, z: 16 (z_hi: 2, z_lo: 8; z = z_hi * 8 + z_lo), core: 2. Of those that a mesh axis runs over, the one named last changes fastest.
Arguments:
- density: bfloat16 [32, 128, 1024], P('gx', 'gy', 'gz'), may hold values from -6 to 6
- first_kernel: bfloat16 [3, 3, 3, 16, 1], replicated, may hold values from -1.75 to 1.75
- first_bias: float32 [16], replicated, may hold values from -2.5 to 2.5
- second_kernel: bfloat16 [3, 3, 3, 16, 16], replicated, may hold values from -0.4375 to 0.4375
- second_bias: float32 [16], replicated, may hold values from -2.5 to 2.5
- coarse_kernel: bfloat16 [3, 3, 3, 32, 16], replicated, may hold values from -0.4375 to 0.4375
- coarse_bias: float32 [32], replicated, may hold values from -2.5 to 2.5
- deeper_kernel: bfloat16 [3, 3, 3, 32, 32], replicated, may hold values from -0.3125 to 0.3125
- deeper_bias: float32 [32], replicated, may hold values from -2.5 to 2.5
- upward_kernel: bfloat16 [2, 2, 2, 16, 32], replicated, may hold values from -1.5 to 1.5
- upward_bias: float32 [16], replicated, may hold values from -2.5 to 2.5
- joined_kernel: bfloat16 [3, 3, 3, 16, 32], replicated, may hold values from -0.3125 to 0.3125
- joined_bias: float32 [16], replicated, may hold values from -2.5 to 2.5
- final_kernel: bfloat16 [3, 3, 3, 16, 16], replicated, may hold values from -0.4375 to 0.4375
- final_bias: float32 [16], replicated, may hold values from -2.5 to 2.5
- output_weight: bfloat16 [16], replicated, may hold values from -2 to 2
Outputs:
- predicted: float32 [32, 128, 1024], P('gx', 'gy', 'gz')
All inputs are finite; a program needn't handle non-finite values.
Results may differ from a plain program's by a relative error of at most 0.02.
Values may be sent and summed in bfloat16 or wider, within the bound.
No kernel may reach another device: no remote copies, remote signals or barrier semaphores. Data moves between devices by JAX's collectives and lax.ppermute only.
A program may use at most 128 MiB of HBM per device.

v0:
```python
import jax
import jax.numpy as jnp
from jax import lax
from jax.sharding import PartitionSpec as P

negative_slope = 0.2


def with_halo(array, sides, width):
    for axis, dim in sides:
        count, length = (lax.axis_size(axis), array.shape[dim])
        up = [(i, (i + 1) % count) for i in range(count)]
        down = [(j, i) for i, j in up]
        last = lax.slice_in_dim(array, length - width, length, axis=dim)
        initial = lax.slice_in_dim(array, 0, width, axis=dim)
        before = lax.ppermute(last, axis, up)
        after = lax.ppermute(initial, axis, down)
        array = jnp.concatenate([before, array, after], axis=dim)
    return array


def leaky_relu(values):
    return jnp.where(values > 0, values, negative_slope * values)


def convolve_local(padded, kernel, biases):
    channels = padded.shape[0]
    extent_x = padded.shape[1] - 2
    extent_y = padded.shape[2] - 2
    extent_z = padded.shape[3] - 2
    outputs = kernel.shape[3]
    summed = jnp.zeros((outputs, extent_x, extent_y, extent_z), jnp.float32)
    for step_x in range(3):
        for step_y in range(3):
            stacked = jnp.concatenate(
                [
                    padded[
                        :,
                        step_x : step_x + extent_x,
                        step_y : step_y + extent_y,
                        step_z : step_z + extent_z,
                    ]
                    for step_z in range(3)
                ],
                axis=0,
            )
            matrix = jnp.transpose(kernel[step_x, step_y], (1, 0, 2)).reshape(outputs, 3 * channels)
            summed = summed + lax.dot_general(
                matrix, stacked, (((1,), (0,)), ((), ())), preferred_element_type=jnp.float32
            )
    return leaky_relu(summed + biases[:, None, None, None]).astype(jnp.bfloat16)


def pool_max(volume):
    channels, extent_x, extent_y, extent_z = volume.shape
    grouped = volume.reshape(channels, extent_x // 2, 2, extent_y // 2, 2, extent_z // 2, 2)
    return jnp.max(grouped, axis=(2, 4, 6))


def upsample_local(coarse_field, kernel, biases):
    channels, extent_x, extent_y, extent_z = coarse_field.shape
    outputs = kernel.shape[3]
    matrix = kernel.reshape(8 * outputs, channels)
    summed = lax.dot_general(
        matrix, coarse_field, (((1,), (0,)), ((), ())), preferred_element_type=jnp.float32
    )
    summed = summed.reshape(2, 2, 2, outputs, extent_x, extent_y, extent_z)
    summed = jnp.transpose(summed, (3, 4, 0, 5, 1, 6, 2)).reshape(
        outputs, 2 * extent_x, 2 * extent_y, 2 * extent_z
    )
    return leaky_relu(summed + biases[:, None, None, None]).astype(jnp.bfloat16)


def body(
    density,
    first_kernel,
    first_bias,
    second_kernel,
    second_bias,
    coarse_kernel,
    coarse_bias,
    deeper_kernel,
    deeper_bias,
    upward_kernel,
    upward_bias,
    joined_kernel,
    joined_bias,
    final_kernel,
    final_bias,
    output_weight,
):
    volume = density[None]
    rimmed = with_halo(volume, (("gx", 1), ("gy", 2), ("gz", 3)), 1)
    first_field = convolve_local(rimmed, first_kernel, first_bias)
    first_rimmed = with_halo(first_field, (("gx", 1), ("gy", 2), ("gz", 3)), 1)
    skipped = convolve_local(first_rimmed, second_kernel, second_bias)
    pooled = pool_max(skipped)
    pooled_rimmed = with_halo(pooled, (("gx", 1), ("gy", 2), ("gz", 3)), 1)
    coarse_field = convolve_local(pooled_rimmed, coarse_kernel, coarse_bias)
    coarse_rimmed = with_halo(coarse_field, (("gx", 1), ("gy", 2), ("gz", 3)), 1)
    deeper = convolve_local(coarse_rimmed, deeper_kernel, deeper_bias)
    raised = upsample_local(deeper, upward_kernel, upward_bias)
    joined = jnp.concatenate([raised, skipped], axis=0)
    joined_rimmed = with_halo(joined, (("gx", 1), ("gy", 2), ("gz", 3)), 1)
    merged = convolve_local(joined_rimmed, joined_kernel, joined_bias)
    merged_rimmed = with_halo(merged, (("gx", 1), ("gy", 2), ("gz", 3)), 1)
    final_field = convolve_local(merged_rimmed, final_kernel, final_bias)
    flat = final_field.reshape(final_field.shape[0], -1)
    predicted = jnp.dot(output_weight[None, :], flat, preferred_element_type=jnp.float32)
    return predicted.reshape(final_field.shape[1:])


def solution(mesh):
    placed = (
        P("gx", "gy", "gz"),
        P(),
        P(),
        P(),
        P(),
        P(),
        P(),
        P(),
        P(),
        P(),
        P(),
        P(),
        P(),
        P(),
        P(),
        P(),
    )
    return jax.shard_map(
        body, mesh=mesh, in_specs=placed, out_specs=P("gx", "gy", "gz"), check_vma=False
    )
```

profile of v0, /device:TPU:6, one launch (start us, length us, event | category | flops | bytes accessed | tf_op | source)
XLA Modules:
  0.0 348.5 jit_solution(12412804096130461397)
XLA Ops:
  0.8 15.7 %collective-permute-start = (bf16[1,1,16,128]{3,0,2,1:T(2,128)(2,1)S(1)}, bf16[1,1,16,128]{3,0,2,1:T(2,128)(2,1)S(1)}, u32[]{:S(2)}, u32[]{:S(2)}) collective-permute-start(bf16[1,1,16,128]{3,0,2,1:T(2,128)(2,1)S(1)} %get-tuple-element.251), channel_id=1, source_target_pairs={{0,64},{64,128},{128,192},{192,256},{256,320},{320,384},{384,448},... | collective-permute-start | bytes 12296 | tf_op jit(solution)/shard_map/ppermute | solution.py:16
  16.5 4.4 %collective-permute-start.1 = (bf16[1,1,16,128]{3,0,2,1:T(2,128)(2,1)S(1)}, bf16[1,1,16,128]{3,0,2,1:T(2,128)(2,1)S(1)}, u32[]{:S(2)}, u32[]{:S(2)}) collective-permute-start(bf16[1,1,16,128]{3,0,2,1:T(2,128)(2,1)S(1)} %get-tuple-element.250), channel_id=1, source_target_pairs={{64,0},{128,64},{192,128},{256,192},{320,256},{384,320},{448,384},... | collective-permute-start | bytes 12296 | tf_op jit(solution)/shard_map/ppermute | solution.py:17
  21.7 9.1 %collective-permute-done.1 = bf16[1,1,16,128]{3,0,2,1:T(2,128)(2,1)S(1)} collective-permute-done((bf16[1,1,16,128]{3,0,2,1:T(2,128)(2,1)S(1)}, bf16[1,1,16,128]{3,0,2,1:T(2,128)(2,1)S(1)}, u32[]{:S(2)}, u32[]{:S(2)}) %collective-permute-start.1) | collective-permute-done | bytes 4128 | tf_op jit(solution)/shard_map/ppermute | solution.py:17
  37.1 9.5 %collective-permute-start.5 = (bf16[1,6,18,1]{3,0,2,1:T(2,128)(2,1)S(1)}, bf16[1,6,18,1]{3,0,2,1:T(2,128)(2,1)S(1)}, u32[]{:S(2)}, u32[]{:S(2)}) collective-permute-start(bf16[1,6,18,1]{3,0,2,1:T(2,128)(2,1)S(1)} %get-tuple-element.241), channel_id=1, source_target_pairs={{1,0},{2,1},{3,2},{4,3},{5,4},{6,5},{7,6},{0,7},{9,8},{10,9},{11,1... | collective-permute-start | bytes 656 | tf_op jit(solution)/shard_map/ppermute | solution.py:17
  55.6 13.3 %collective-permute-start.7 = (bf16[16,1,16,128]{3,0,2,1:T(8,128)(2,1)S(1)}, bf16[16,1,16,128]{3,0,2,1:T(8,128)(2,1)S(1)}, u32[]{:S(2)}, u32[]{:S(2)}) collective-permute-start(bf16[16,1,16,128]{3,0,2,1:T(8,128)(2,1)S(1)} %get-tuple-element.138), channel_id=1, source_target_pairs={{64,0},{128,64},{192,128},{256,192},{320,256},{384,320},{448,384},... | collective-permute-start | bytes 196616 | tf_op jit(solution)/shard_map/ppermute | solution.py:17
  76.7 13.6 %collective-permute-start.11 = (bf16[16,6,18,1]{3,0,2,1:T(8,128)(2,1)S(1)}, bf16[16,6,18,1]{3,0,2,1:T(8,128)(2,1)S(1)}, u32[]{:S(2)}, u32[]{:S(2)}) collective-permute-start(bf16[16,6,18,1]{3,0,2,1:T(8,128)(2,1)S(1)} %get-tuple-element.82), channel_id=1, source_target_pairs={{1,0},{2,1},{3,2},{4,3},{5,4},{6,5},{7,6},{0,7},{9,8},{10,9},{11,1... | collective-permute-start | bytes 10376 | tf_op jit(solution)/shard_map/ppermute | solution.py:17
  90.4 7.3 %collective-permute-done.10 = bf16[16,6,18,1]{3,0,2,1:T(8,128)(2,1)S(1)} collective-permute-done((bf16[16,6,18,1]{3,0,2,1:T(8,128)(2,1)S(1)}, bf16[16,6,18,1]{3,0,2,1:T(8,128)(2,1)S(1)}, u32[]{:S(2)}, u32[]{:S(2)}) %collective-permute-start.10) | collective-permute-done | bytes 3488 | tf_op jit(solution)/shard_map/ppermute | solution.py:16
  104.3 3.7 %reduce_max.9 = bf16[16,2,8,64]{0,3,2,1:T(8,128)(2,1)S(1)} reduce(bf16[16,2,2,8,2,64,2]{0,6,5,4,3,2,1:T(2,128)(2,1)S(1)} %bitcast.496, bf16[]{:T(256)} %constant.0.clone.1), dimensions={2,4,6}, to_apply=%region_0.1 | reduce | flops 114688 | bytes 294914 | tf_op jit(solution)/shard_map/reduce_max | solution.py:57
  108.1 13.9 %collective-permute-start.12 = (bf16[16,1,8,64]{3,0,2,1:T(8,128)(2,1)S(1)}, bf16[16,1,8,64]{3,0,2,1:T(8,128)(2,1)S(1)}, u32[]{:S(2)}, u32[]{:S(2)}) collective-permute-start(bf16[16,1,8,64]{3,0,2,1:T(8,128)(2,1)S(1)} %get-tuple-element.236), channel_id=1, source_target_pairs={{0,64},{64,128},{128,192},{192,256},{256,320},{320,384},{384,448},... | collective-permute-start | bytes 49160 | tf_op jit(solution)/shard_map/ppermute | solution.py:16
  122.1 3.5 %collective-permute-start.13 = (bf16[16,1,8,64]{3,0,2,1:T(8,128)(2,1)S(1)}, bf16[16,1,8,64]{3,0,2,1:T(8,128)(2,1)S(1)}, u32[]{:S(2)}, u32[]{:S(2)}) collective-permute-start(bf16[16,1,8,64]{3,0,2,1:T(8,128)(2,1)S(1)} %get-tuple-element.237), channel_id=1, source_target_pairs={{64,0},{128,64},{192,128},{256,192},{320,256},{384,320},{448,384},... | collective-permute-start | bytes 49160 | tf_op jit(solution)/shard_map/ppermute | solution.py:17
  125.7 11.3 %collective-permute-done.13 = bf16[16,1,8,64]{3,0,2,1:T(8,128)(2,1)S(1)} collective-permute-done((bf16[16,1,8,64]{3,0,2,1:T(8,128)(2,1)S(1)}, bf16[16,1,8,64]{3,0,2,1:T(8,128)(2,1)S(1)}, u32[]{:S(2)}, u32[]{:S(2)}) %collective-permute-start.13) | collective-permute-done | bytes 16416 | tf_op jit(solution)/shard_map/ppermute | solution.py:17
  143.2 10.4 %collective-permute-start.17 = (bf16[16,4,10,1]{3,0,2,1:T(8,128)(2,1)S(1)}, bf16[16,4,10,1]{3,0,2,1:T(8,128)(2,1)S(1)}, u32[]{:S(2)}, u32[]{:S(2)}) collective-permute-start(bf16[16,4,10,1]{3,0,2,1:T(8,128)(2,1)S(1)} %get-tuple-element.169), channel_id=1, source_target_pairs={{1,0},{2,1},{3,2},{4,3},{5,4},{6,5},{7,6},{0,7},{9,8},{10,9},{11,1... | collective-permute-start | bytes 3848 | tf_op jit(solution)/shard_map/ppermute | solution.py:17
  159.2 5.3 %collective-permute-start.18 = (bf16[32,1,8,64]{3,0,2,1:T(8,128)(2,1)S(1)}, bf16[32,1,8,64]{3,0,2,1:T(8,128)(2,1)S(1)}, u32[]{:S(2)}, u32[]{:S(2)}) collective-permute-start(bf16[32,1,8,64]{3,0,2,1:T(8,128)(2,1)S(1)} %get-tuple-element.176), channel_id=1, source_target_pairs={{0,64},{64,128},{128,192},{192,256},{256,320},{320,384},{384,448},... | collective-permute-start | bytes 98312 | tf_op jit(solution)/shard_map/ppermute | solution.py:16
  164.5 11.4 %collective-permute-start.19 = (bf16[32,1,8,64]{3,0,2,1:T(8,128)(2,1)S(1)}, bf16[32,1,8,64]{3,0,2,1:T(8,128)(2,1)S(1)}, u32[]{:S(2)}, u32[]{:S(2)}) collective-permute-start(bf16[32,1,8,64]{3,0,2,1:T(8,128)(2,1)S(1)} %get-tuple-element.177), channel_id=1, source_target_pairs={{64,0},{128,64},{192,128},{256,192},{320,256},{384,320},{448,384},... | collective-permute-start | bytes 98312 | tf_op jit(solution)/shard_map/ppermute | solution.py:17
  176.2 4.2 %collective-permute-done.19 = bf16[32,1,8,64]{3,0,2,1:T(8,128)(2,1)S(1)} collective-permute-done((bf16[32,1,8,64]{3,0,2,1:T(8,128)(2,1)S(1)}, bf16[32,1,8,64]{3,0,2,1:T(8,128)(2,1)S(1)}, u32[]{:S(2)}, u32[]{:S(2)}) %collective-permute-start.19) | collective-permute-done | bytes 32800 | tf_op jit(solution)/shard_map/ppermute | solution.py:17
  184.2 4.3 %collective-permute-start.22 = (bf16[32,4,10,1]{3,0,2,1:T(8,128)(2,1)S(1)}, bf16[32,4,10,1]{3,0,2,1:T(8,128)(2,1)S(1)}, u32[]{:S(2)}, u32[]{:S(2)}) collective-permute-start(bf16[32,4,10,1]{3,0,2,1:T(8,128)(2,1)S(1)} %get-tuple-element.123), channel_id=1, source_target_pairs={{0,1},{1,2},{2,3},{3,4},{4,5},{5,6},{6,7},{7,0},{8,9},{9,10},{10,1... | collective-permute-start | bytes 7688 | tf_op jit(solution)/shard_map/ppermute | solution.py:16
  188.5 8.6 %collective-permute-start.23 = (bf16[32,4,10,1]{3,0,2,1:T(8,128)(2,1)S(1)}, bf16[32,4,10,1]{3,0,2,1:T(8,128)(2,1)S(1)}, u32[]{:S(2)}, u32[]{:S(2)}) collective-permute-start(bf16[32,4,10,1]{3,0,2,1:T(8,128)(2,1)S(1)} %get-tuple-element.124), channel_id=1, source_target_pairs={{1,0},{2,1},{3,2},{4,3},{5,4},{6,5},{7,6},{0,7},{9,8},{10,9},{11,1... | collective-permute-start | bytes 7688 | tf_op jit(solution)/shard_map/ppermute | solution.py:17
  197.1 4.4 %collective-permute-done.22 = bf16[32,4,10,1]{3,0,2,1:T(8,128)(2,1)S(1)} collective-permute-done((bf16[32,4,10,1]{3,0,2,1:T(8,128)(2,1)S(1)}, bf16[32,4,10,1]{3,0,2,1:T(8,128)(2,1)S(1)}, u32[]{:S(2)}, u32[]{:S(2)}) %collective-permute-start.22) | collective-permute-done | bytes 2592 | tf_op jit(solution)/shard_map/ppermute | solution.py:16
  201.5 5.1 %collective-permute-done.23 = bf16[32,4,10,1]{3,0,2,1:T(8,128)(2,1)S(1)} collective-permute-done((bf16[32,4,10,1]{3,0,2,1:T(8,128)(2,1)S(1)}, bf16[32,4,10,1]{3,0,2,1:T(8,128)(2,1)S(1)}, u32[]{:S(2)}, u32[]{:S(2)}) %collective-permute-start.23) | collective-permute-done | bytes 2592 | tf_op jit(solution)/shard_map/ppermute | solution.py:17
  210.2 4.5 %copy.190 = f32[16,2,2,8,2,64,2]{0,6,5,4,3,2,1:T(2,128)} copy(f32[16,2,2,8,2,64,2]{5,3,1,0,6,4,2:T(8,128)S(1)} %bitcast.497) | data formatting | bytes 1048576 | tf_op jit(solution)/shard_map/transpose | solution.py:68
  217.7 9.1 %collective-permute-start.24 = (bf16[32,1,16,128]{3,0,2,1:T(8,128)(2,1)S(1)}, bf16[32,1,16,128]{3,0,2,1:T(8,128)(2,1)S(1)}, u32[]{:S(2)}, u32[]{:S(2)}) collective-permute-start(bf16[32,1,16,128]{3,0,2,1:T(8,128)(2,1)S(1)} %get-tuple-element.73), channel_id=1, source_target_pairs={{0,64},{64,128},{128,192},{192,256},{256,320},{320,384},{384,448},... | collective-permute-start | bytes 393224 | tf_op jit(solution)/shard_map/ppermute | solution.py:16
  226.9 7.5 %collective-permute-start.25 = (bf16[32,1,16,128]{3,0,2,1:T(8,128)(2,1)S(1)}, bf16[32,1,16,128]{3,0,2,1:T(8,128)(2,1)S(1)}, u32[]{:S(2)}, u32[]{:S(2)}) collective-permute-start(bf16[32,1,16,128]{3,0,2,1:T(8,128)(2,1)S(1)} %get-tuple-element.74), channel_id=1, source_target_pairs={{64,0},{128,64},{192,128},{256,192},{320,256},{384,320},{448,384},... | collective-permute-start | bytes 393224 | tf_op jit(solution)/shard_map/ppermute | solution.py:17
  237.2 11.8 %collective-permute-done.25 = bf16[32,1,16,128]{3,0,2,1:T(8,128)(2,1)S(1)} collective-permute-done((bf16[32,1,16,128]{3,0,2,1:T(8,128)(2,1)S(1)}, bf16[32,1,16,128]{3,0,2,1:T(8,128)(2,1)S(1)}, u32[]{:S(2)}, u32[]{:S(2)}) %collective-permute-start.25) | collective-permute-done | bytes 131104 | tf_op jit(solution)/shard_map/ppermute | solution.py:17
  253.9 9.2 %collective-permute-start.28 = (bf16[32,6,18,1]{0,2,3,1:T(8,128)(2,1)S(1)}, bf16[32,6,18,1]{0,2,3,1:T(8,128)(2,1)S(1)}, u32[]{:S(2)}, u32[]{:S(2)}) collective-permute-start(bf16[32,6,18,1]{0,2,3,1:T(8,128)(2,1)S(1)} %copy.192), channel_id=1, source_target_pairs={{0,1},{1,2},{2,3},{3,4},{4,5},{5,6},{6,7},{7,0},{8,9},{9,10},{10,1... | collective-permute-start | bytes 20744 | tf_op jit(solution)/shard_map/ppermute | solution.py:16
  264.0 6.7 %collective-permute-start.29 = (bf16[32,6,18,1]{0,2,3,1:T(8,128)(2,1)S(1)}, bf16[32,6,18,1]{0,2,3,1:T(8,128)(2,1)S(1)}, u32[]{:S(2)}, u32[]{:S(2)}) collective-permute-start(bf16[32,6,18,1]{0,2,3,1:T(8,128)(2,1)S(1)} %copy.194), channel_id=1, source_target_pairs={{1,0},{2,1},{3,2},{4,3},{5,4},{6,5},{7,6},{0,7},{9,8},{10,9},{11,1... | collective-permute-start | bytes 20744 | tf_op jit(solution)/shard_map/ppermute | solution.py:17
  286.8 10.4 %collective-permute-start.30 = (bf16[16,1,16,128]{3,0,2,1:T(8,128)(2,1)S(1)}, bf16[16,1,16,128]{3,0,2,1:T(8,128)(2,1)S(1)}, u32[]{:S(2)}, u32[]{:S(2)}) collective-permute-start(bf16[16,1,16,128]{3,0,2,1:T(8,128)(2,1)S(1)} %get-tuple-element.131), channel_id=1, source_target_pairs={{0,64},{64,128},{128,192},{192,256},{256,320},{320,384},{384,448},... | collective-permute-start | bytes 196616 | tf_op jit(solution)/shard_map/ppermute | solution.py:16
  297.2 6.5 %collective-permute-start.31 = (bf16[16,1,16,128]{3,0,2,1:T(8,128)(2,1)S(1)}, bf16[16,1,16,128]{3,0,2,1:T(8,128)(2,1)S(1)}, u32[]{:S(2)}, u32[]{:S(2)}) collective-permute-start(bf16[16,1,16,128]{3,0,2,1:T(8,128)(2,1)S(1)} %get-tuple-element.132), channel_id=1, source_target_pairs={{64,0},{128,64},{192,128},{256,192},{320,256},{384,320},{448,384},... | collective-permute-start | bytes 196616 | tf_op jit(solution)/shard_map/ppermute | solution.py:17
  303.7 8.5 %collective-permute-done.31 = bf16[16,1,16,128]{3,0,2,1:T(8,128)(2,1)S(1)} collective-permute-done((bf16[16,1,16,128]{3,0,2,1:T(8,128)(2,1)S(1)}, bf16[16,1,16,128]{3,0,2,1:T(8,128)(2,1)S(1)}, u32[]{:S(2)}, u32[]{:S(2)}) %collective-permute-start.31) | collective-permute-done | bytes 65568 | tf_op jit(solution)/shard_map/ppermute | solution.py:17
  312.3 3.5 collective-permute-start.32
  320.6 10.5 %collective-permute-start.35 = (bf16[16,6,18,1]{3,0,2,1:T(8,128)(2,1)S(1)}, bf16[16,6,18,1]{3,0,2,1:T(8,128)(2,1)S(1)}, u32[]{:S(2)}, u32[]{:S(2)}) collective-permute-start(bf16[16,6,18,1]{3,0,2,1:T(8,128)(2,1)S(1)} %get-tuple-element.78), channel_id=1, source_target_pairs={{1,0},{2,1},{3,2},{4,3},{5,4},{6,5},{7,6},{0,7},{9,8},{10,9},{11,1... | collective-permute-start | bytes 10376 | tf_op jit(solution)/shard_map/ppermute | solution.py:17
  331.2 7.3 %collective-permute-done.34 = bf16[16,6,18,1]{3,0,2,1:T(8,128)(2,1)S(1)} collective-permute-done((bf16[16,6,18,1]{3,0,2,1:T(8,128)(2,1)S(1)}, bf16[16,6,18,1]{3,0,2,1:T(8,128)(2,1)S(1)}, u32[]{:S(2)}, u32[]{:S(2)}) %collective-permute-start.34) | collective-permute-done | bytes 3488 | tf_op jit(solution)/shard_map/ppermute | solution.py:16
  338.6 4.4 %collective-permute-done.35 = bf16[16,6,18,1]{3,0,2,1:T(8,128)(2,1)S(1)} collective-permute-done((bf16[16,6,18,1]{3,0,2,1:T(8,128)(2,1)S(1)}, bf16[16,6,18,1]{3,0,2,1:T(8,128)(2,1)S(1)}, u32[]{:S(2)}, u32[]{:S(2)}) %collective-permute-start.35) | collective-permute-done | bytes 3488 | tf_op jit(solution)/shard_map/ppermute | solution.py:17
  (289 shorter events, 88.1 us)
Async XLA Ops:
  0.8 20.1 %collective-permute-start = (bf16[1,1,16,128]{3,0,2,1:T(2,128)(2,1)S(1)}, bf16[1,1,16,128]{3,0,2,1:T(2,128)(2,1)S(1)}, u32[]{:S(2)}, u32[]{:S(2)}) collective-permute-start(bf16[1,1,16,128]{3,0,2,1:T(2,128)(2,1)S(1)} %get-tuple-element.251), channel_id=1, source_target_pairs={{0,64},{64,128},{128,192},{192,256},{256,320},{320,384},{384,448},... | collective-permute-start | bytes 12296 | tf_op jit(solution)/shard_map/ppermute | solution.py:16
  16.5 14.3 %collective-permute-start.1 = (bf16[1,1,16,128]{3,0,2,1:T(2,128)(2,1)S(1)}, bf16[1,1,16,128]{3,0,2,1:T(2,128)(2,1)S(1)}, u32[]{:S(2)}, u32[]{:S(2)}) collective-permute-start(bf16[1,1,16,128]{3,0,2,1:T(2,128)(2,1)S(1)} %get-tuple-element.250), channel_id=1, source_target_pairs={{64,0},{128,64},{192,128},{256,192},{320,256},{384,320},{448,384},... | collective-permute-start | bytes 12296 | tf_op jit(solution)/shard_map/ppermute | solution.py:17
  34.1 12.7 %collective-permute-start.4 = (bf16[1,6,18,1]{3,0,2,1:T(2,128)(2,1)S(1)}, bf16[1,6,18,1]{3,0,2,1:T(2,128)(2,1)S(1)}, u32[]{:S(2)}, u32[]{:S(2)}) collective-permute-start(bf16[1,6,18,1]{3,0,2,1:T(2,128)(2,1)S(1)} %get-tuple-element.240), channel_id=1, source_target_pairs={{0,1},{1,2},{2,3},{3,4},{4,5},{5,6},{6,7},{7,0},{8,9},{9,10},{10,1... | collective-permute-start | bytes 656 | tf_op jit(solution)/shard_map/ppermute | solution.py:16
  37.1 11.3 %collective-permute-start.5 = (bf16[1,6,18,1]{3,0,2,1:T(2,128)(2,1)S(1)}, bf16[1,6,18,1]{3,0,2,1:T(2,128)(2,1)S(1)}, u32[]{:S(2)}, u32[]{:S(2)}) collective-permute-start(bf16[1,6,18,1]{3,0,2,1:T(2,128)(2,1)S(1)} %get-tuple-element.241), channel_id=1, source_target_pairs={{1,0},{2,1},{3,2},{4,3},{5,4},{6,5},{7,6},{0,7},{9,8},{10,9},{11,1... | collective-permute-start | bytes 656 | tf_op jit(solution)/shard_map/ppermute | solution.py:17
  52.2 17.9 %collective-permute-start.6 = (bf16[16,1,16,128]{3,0,2,1:T(8,128)(2,1)S(1)}, bf16[16,1,16,128]{3,0,2,1:T(8,128)(2,1)S(1)}, u32[]{:S(2)}, u32[]{:S(2)}) collective-permute-start(bf16[16,1,16,128]{3,0,2,1:T(8,128)(2,1)S(1)} %get-tuple-element.137), channel_id=1, source_target_pairs={{0,64},{64,128},{128,192},{192,256},{256,320},{320,384},{384,448},... | collective-permute-start | bytes 196616 | tf_op jit(solution)/shard_map/ppermute | solution.py:16
  55.6 15.4 %collective-permute-start.7 = (bf16[16,1,16,128]{3,0,2,1:T(8,128)(2,1)S(1)}, bf16[16,1,16,128]{3,0,2,1:T(8,128)(2,1)S(1)}, u32[]{:S(2)}, u32[]{:S(2)}) collective-permute-start(bf16[16,1,16,128]{3,0,2,1:T(8,128)(2,1)S(1)} %get-tuple-element.138), channel_id=1, source_target_pairs={{64,0},{128,64},{192,128},{256,192},{320,256},{384,320},{448,384},... | collective-permute-start | bytes 196616 | tf_op jit(solution)/shard_map/ppermute | solution.py:17
  71.0 3.3 collective-permute-start.8
  71.0 3.3 collective-permute-start.9
  74.8 22.9 %collective-permute-start.10 = (bf16[16,6,18,1]{3,0,2,1:T(8,128)(2,1)S(1)}, bf16[16,6,18,1]{3,0,2,1:T(8,128)(2,1)S(1)}, u32[]{:S(2)}, u32[]{:S(2)}) collective-permute-start(bf16[16,6,18,1]{3,0,2,1:T(8,128)(2,1)S(1)} %get-tuple-element.81), channel_id=1, source_target_pairs={{0,1},{1,2},{2,3},{3,4},{4,5},{5,6},{6,7},{7,0},{8,9},{9,10},{10,1... | collective-permute-start | bytes 10376 | tf_op jit(solution)/shard_map/ppermute | solution.py:16
  76.7 22.3 %collective-permute-start.11 = (bf16[16,6,18,1]{3,0,2,1:T(8,128)(2,1)S(1)}, bf16[16,6,18,1]{3,0,2,1:T(8,128)(2,1)S(1)}, u32[]{:S(2)}, u32[]{:S(2)}) collective-permute-start(bf16[16,6,18,1]{3,0,2,1:T(8,128)(2,1)S(1)} %get-tuple-element.82), channel_id=1, source_target_pairs={{1,0},{2,1},{3,2},{4,3},{5,4},{6,5},{7,6},{0,7},{9,8},{10,9},{11,1... | collective-permute-start | bytes 10376 | tf_op jit(solution)/shard_map/ppermute | solution.py:17
  108.1 17.5 %collective-permute-start.12 = (bf16[16,1,8,64]{3,0,2,1:T(8,128)(2,1)S(1)}, bf16[16,1,8,64]{3,0,2,1:T(8,128)(2,1)S(1)}, u32[]{:S(2)}, u32[]{:S(2)}) collective-permute-start(bf16[16,1,8,64]{3,0,2,1:T(8,128)(2,1)S(1)} %get-tuple-element.236), channel_id=1, source_target_pairs={{0,64},{64,128},{128,192},{192,256},{256,320},{320,384},{384,448},... | collective-permute-start | bytes 49160 | tf_op jit(solution)/shard_map/ppermute | solution.py:16
  122.1 14.9 %collective-permute-start.13 = (bf16[16,1,8,64]{3,0,2,1:T(8,128)(2,1)S(1)}, bf16[16,1,8,64]{3,0,2,1:T(8,128)(2,1)S(1)}, u32[]{:S(2)}, u32[]{:S(2)}) collective-permute-start(bf16[16,1,8,64]{3,0,2,1:T(8,128)(2,1)S(1)} %get-tuple-element.237), channel_id=1, source_target_pairs={{64,0},{128,64},{192,128},{256,192},{320,256},{384,320},{448,384},... | collective-permute-start | bytes 49160 | tf_op jit(solution)/shard_map/ppermute | solution.py:17
  137.1 3.8 %collective-permute-start.15 = (bf16[16,4,1,64]{3,0,2,1:T(8,128)(2,1)S(1)}, bf16[16,4,1,64]{3,0,2,1:T(8,128)(2,1)S(1)}, u32[]{:S(2)}, u32[]{:S(2)}) collective-permute-start(bf16[16,4,1,64]{3,0,2,1:T(8,128)(2,1)S(1)} %get-tuple-element.181), channel_id=1, source_target_pairs={{8,0},{16,8},{24,16},{32,24},{40,32},{48,40},{56,48},{0,56},{9,1},... | collective-permute-start | bytes 24584 | tf_op jit(solution)/shard_map/ppermute | solution.py:17
  141.2 14.1 %collective-permute-start.16 = (bf16[16,4,10,1]{3,0,2,1:T(8,128)(2,1)S(1)}, bf16[16,4,10,1]{3,0,2,1:T(8,128)(2,1)S(1)}, u32[]{:S(2)}, u32[]{:S(2)}) collective-permute-start(bf16[16,4,10,1]{3,0,2,1:T(8,128)(2,1)S(1)} %get-tuple-element.168), channel_id=1, source_target_pairs={{0,1},{1,2},{2,3},{3,4},{4,5},{5,6},{6,7},{7,0},{8,9},{9,10},{10,1... | collective-permute-start | bytes 3848 | tf_op jit(solution)/shard_map/ppermute | solution.py:16
  143.2 13.2 %collective-permute-start.17 = (bf16[16,4,10,1]{3,0,2,1:T(8,128)(2,1)S(1)}, bf16[16,4,10,1]{3,0,2,1:T(8,128)(2,1)S(1)}, u32[]{:S(2)}, u32[]{:S(2)}) collective-permute-start(bf16[16,4,10,1]{3,0,2,1:T(8,128)(2,1)S(1)} %get-tuple-element.169), channel_id=1, source_target_pairs={{1,0},{2,1},{3,2},{4,3},{5,4},{6,5},{7,6},{0,7},{9,8},{10,9},{11,1... | collective-permute-start | bytes 3848 | tf_op jit(solution)/shard_map/ppermute | solution.py:17
  159.2 17.0 %collective-permute-start.18 = (bf16[32,1,8,64]{3,0,2,1:T(8,128)(2,1)S(1)}, bf16[32,1,8,64]{3,0,2,1:T(8,128)(2,1)S(1)}, u32[]{:S(2)}, u32[]{:S(2)}) collective-permute-start(bf16[32,1,8,64]{3,0,2,1:T(8,128)(2,1)S(1)} %get-tuple-element.176), channel_id=1, source_target_pairs={{0,64},{64,128},{128,192},{192,256},{256,320},{320,384},{384,448},... | collective-permute-start | bytes 98312 | tf_op jit(solution)/shard_map/ppermute | solution.py:16
  164.5 15.9 %collective-permute-start.19 = (bf16[32,1,8,64]{3,0,2,1:T(8,128)(2,1)S(1)}, bf16[32,1,8,64]{3,0,2,1:T(8,128)(2,1)S(1)}, u32[]{:S(2)}, u32[]{:S(2)}) collective-permute-start(bf16[32,1,8,64]{3,0,2,1:T(8,128)(2,1)S(1)} %get-tuple-element.177), channel_id=1, source_target_pairs={{64,0},{128,64},{192,128},{256,192},{320,256},{384,320},{448,384},... | collective-permute-start | bytes 98312 | tf_op jit(solution)/shard_map/ppermute | solution.py:17
  180.4 3.4 collective-permute-start.20
  180.4 3.3 collective-permute-start.21
  184.2 17.3 %collective-permute-start.22 = (bf16[32,4,10,1]{3,0,2,1:T(8,128)(2,1)S(1)}, bf16[32,4,10,1]{3,0,2,1:T(8,128)(2,1)S(1)}, u32[]{:S(2)}, u32[]{:S(2)}) collective-permute-start(bf16[32,4,10,1]{3,0,2,1:T(8,128)(2,1)S(1)} %get-tuple-element.123), channel_id=1, source_target_pairs={{0,1},{1,2},{2,3},{3,4},{4,5},{5,6},{6,7},{7,0},{8,9},{9,10},{10,1... | collective-permute-start | bytes 7688 | tf_op jit(solution)/shard_map/ppermute | solution.py:16
  188.5 18.2 %collective-permute-start.23 = (bf16[32,4,10,1]{3,0,2,1:T(8,128)(2,1)S(1)}, bf16[32,4,10,1]{3,0,2,1:T(8,128)(2,1)S(1)}, u32[]{:S(2)}, u32[]{:S(2)}) collective-permute-start(bf16[32,4,10,1]{3,0,2,1:T(8,128)(2,1)S(1)} %get-tuple-element.124), channel_id=1, source_target_pairs={{1,0},{2,1},{3,2},{4,3},{5,4},{6,5},{7,6},{0,7},{9,8},{10,9},{11,1... | collective-permute-start | bytes 7688 | tf_op jit(solution)/shard_map/ppermute | solution.py:17
  217.7 19.4 %collective-permute-start.24 = (bf16[32,1,16,128]{3,0,2,1:T(8,128)(2,1)S(1)}, bf16[32,1,16,128]{3,0,2,1:T(8,128)(2,1)S(1)}, u32[]{:S(2)}, u32[]{:S(2)}) collective-permute-start(bf16[32,1,16,128]{3,0,2,1:T(8,128)(2,1)S(1)} %get-tuple-element.73), channel_id=1, source_target_pairs={{0,64},{64,128},{128,192},{192,256},{256,320},{320,384},{384,448},... | collective-permute-start | bytes 393224 | tf_op jit(solution)/shard_map/ppermute | solution.py:16
  226.9 22.1 %collective-permute-start.25 = (bf16[32,1,16,128]{3,0,2,1:T(8,128)(2,1)S(1)}, bf16[32,1,16,128]{3,0,2,1:T(8,128)(2,1)S(1)}, u32[]{:S(2)}, u32[]{:S(2)}) collective-permute-start(bf16[32,1,16,128]{3,0,2,1:T(8,128)(2,1)S(1)} %get-tuple-element.74), channel_id=1, source_target_pairs={{64,0},{128,64},{192,128},{256,192},{320,256},{384,320},{448,384},... | collective-permute-start | bytes 393224 | tf_op jit(solution)/shard_map/ppermute | solution.py:17
  249.0 3.5 %collective-permute-start.26 = (bf16[32,6,1,128]{3,0,2,1:T(8,128)(2,1)S(1)}, bf16[32,6,1,128]{3,0,2,1:T(8,128)(2,1)S(1)}, u32[]{:S(2)}, u32[]{:S(2)}) collective-permute-start(bf16[32,6,1,128]{3,0,2,1:T(8,128)(2,1)S(1)} %get-tuple-element.71), channel_id=1, source_target_pairs={{0,8},{8,16},{16,24},{24,32},{32,40},{40,48},{48,56},{56,0},{1,9},... | collective-permute-start | bytes 147464 | tf_op jit(solution)/shard_map/ppermute | solution.py:16
  249.0 3.5 %collective-permute-start.27 = (bf16[32,6,1,128]{3,0,2,1:T(8,128)(2,1)S(1)}, bf16[32,6,1,128]{3,0,2,1:T(8,128)(2,1)S(1)}, u32[]{:S(2)}, u32[]{:S(2)}) collective-permute-start(bf16[32,6,1,128]{3,0,2,1:T(8,128)(2,1)S(1)} %get-tuple-element.72), channel_id=1, source_target_pairs={{8,0},{16,8},{24,16},{32,24},{40,32},{48,40},{56,48},{0,56},{9,1},... | collective-permute-start | bytes 147464 | tf_op jit(solution)/shard_map/ppermute | solution.py:17
  253.9 19.6 %collective-permute-start.28 = (bf16[32,6,18,1]{0,2,3,1:T(8,128)(2,1)S(1)}, bf16[32,6,18,1]{0,2,3,1:T(8,128)(2,1)S(1)}, u32[]{:S(2)}, u32[]{:S(2)}) collective-permute-start(bf16[32,6,18,1]{0,2,3,1:T(8,128)(2,1)S(1)} %copy.192), channel_id=1, source_target_pairs={{0,1},{1,2},{2,3},{3,4},{4,5},{5,6},{6,7},{7,0},{8,9},{9,10},{10,1... | collective-permute-start | bytes 20744 | tf_op jit(solution)/shard_map/ppermute | solution.py:16
  264.0 10.2 %collective-permute-start.29 = (bf16[32,6,18,1]{0,2,3,1:T(8,128)(2,1)S(1)}, bf16[32,6,18,1]{0,2,3,1:T(8,128)(2,1)S(1)}, u32[]{:S(2)}, u32[]{:S(2)}) collective-permute-start(bf16[32,6,18,1]{0,2,3,1:T(8,128)(2,1)S(1)} %copy.194), channel_id=1, source_target_pairs={{1,0},{2,1},{3,2},{4,3},{5,4},{6,5},{7,6},{0,7},{9,8},{10,9},{11,1... | collective-permute-start | bytes 20744 | tf_op jit(solution)/shard_map/ppermute | solution.py:17
  286.8 17.0 %collective-permute-start.30 = (bf16[16,1,16,128]{3,0,2,1:T(8,128)(2,1)S(1)}, bf16[16,1,16,128]{3,0,2,1:T(8,128)(2,1)S(1)}, u32[]{:S(2)}, u32[]{:S(2)}) collective-permute-start(bf16[16,1,16,128]{3,0,2,1:T(8,128)(2,1)S(1)} %get-tuple-element.131), channel_id=1, source_target_pairs={{0,64},{64,128},{128,192},{192,256},{256,320},{320,384},{384,448},... | collective-permute-start | bytes 196616 | tf_op jit(solution)/shard_map/ppermute | solution.py:16
  297.2 15.1 %collective-permute-start.31 = (bf16[16,1,16,128]{3,0,2,1:T(8,128)(2,1)S(1)}, bf16[16,1,16,128]{3,0,2,1:T(8,128)(2,1)S(1)}, u32[]{:S(2)}, u32[]{:S(2)}) collective-permute-start(bf16[16,1,16,128]{3,0,2,1:T(8,128)(2,1)S(1)} %get-tuple-element.132), channel_id=1, source_target_pairs={{64,0},{128,64},{192,128},{256,192},{320,256},{384,320},{448,384},... | collective-permute-start | bytes 196616 | tf_op jit(solution)/shard_map/ppermute | solution.py:17
  312.3 5.8 %collective-permute-start.32 = (bf16[16,6,1,128]{3,0,2,1:T(8,128)(2,1)S(1)}, bf16[16,6,1,128]{3,0,2,1:T(8,128)(2,1)S(1)}, u32[]{:S(2)}, u32[]{:S(2)}) collective-permute-start(bf16[16,6,1,128]{3,0,2,1:T(8,128)(2,1)S(1)} %get-tuple-element.97), channel_id=1, source_target_pairs={{0,8},{8,16},{16,24},{24,32},{32,40},{40,48},{48,56},{56,0},{1,9},... | collective-permute-start | bytes 73736 | tf_op jit(solution)/shard_map/ppermute | solution.py:16
  318.6 19.9 %collective-permute-start.34 = (bf16[16,6,18,1]{3,0,2,1:T(8,128)(2,1)S(1)}, bf16[16,6,18,1]{3,0,2,1:T(8,128)(2,1)S(1)}, u32[]{:S(2)}, u32[]{:S(2)}) collective-permute-start(bf16[16,6,18,1]{3,0,2,1:T(8,128)(2,1)S(1)} %get-tuple-element.77), channel_id=1, source_target_pairs={{0,1},{1,2},{2,3},{3,4},{4,5},{5,6},{6,7},{7,0},{8,9},{9,10},{10,1... | collective-permute-start | bytes 10376 | tf_op jit(solution)/shard_map/ppermute | solution.py:16
  320.6 22.4 %collective-permute-start.35 = (bf16[16,6,18,1]{3,0,2,1:T(8,128)(2,1)S(1)}, bf16[16,6,18,1]{3,0,2,1:T(8,128)(2,1)S(1)}, u32[]{:S(2)}, u32[]{:S(2)}) collective-permute-start(bf16[16,6,18,1]{3,0,2,1:T(8,128)(2,1)S(1)} %get-tuple-element.78), channel_id=1, source_target_pairs={{1,0},{2,1},{3,2},{4,3},{5,4},{6,5},{7,6},{0,7},{9,8},{10,9},{11,1... | collective-permute-start | bytes 10376 | tf_op jit(solution)/shard_map/ppermute | solution.py:17
  (25 other events, 428.4 us)
where the time goes:
time: 355 us; the launch traced here: 348 us
  starting transfers between devices  199 us (56%)
  waiting for transfers between devices  90.6 us (26%)
  local copies, waits for them, and re-layouts  32.8 us (9%)
  matrix products  15 us (4%)
  other arithmetic  9.65 us (3%)
    ppermute x18, starting transfers between devices, with_halo(): after = lax.ppermute(initial, axis, down)  115 us
    ppermute x18, starting transfers between devices, with_halo(): before = lax.ppermute(last, axis, up)  83.8 us
    ppermute x18, waiting for transfers between devices, with_halo(): after = lax.ppermute(initial, axis, down)  60.3 us
    ppermute x18, waiting for transfers between devices, with_halo(): before = lax.ppermute(last, axis, up)  30.3 us
    dot_general x53, matrix products, convolve_local(): lax.dot_general(matrix, stacked, (((1,), (0,)), ((), ())), preferred_elem...  13.7 us
    slice x21, local copies, waits for them, and re-layouts, convolve_local(): padded[:, step_x:step_x + extent_x, step_y:step_y + extent_y, step_z:step...  9.09 us
  transfers between devices with their start and end apart: 36, of which 26 were waited for; matrix products, arithmetic and copies ran while one was open for 3% of the time, Pallas kernels for 0%

commit v1 on v0

v1 whole, which is shorter than its diff:
```python
import functools

import jax
import jax.numpy as jnp
from jax import lax
from jax.experimental import pallas as pl
from jax.experimental.pallas import tpu as pltpu
from jax.sharding import PartitionSpec as P

F32 = jnp.float32
BF16 = jnp.bfloat16
ROW = 72
WIDTH = 16 * ROW
INNER = slice(128, 1024)


def leaky(values):
    return jnp.maximum(values, 0.2 * values)


def iota(shape, dim):
    return lax.broadcasted_iota(jnp.int32, shape, dim)


def spread_bias(bias_ref, rows):
    count = bias_ref.shape[1]
    match = iota((rows, count), 0) % count == iota((rows, count), 1)
    return jnp.broadcast_to(jnp.sum(jnp.where(match, bias_ref[...], 0.0), axis=1, keepdims=True), (rows, 128))


def weights_kernel(half_ref, first_ref, second_ref, coarse_ref, deeper_ref, joined_ref, final_ref, upward_ref, output_ref,
                   b1_ref, b2_ref, b4_ref, b5_ref, b6_ref, b7_ref, b8_ref,
                   w1_ref, w2_ref, w4_ref, w5_ref, w7_ref, w8_ref, sz_ref, w6_ref, w9_ref, bias_ref,
                   fine_ref, joint_ref, coarse_base_ref, deeper_base_ref):
    tap = iota((27, 256), 0)
    lane = iota((27, 256), 1)
    place = (tap % 3) * 64 + (tap // 3 % 3) * 16 + tap // 9
    base = lax.dot_general(first_ref[...], (place == lane).astype(BF16), (((0,), (0,)), ((), ())),
                           preferred_element_type=F32)
    base = jnp.where(half_ref[0] == 0, base, pltpu.roll(base, 4, 1))
    old = iota((256, 256), 0)
    new = iota((256, 256), 1)
    order = (old % 16 // 8) * 128 + (old // 16 % 4) * 32 + (old // 64) * 8 + old % 8
    permute = (order == new).astype(BF16)
    for x in range(8):
        rows = jnp.concatenate(
            [pltpu.roll(base, x + 16 * b + 64 * e, 1) if x + b + e else base for b in range(2) for e in range(2)], axis=0)
        w1_ref[64 * x:64 * x + 64] = jnp.dot(rows.astype(BF16), permute, preferred_element_type=F32).astype(BF16)

    for source, target in ((second_ref, w2_ref), (final_ref, w8_ref)):
        fine_ref[...] = jnp.zeros_like(fine_ref)
        for t in range(27):
            at = (t // 3 % 3) * 64 + (t % 3) * 16
            fine_ref[16 * (t // 9):16 * (t // 9) + 16, at:at + 16] = source[16 * t:16 * t + 16].astype(F32)
        for u in range(3):
            block = fine_ref[16 * u:16 * u + 16]
            for n in range(4):
                move = (n // 2) * 64 + (n % 2) * 16
                at = 64 * u + 16 * n
                target[at:at + 16] = (pltpu.roll(block, move, 1) if n else block).astype(BF16)

    joint_ref[...] = jnp.zeros_like(joint_ref)
    for t in range(27):
        piece = joined_ref[16 * t:16 * t + 16].astype(F32)
        for side in range(2):
            at = side * 256 + (t // 3 % 3) * 64 + (t % 3) * 16
            joint_ref[16 * (t // 9):16 * (t // 9) + 16, at:at + 16] = piece[:, 16 * side:16 * side + 16]
    for u in range(3):
        block = joint_ref[16 * u:16 * u + 16]
        for n in range(4):
            move = (n // 2) * 64 + (n % 2) * 16
            at = 64 * u + 16 * n
            w7_ref[at:at + 16] = (pltpu.roll(block, move, 1) if n else block).astype(BF16)

    for source, scratch, target, width, count in (
        (coarse_ref, coarse_base_ref, w4_ref, 16, 3), (deeper_ref, deeper_base_ref, w5_ref, 32, 4)):
        scratch[...] = jnp.zeros_like(scratch)
        for t in range(27):
            scratch[:, width * t:width * t + width] = source[32 * t:32 * t + 32].astype(F32)
        block = scratch[...]
        for p in range(count):
            target[32 * p:32 * p + 32] = (pltpu.roll(block, 9 * width * p, 1) if p else block).astype(BF16)

    row = iota((256, 512), 0)
    col = iota((256, 512), 1)
    cell = jnp.where(row < 128, row + 8, jnp.where(row < 136, row - 128, row))
    sz_ref[...] = ((cell == 2 * (col % 128) + col // 128 - 1) & (row < 144)).astype(BF16)

    w6_ref[...] = upward_ref[...]
    spread = (iota((16, 64), 0) == iota((16, 64), 1) % 16).astype(BF16)
    row_weights = jnp.dot(output_ref[...], spread, preferred_element_type=F32)
    row = iota((8, 64), 0)
    group = iota((8, 64), 1) // 16
    chosen = (row % 2 == group // 2) & (row // 2 == group % 2)
    w9_ref[...] = jnp.where(chosen, row_weights, 0.0)
    for n, ref in enumerate((b1_ref, b2_ref, b6_ref, b7_ref, b8_ref, b4_ref, b5_ref)):
        bias_ref[n] = spread_bias(ref, 64)


def prepare_weights(half, *parameters):
    shapes = [(512, 256), (192, 256), (96, 768), (128, 1792), (192, 512), (192, 256), (256, 512), (128, 32)]
    vmem = pl.BlockSpec(memory_space=pltpu.VMEM)
    return pl.pallas_call(
        weights_kernel,
        out_shape=[jax.ShapeDtypeStruct(s, BF16) for s in shapes]
        + [jax.ShapeDtypeStruct((8, 64), F32), jax.ShapeDtypeStruct((7, 64, 128), F32)],
        in_specs=[pl.BlockSpec(memory_space=pltpu.SMEM)] + [vmem] * len(parameters),
        out_specs=[vmem] * 10,
        scratch_shapes=[pltpu.VMEM((48, 256), F32), pltpu.VMEM((48, 512), F32),
                        pltpu.VMEM((32, 768), F32), pltpu.VMEM((32, 1792), F32)],
        compiler_params=pltpu.CompilerParams(vmem_limit_bytes=24 * 2**20),
        cost_estimate=pl.CostEstimate(flops=10**7, bytes_accessed=2 * 10**6, transcendentals=0),
        name="weights",
    )(half, *parameters)


def collect(low_ref, a_ref, mid_ref, b_ref, high_ref, all_ref):
    for g, ref in enumerate((a_ref, mid_ref, b_ref)):
        for x in range(8):
            at = 32 * (8 * g + x)
            all_ref[at:at + 8] = low_ref[8 * g + x].astype(F32)
            all_ref[at + 8:at + 24] = ref[x].astype(F32)
            all_ref[at + 24:at + 32] = high_ref[8 * g + x].astype(F32)


def edges_kernel(odd_ref, low_ref, a_ref, mid_ref, b_ref, high_ref, edge_a_ref, edge_b_ref, all_ref):
    collect(low_ref, a_ref, mid_ref, b_ref, high_ref, all_ref)
    left = jnp.zeros((48, 128), F32)
    right = jnp.zeros((48, 128), F32)
    lane = iota((48, 128), 1)
    for k in range(16):
        rows = all_ref[48 * k:48 * k + 48]
        inside = (lane >= 8 * k) & (lane < 8 * k + 8)
        left = jnp.where(inside, pltpu.roll(rows, 8 * k, 1) if k else rows, left)
        right = jnp.where(inside, pltpu.roll(rows, (8 * k + 8) % 128, 1) if k < 15 else rows, right)
    odd = odd_ref[1] == 1
    edge_a_ref[...] = jnp.where(odd, right, left).astype(BF16)
    edge_b_ref[...] = jnp.where(odd, left, right).astype(BF16)


def pack_edges(odd, *pieces):
    vmem = pl.BlockSpec(memory_space=pltpu.VMEM)
    return pl.pallas_call(
        edges_kernel,
        out_shape=[jax.ShapeDtypeStruct((48, 128), BF16)] * 2,
        in_specs=[pl.BlockSpec(memory_space=pltpu.SMEM)] + [vmem] * 5,
        out_specs=[vmem] * 2,
        scratch_shapes=[pltpu.VMEM((768, 128), F32)],
        compiler_params=pltpu.CompilerParams(vmem_limit_bytes=8 * 2**20),
        name="edges",
    )(odd, *pieces)


def chunks(width):
    return [slice(at, min(at + 256, width)) for at in range(0, width, 256)]


def moved(values, step):
    return pltpu.roll(values, step % values.shape[1], 1)


def window(values):
    rows = []
    for b in range(2):
        even = values[32 * b:32 * b + 16]
        odd = values[32 * b + 16:32 * b + 32]
        rows.append(jnp.concatenate([moved(odd, 1), even, odd, moved(even, -1)], axis=0))
    return jnp.concatenate([moved(rows[1], ROW), rows[0], rows[1], moved(rows[0], -ROW)], axis=0)


def neighbours(values):
    rows = jnp.concatenate([moved(values, 1), values, moved(values, -1)], axis=0)
    return jnp.concatenate([moved(rows, ROW), rows, moved(rows, -ROW)], axis=0)


def two_planes(sums_a, sums_b, acc_ref, part):
    done_a = acc_ref[1, :, part] + sums_a[128:192]
    done_b = acc_ref[0, :, part] + sums_a[64:128] + sums_b[128:192]
    acc_ref[1, :, part] = sums_a[0:64] + sums_b[64:128]
    acc_ref[0, :, part] = sums_b[0:64]
    return done_a, done_b


def paired_dots(w_ref, ref_a, ref_b, width):
    whole = width // 256 * 256
    for at in range(0, whole, 256):
        part = slice(at, at + 256)
        yield part, [jnp.dot(w_ref[...], ref[:, part], preferred_element_type=F32) for ref in (ref_a, ref_b)]
    if whole < width:
        part = slice(whole, width)
        both = jnp.dot(w_ref[...], jnp.concatenate([ref_a[:, part], ref_b[:, part]], axis=1), preferred_element_type=F32)
        yield part, [both[:, 0:width - whole], both[:, width - whole:]]


def wide(bias, values):
    rows, columns = values.shape
    bias = jnp.concatenate([bias] * (columns // 128), axis=1) if columns > 128 else bias
    return jnp.concatenate([bias] * (rows // bias.shape[0]), axis=0) if rows > bias.shape[0] else bias


def network_kernel(odd_ref, low_ref, a_ref, mid_ref, b_ref, high_ref, edge_a_ref, edge_b_ref,
                   w1_ref, w2_ref, w4_ref, w5_ref, w7_ref, w8_ref, sz_ref, w6_ref, w9_ref, bias_ref,
                   out_ref,
                   cells_ref, rim_ref, sampled_ref, phase_ref, col0_ref, first_ref, slot_a_ref, slot_b_ref, acc_ref,
                   skip_ref, pool_ref, col4_ref, col5_ref, col7_ref, col8_ref, flat_ref, last_ref):
    collect(low_ref, a_ref, mid_ref, b_ref, high_ref, cells_ref)
    rim_ref[...] = jnp.zeros_like(rim_ref)
    edge_a = edge_a_ref[...].astype(F32)
    edge_b = edge_b_ref[...].astype(F32)
    odd = odd_ref[1] == 1
    left = jnp.where(odd, edge_b, edge_a)
    right = jnp.where(odd, edge_a, edge_b)
    for k in range(16):
        rim_ref[48 * k:48 * k + 48, 0:8] = left[:, 8 * k:8 * k + 8]
        rim_ref[48 * k:48 * k + 48, 8:16] = right[:, 8 * k:8 * k + 8]
    for at in range(0, 768, 256):
        rows = jnp.concatenate([cells_ref[at:at + 256], rim_ref[at:at + 256]], axis=1).astype(BF16)
        sampled = jnp.dot(rows, sz_ref[...], preferred_element_type=F32)
        for w in range(4):
            sampled_ref[w, at:at + 256] = sampled[:, 128 * w:128 * w + 128]

    order = (2 - 2 * odd_ref[0], 1, 2 * odd_ref[0])
    for y in range(32):
        for w in range(4):
            column_of_x = sampled_ref.at[w][pl.ds(y, 24, stride=32), :]
            for g in range(3):
                phase_ref[3 * (y % 2) + order[g], 8 * w:8 * w + 8, ROW * (y // 2):ROW * (y // 2) + ROW] = column_of_x[
                    8 * g:8 * g + 8, 0:ROW]
    for g in range(3):
        even = phase_ref[g].astype(BF16)
        odd = phase_ref[3 + g].astype(BF16)
        col0_ref[128 * g:128 * g + 128] = jnp.concatenate([moved(odd, ROW), even, odd, moved(even, -ROW)], axis=0)

    bias = bias_ref[0]
    w1_first_ref = w1_ref.at[0:128, 0:128]
    for part, sums in paired_dots(w1_ref, col0_ref.at[0:256], col0_ref.at[128:384], WIDTH):
        for g in range(2):
            values = leaky(sums[g] + wide(bias, sums[g])).astype(BF16)
            first_ref[8 * g:8 * g + 8, :, part] = values.reshape(8, 64, values.shape[1])
    for part in chunks(WIDTH):
        sums = jnp.dot(w1_first_ref[...], col0_ref[256:384, part], preferred_element_type=F32)
        values = leaky(sums + wide(bias, sums)).astype(BF16)
        first_ref[16:18, :, part] = values.reshape(2, 64, values.shape[1])

    bias_second = bias_ref[1]

    def gather_first(j, slot_ref):
        for a in range(2):
            slot_ref[a] = window(first_ref[2 * j + a])

    def skipped_planes(j, slot_ref):
        for part, sums in paired_dots(w2_ref, slot_ref.at[0], slot_ref.at[1], WIDTH):
            top = None
            for a, done in enumerate(two_planes(*sums, acc_ref, part)):
                values = leaky(done + wide(bias_second, done))
                skip_ref[j, 64 * a:64 * a + 64, part] = values.astype(BF16)
                highest = jnp.max(values.reshape(4, 16, values.shape[1]), axis=0)
                top = highest if top is None else jnp.maximum(top, highest)
            pool_ref[j, :, part] = top.astype(BF16)

    gather_first(0, slot_a_ref)

    def two_steps(t, carry):
        gather_first(2 * t + 1, slot_b_ref)
        skipped_planes(2 * t, slot_a_ref)
        gather_first(2 * t + 2, slot_a_ref)
        skipped_planes(2 * t + 1, slot_b_ref)
        return carry

    lax.fori_loop(0, 4, two_steps, 0)
    skipped_planes(8, slot_a_ref)

    for s in range(8):
        col4_ref[144 * s:144 * s + 144] = neighbours(pool_ref[s + 1])[:, INNER]
    col4_ref[1152:1200] = jnp.zeros((48, 896), BF16)
    for d in range(4):
        for a in range(2):
            col7_ref[2 * d + a, 256:512] = window(skip_ref[d + 3, 64 * a:64 * a + 64])[:, INNER]
    bias_coarse = bias_ref[5, 0:32]
    parts = [[], []]
    for _, sums in paired_dots(w4_ref, col4_ref.at[0:768], col4_ref.at[432:1200], 896):
        for m in range(2):
            parts[m].append(leaky(sums[m] + wide(bias_coarse, sums[m])).astype(BF16))
    for m in range(2):
        values = jnp.concatenate(parts[m], axis=1)
        for p in range(3):
            at = 288 * (3 * m + p)
            col5_ref[at:at + 288] = neighbours(values[32 * p:32 * p + 32])
    col5_ref[1728:1792] = jnp.zeros((64, 896), BF16)

    bias_deeper = bias_ref[6, 0:32]
    bias_raised = bias_ref[2]
    parts = []
    for part in chunks(896):
        sums = jnp.dot(w5_ref[...], col5_ref[:, part], preferred_element_type=F32)
        parts.append(leaky(sums + wide(bias_deeper, sums)).astype(BF16))
    deeper = jnp.concatenate(parts, axis=1)
    for d in range(4):
        parts = []
        for part in chunks(896):
            sums = jnp.dot(w6_ref[...], deeper[32 * d:32 * d + 32, part], preferred_element_type=F32)
            parts.append(leaky(sums + wide(bias_raised, sums)).astype(BF16))
        values = jnp.concatenate(parts, axis=1)
        for a in range(2):
            col7_ref[2 * d + a, 0:256] = window(values[64 * a:64 * a + 64])

    bias_joined = bias_ref[3]
    for j in range(4):
        done = [two_planes(*sums, acc_ref, part)
                for part, sums in paired_dots(w7_ref, col7_ref.at[2 * j], col7_ref.at[2 * j + 1], 896)]
        if j > 0:
            for a in range(2):
                values = jnp.concatenate([leaky(pair[a] + wide(bias_joined, pair[a])).astype(BF16) for pair in done], axis=1)
                col8_ref[2 * j + a - 2] = window(values)[:, 128:768]

    bias_final = bias_ref[4]
    output_matrix = w9_ref[...].astype(BF16)
    for j in range(3):
        for part, sums in paired_dots(w8_ref, col8_ref.at[2 * j], col8_ref.at[2 * j + 1], 640):
            done = two_planes(*sums, acc_ref, part)
            if j > 0:
                for a in range(2):
                    values = leaky(done[a] + wide(bias_final, done[a])).astype(BF16)
                    predicted = jnp.dot(output_matrix, values, preferred_element_type=F32)
                    to = 4 * (j - 1) + 2 * a
                    flat_ref[0, to:to + 2, part] = predicted[0:2]
                    flat_ref[1, to:to + 2, part] = predicted[2:4]

    for y in range(8):
        at = ROW * (y + 4) - 256 + 4
        last_ref[8 * y:8 * y + 8, 0:64] = flat_ref[0, :, at:at + 64]
        last_ref[8 * y:8 * y + 8, 64:128] = flat_ref[1, :, at:at + 64]
    old = iota((128, 128), 0)
    turns = (2 * (old % 64) + old // 64 == iota((128, 128), 1)).astype(F32)
    result = jnp.dot(last_ref[...], turns, preferred_element_type=F32, precision=lax.Precision.HIGHEST)
    for y in range(8):
        for x in range(4):
            at = 8 * y + 2 * x
            out_ref[x, 2 * y:2 * y + 2, :] = result[at:at + 2]


def network(odd, pieces, weights):
    vmem = pl.BlockSpec(memory_space=pltpu.VMEM)
    scratch = [
        ((768, 128), F32), ((768, 128), F32), ((4, 768, 128), F32), ((6, 32, WIDTH), F32),
        ((384, WIDTH), BF16), ((18, 64, WIDTH), BF16), ((2, 256, WIDTH), BF16), ((2, 256, WIDTH), BF16),
        ((2, 64, WIDTH), F32), ((9, 128, WIDTH), BF16), ((9, 16, WIDTH), BF16),
        ((1200, 896), BF16), ((1792, 896), BF16), ((8, 512, 896), BF16), ((6, 256, 640), BF16),
        ((2, 8, 640), F32), ((64, 128), F32),
    ]
    operands = (odd, *pieces, *weights)
    return pl.pallas_call(
        network_kernel,
        out_shape=jax.ShapeDtypeStruct((4, 16, 128), F32),
        in_specs=[pl.BlockSpec(memory_space=pltpu.SMEM)] + [vmem] * (len(operands) - 1),
        out_specs=vmem,
        scratch_shapes=[pltpu.VMEM(shape, kind) for shape, kind in scratch],
        compiler_params=pltpu.CompilerParams(vmem_limit_bytes=50 * 2**20),
        cost_estimate=pl.CostEstimate(flops=4 * 10**9, bytes_accessed=4 * 10**6, transcendentals=0),
        name="network",
    )(*operands)


def ring(size, step):
    return [(i, (i + step) % size) for i in range(size)]


def partner(i, size, first):
    return (i + 1 if (i % 2 == 1) == first else i - 1) % size


def swaps_y(first):
    return [(gx, 2 * partner(gx // 2, 4, first) + gx % 2) for gx in range(8)]


def swaps_z(first):
    pairs = []
    for gx in range(8):
        for gz in range(8):
            to = partner(gx % 2 * 8 + gz, 16, first)
            pairs.append((gx * 8 + gz, (gx // 2 * 2 + to // 8) * 8 + to % 8))
    return pairs


def exchange(density, half, odd, pack):
    other = lax.ppermute(density, "gx", [(i, i ^ 1) for i in range(8)])
    other = yield other
    mid = jnp.concatenate([jnp.where(half == 0, density, other), jnp.where(half == 0, other, density)], axis=0)
    a = lax.ppermute(mid, "gx", swaps_y(False))
    b = lax.ppermute(mid, "gx", swaps_y(True))
    high = jnp.concatenate([a[:, 8:], mid[:, 8:], b[:, 8:]], axis=0)
    low = jnp.concatenate([a[:, :8], mid[:, :8], b[:, :8]], axis=0)
    low, high = lax.ppermute(high, "gy", ring(8, 1)), lax.ppermute(low, "gy", ring(8, -1))
    pieces = (low, a, mid, b, high)
    edge_a, edge_b = pack(odd, *pieces)
    edge_a = lax.ppermute(edge_a, ("gx", "gz"), swaps_z(True))
    edge_b = lax.ppermute(edge_b, ("gx", "gz"), swaps_z(False))
    yield *pieces, edge_a, edge_b


def body(density, first_kernel, first_bias, second_kernel, second_bias, coarse_kernel, coarse_bias, deeper_kernel,
         deeper_bias, upward_kernel, upward_bias, joined_kernel, joined_bias, final_kernel, final_bias, output_weight):
    half = (lax.axis_index("gx") % 2).astype(jnp.int32)
    odd = jnp.stack([lax.axis_index("gx") // 2 % 2, lax.axis_index("gz") % 2]).astype(jnp.int32)
    steps = exchange(density, half, odd, pack_edges)
    other = next(steps)
    weights = prepare_weights(
        half.reshape(1), first_kernel.reshape(27, 16), second_kernel.reshape(432, 16),
        coarse_kernel.reshape(864, 16), deeper_kernel.reshape(864, 32), joined_kernel.reshape(432, 32),
        final_kernel.reshape(432, 16), upward_kernel.reshape(128, 32), output_weight.reshape(1, 16),
        *(b.reshape(1, -1) for b in (first_bias, second_bias, coarse_bias, deeper_bias, upward_bias, joined_bias,
                                     final_bias)))
    other, weights = lax.optimization_barrier((other, weights))
    pieces = steps.send(other)
    return network(odd, pieces, weights)


def solution(mesh):
    placed = (P("gx", "gy", "gz"),) + (P(),) * 15
    return jax.shard_map(body, mesh=mesh, in_specs=placed, out_specs=P("gx", "gy", "gz"), check_vma=False)
```

time: 355 us -> 62.4 us (0.18)
  the two profiles are of different devices: /device:TPU:6 before, /device:TPU:1 now
where the time goes in v1:
time: 62.4 us; the launch traced here: 62 us
  starting transfers between devices  32.5 us (52%)
  Pallas kernels  15.7 us (25%)
  waiting for transfers between devices  8.64 us (14%)
  local copies, waits for them, and re-layouts  4.64 us (7%)
    ppermute x1, starting transfers between devices, exchange(): other = lax.ppermute(density, 'gx', [(i, i ^ 1) for i in range(8)])  16.3 us
    pallas_call x1, Pallas kernels, network(): pl.pallas_call(network_kernel, out_shape=jax.ShapeDtypeStruct((4, 16, 128...  14 us
    ppermute x1, starting transfers between devices, exchange(): b = lax.ppermute(mid, 'gx', swaps_y(True))  4.64 us
    unnamed x31, local copies, waits for them, and re-layouts  4.62 us
    ppermute x1, starting transfers between devices, exchange(): edge_a = lax.ppermute(edge_a, ('gx', 'gz'), swaps_z(True))  4.26 us
    ppermute x1, starting transfers between devices, exchange(): lax.ppermute(high, 'gy', ring(8, 1))  3.49 us
    ppermute x1, waiting for transfers between devices, exchange(): a = lax.ppermute(mid, 'gx', swaps_y(False))  2.71 us
    ppermute x1, waiting for transfers between devices, exchange(): edge_b = lax.ppermute(edge_b, ('gx', 'gz'), swaps_z(False))  2.5 us
  transfers between devices with their start and end apart: 7, of which 4 were waited for; matrix products, arithmetic and copies ran while one was open for 2% of the time, Pallas kernels for 2%

profile of v1, /device:TPU:1, one launch (start us, length us, event | category | flops | bytes accessed | tf_op | source)
XLA Modules:
  0.0 62.0 jit_solution(16251624788844416035)
XLA Ops:
  0.0 16.3 %collective-permute-start = (bf16[4,16,128]{2,1,0:T(8,128)(2,1)}, bf16[4,16,128]{2,1,0:T(8,128)(2,1)S(1)}, u32[]{:S(2)}, u32[]{:S(2)}) collective-permute-start(bf16[4,16,128]{2,1,0:T(8,128)(2,1)} %param.16), channel_id=1, source_target_pairs={{0,64},{64,0},{128,192},{192,128},{256,320},{320,256},{384,448},{4... | collective-permute-start | bytes 49160 | tf_op jit(solution)/shard_map/ppermute | solution.py:386
  16.3 0.0 copy-start.14
  16.3 0.0 copy-start.10
  16.3 0.0 copy-start.11
  16.3 0.0 copy-start.12
  16.4 0.0 copy-start
  16.4 0.6 copy-done.14
  17.0 0.0 copy-start.2
  17.0 1.1 %copy.18 = bf16[3,3,3,32,16]{4,3,2,1,0:T(8,128)(2,1)S(1)} copy(bf16[3,3,3,32,16]{3,4,2,1,0:T(8,128)(2,1)} %param.21) | data formatting | bytes 55296 | tf_op args[5]
  18.1 0.0 copy-start.5
  18.2 0.5 copy-done.5
  18.8 0.9 %copy-done.3 = bf16[3,3,3,16,16]{4,3,2,1,0:T(8,128)(2,1)S(1)} copy-done((bf16[3,3,3,16,16]{4,3,2,1,0:T(8,128)(2,1)S(1)}, bf16[3,3,3,16,16]{4,3,2,1,0:T(8,128)(2,1)}, u32[]{:S(2)}) %copy-start.3) | copy-done | bytes 13848
  19.7 0.8 %copy-done.4 = bf16[2,2,2,16,32]{4,3,2,1,0:T(8,128)(2,1)S(1)} copy-done((bf16[2,2,2,16,32]{4,3,2,1,0:T(8,128)(2,1)S(1)}, bf16[2,2,2,16,32]{4,3,2,1,0:T(8,128)(2,1)}, u32[]{:S(2)}) %copy-start.4) | copy-done | bytes 8216
  20.4 1.0 %weights.1 = (bf16[512,256]{1,0:T(8,128)(2,1)S(1)}, bf16[192,256]{1,0:T(8,128)(2,1)S(1)}, bf16[96,768]{1,0:T(8,128)(2,1)S(1)}, bf16[128,1792]{1,0:T(8,128)(2,1)S...) custom-call(s32[1]{0:T(128)} %bitcast.2.half_ref, ...), custom_call_target="tpu_custom_call" | custom-call | flops 10000000 | bytes 2000000 | tf_op jit(solution)/shard_map/weights/pallas_call | solution.py:103
  21.4 0.0 copy-start.13
  21.5 0.0 collective-permute-done
  21.5 0.7 %copy-done.13 = bf16[4,16,128]{2,1,0:T(8,128)(2,1)S(1)} copy-done((bf16[4,16,128]{2,1,0:T(8,128)(2,1)S(1)}, bf16[4,16,128]{2,1,0:T(8,128)(2,1)}, u32[]{:S(2)}) %copy-start.13) | copy-done | bytes 16408
  22.2 4.6 %collective-permute-start.2 = (bf16[8,16,128]{2,1,0:T(8,128)(2,1)S(1)}, bf16[8,16,128]{2,1,0:T(8,128)(2,1)S(1)}, u32[]{:S(2)}, u32[]{:S(2)}) collective-permute-start(bf16[8,16,128]{2,1,0:T(8,128)(2,1)S(1)} %pad_maximum_fusion.2.mid_ref), channel_id=1, source_target_pairs={{0,384},{64,448},{128,256},{192,320},{256,128},{320,192},{384,0},{... | collective-permute-start | bytes 98312 | tf_op jit(solution)/shard_map/ppermute | solution.py:390
  26.8 1.9 %collective-permute-start.1 = (bf16[8,16,128]{2,1,0:T(8,128)(2,1)S(1)}, bf16[8,16,128]{2,1,0:T(8,128)(2,1)S(1)}, u32[]{:S(2)}, u32[]{:S(2)}) collective-permute-start(bf16[8,16,128]{2,1,0:T(8,128)(2,1)S(1)} %pad_maximum_fusion.2.mid_ref), channel_id=1, source_target_pairs={{0,128},{64,192},{128,0},{192,64},{256,384},{320,448},{384,256},{4... | collective-permute-start | bytes 98312 | tf_op jit(solution)/shard_map/ppermute | solution.py:389
  28.8 0.0 collective-permute-done.2.b_ref
  28.8 2.7 %collective-permute-done.1.a_ref = bf16[8,16,128]{2,1,0:T(8,128)(2,1)S(1)} collective-permute-done((bf16[8,16,128]{2,1,0:T(8,128)(2,1)S(1)}, bf16[8,16,128]{2,1,0:T(8,128)(2,1)S(1)}, u32[]{:S(2)}, u32[]{:S(2)}) %collective-permute-start.1) | collective-permute-done | bytes 32800 | tf_op jit(solution)/shard_map/ppermute | solution.py:389
  31.5 3.5 %collective-permute-start.3 = (bf16[24,8,128]{2,1,0:T(8,128)(2,1)S(1)}, bf16[24,8,128]{2,1,0:T(8,128)(2,1)S(1)}, u32[]{:S(2)}, u32[]{:S(2)}) collective-permute-start(bf16[24,8,128]{2,1,0:T(8,128)(2,1)S(1)} %pad_maximum_fusion), channel_id=1, source_target_pairs={{0,8},{8,16},{16,24},{24,32},{32,40},{40,48},{48,56},{56,0},{1,9},... | collective-permute-start | bytes 147464 | tf_op jit(solution)/shard_map/ppermute | solution.py:393
  35.0 0.0 collective-permute-start.4
  35.0 0.1 pad_add_fusion.odd_ref
  35.1 1.1 %collective-permute-done.3.low_ref = bf16[24,8,128]{2,1,0:T(8,128)(2,1)S(1)} collective-permute-done((bf16[24,8,128]{2,1,0:T(8,128)(2,1)S(1)}, bf16[24,8,128]{2,1,0:T(8,128)(2,1)S(1)}, u32[]{:S(2)}, u32[]{:S(2)}) %collective-permute-start.3) | collective-permute-done | bytes 49184 | tf_op jit(solution)/shard_map/ppermute | solution.py:393
  36.2 2.4 %collective-permute-done.4.high_ref = bf16[24,8,128]{2,1,0:T(8,128)(2,1)S(1)} collective-permute-done((bf16[24,8,128]{2,1,0:T(8,128)(2,1)S(1)}, bf16[24,8,128]{2,1,0:T(8,128)(2,1)S(1)}, u32[]{:S(2)}, u32[]{:S(2)}) %collective-permute-start.4) | collective-permute-done | bytes 49184 | tf_op jit(solution)/shard_map/ppermute | solution.py:393
  38.5 0.7 %edges.1 = (bf16[48,128]{1,0:T(8,128)(2,1)S(1)}, bf16[48,128]{1,0:T(8,128)(2,1)S(1)}) custom-call(s32[2]{0:T(128)S(1)} %pad_add_fusion.odd_ref, bf16[24,8,128]{2,1,0:T(8,128)(2,1)S(1)} %collective-permute-done.3.low_ref, bf16[8,16,128]{2,1,0:T(8,128)(2,1)S(1)} %collective-permute-done.1.a_ref, bf16[8,16,128]{2,1,0:T(8,128)(2,1)S(1)} %pad_maximum_fusion.2.mid_ref, ...), custom_call_target="tpu_custom_call" | custom-call | tf_op jit(solution)/shard_map/edges/pallas_call | solution.py:143
  39.3 4.3 %collective-permute-start.5 = (bf16[48,128]{1,0:T(8,128)(2,1)S(1)}, bf16[48,128]{1,0:T(8,128)(2,1)S(1)}, u32[]{:S(2)}, u32[]{:S(2)}) collective-permute-start(bf16[48,128]{1,0:T(8,128)(2,1)S(1)} %get-tuple-element.39), channel_id=1, source_target_pairs={{0,71},{1,2},{2,1},{3,4},{4,3},{5,6},{6,5},{7,64},{64,7},{65,66},{... | collective-permute-start | bytes 36872 | tf_op jit(solution)/shard_map/ppermute | solution.py:396
  43.5 1.9 %collective-permute-start.6 = (bf16[48,128]{1,0:T(8,128)(2,1)S(1)}, bf16[48,128]{1,0:T(8,128)(2,1)S(1)}, u32[]{:S(2)}, u32[]{:S(2)}) collective-permute-start(bf16[48,128]{1,0:T(8,128)(2,1)S(1)} %get-tuple-element.40), channel_id=1, source_target_pairs={{0,1},{1,0},{2,3},{3,2},{4,5},{5,4},{6,7},{7,6},{64,65},{65,64},{6... | collective-permute-start | bytes 36872 | tf_op jit(solution)/shard_map/ppermute | solution.py:397
  45.5 0.0 collective-permute-done.5.edge_a_ref
  45.5 2.5 %collective-permute-done.6.edge_b_ref = bf16[48,128]{1,0:T(8,128)(2,1)S(1)} collective-permute-done((bf16[48,128]{1,0:T(8,128)(2,1)S(1)}, bf16[48,128]{1,0:T(8,128)(2,1)S(1)}, u32[]{:S(2)}, u32[]{:S(2)}) %collective-permute-start.6) | collective-permute-done | bytes 12320 | tf_op jit(solution)/shard_map/ppermute | solution.py:397
  48.0 14.0 %network.1 = f32[4,16,128]{2,1,0:T(8,128)} custom-call(s32[2]{0:T(128)S(1)} %pad_add_fusion.odd_ref, bf16[24,8,128]{2,1,0:T(8,128)(2,1)S(1)} %collective-permute-done.3.low_ref, bf16[8,16,128]{2,1,0:T(8,128)(2,1)S(1)} %collective-permute-done.1.a_ref, bf16[8,16,128]{2,1,0:T(8,128)(2,1)S(1)} %pad_maximum_fusion.2.mid_ref, ...), custom_call_target="tpu_custom_call" | custom-call | flops 4000000000 | bytes 4000000 | tf_op jit(solution)/shard_map/network/pallas_call | solution.py:352
  (25 shorter events, 0.1 us)
Async XLA Ops:
  0.0 21.5 %collective-permute-start = (bf16[4,16,128]{2,1,0:T(8,128)(2,1)}, bf16[4,16,128]{2,1,0:T(8,128)(2,1)S(1)}, u32[]{:S(2)}, u32[]{:S(2)}) collective-permute-start(bf16[4,16,128]{2,1,0:T(8,128)(2,1)} %param.16), channel_id=1, source_target_pairs={{0,64},{64,0},{128,192},{192,128},{256,320},{320,256},{384,448},{4... | collective-permute-start | bytes 49160 | tf_op jit(solution)/shard_map/ppermute | solution.py:386
  16.3 0.7 %copy-start.14 = (bf16[3,3,3,16,1]{3,2,4,1,0:T(4,128)(2,1)S(1)}, bf16[3,3,3,16,1]{3,2,4,1,0:T(4,128)(2,1)}, u32[]{:S(2)}) copy-start(bf16[3,3,3,16,1]{3,2,4,1,0:T(4,128)(2,1)} %param.17) | copy-start | bytes 2596
  16.3 1.8 %copy-start.10 = (f32[16]{0:T(128)S(1)}, f32[16]{0:T(128)}, u32[]{:S(2)}) copy-start(f32[16]{0:T(128)} %param.26) | copy-start | bytes 196
  16.3 1.8 %copy-start.11 = (f32[16]{0:T(128)S(1)}, f32[16]{0:T(128)}, u32[]{:S(2)}) copy-start(f32[16]{0:T(128)} %param.28) | copy-start | bytes 196
  16.3 1.8 %copy-start.12 = (f32[16]{0:T(128)S(1)}, f32[16]{0:T(128)}, u32[]{:S(2)}) copy-start(f32[16]{0:T(128)} %param.30) | copy-start | bytes 196
  16.3 1.8 %copy-start.6 = (f32[16]{0:T(128)S(1)}, f32[16]{0:T(128)}, u32[]{:S(2)}) copy-start(f32[16]{0:T(128)} %param.18) | copy-start | bytes 196
  16.3 1.8 %copy-start.7 = (f32[16]{0:T(128)S(1)}, f32[16]{0:T(128)}, u32[]{:S(2)}) copy-start(f32[16]{0:T(128)} %param.20) | copy-start | bytes 196
  16.3 1.8 %copy-start.8 = (f32[32]{0:T(128)S(1)}, f32[32]{0:T(128)}, u32[]{:S(2)}) copy-start(f32[32]{0:T(128)} %param.22) | copy-start | bytes 388
  16.3 1.8 %copy-start.9 = (f32[32]{0:T(128)S(1)}, f32[32]{0:T(128)}, u32[]{:S(2)}) copy-start(f32[32]{0:T(128)} %param.24) | copy-start | bytes 388
  16.4 1.8 %copy-start = (bf16[3,3,3,32,32]{4,3,2,1,0:T(8,128)(2,1)S(1)}, bf16[3,3,3,32,32]{4,3,2,1,0:T(8,128)(2,1)}, u32[]{:S(2)}) copy-start(bf16[3,3,3,32,32]{4,3,2,1,0:T(8,128)(2,1)} %param.23) | copy-start | bytes 165892
  17.0 1.2 %copy-start.1 = (bf16[3,3,3,16,16]{4,3,2,1,0:T(8,128)(2,1)S(1)}, bf16[3,3,3,16,16]{4,3,2,1,0:T(8,128)(2,1)}, u32[]{:S(2)}) copy-start(bf16[3,3,3,16,16]{4,3,2,1,0:T(8,128)(2,1)} %param.19) | copy-start | bytes 41476
  17.0 1.2 %copy-start.2 = (bf16[3,3,3,16,32]{4,3,2,1,0:T(8,128)(2,1)S(1)}, bf16[3,3,3,16,32]{4,3,2,1,0:T(8,128)(2,1)}, u32[]{:S(2)}) copy-start(bf16[3,3,3,16,32]{4,3,2,1,0:T(8,128)(2,1)} %param.27) | copy-start | bytes 82948
  18.1 0.7 %copy-start.5 = (bf16[16]{0:T(256)(128)(2,1)S(1)}, bf16[16]{0:T(256)(128)(2,1)}, u32[]{:S(2)}) copy-start(bf16[16]{0:T(256)(128)(2,1)} %param.31) | copy-start | bytes 100
  18.8 0.9 %copy-start.3 = (bf16[3,3,3,16,16]{4,3,2,1,0:T(8,128)(2,1)S(1)}, bf16[3,3,3,16,16]{4,3,2,1,0:T(8,128)(2,1)}, u32[]{:S(2)}) copy-start(bf16[3,3,3,16,16]{4,3,2,1,0:T(8,128)(2,1)} %param.29) | copy-start | bytes 41476
  19.7 0.8 %copy-start.4 = (bf16[2,2,2,16,32]{4,3,2,1,0:T(8,128)(2,1)S(1)}, bf16[2,2,2,16,32]{4,3,2,1,0:T(8,128)(2,1)}, u32[]{:S(2)}) copy-start(bf16[2,2,2,16,32]{4,3,2,1,0:T(8,128)(2,1)} %param.25) | copy-start | bytes 24580
  21.4 0.7 %copy-start.13 = (bf16[4,16,128]{2,1,0:T(8,128)(2,1)S(1)}, bf16[4,16,128]{2,1,0:T(8,128)(2,1)}, u32[]{:S(2)}) copy-start(bf16[4,16,128]{2,1,0:T(8,128)(2,1)} %param.16) | copy-start | bytes 49156
  22.2 6.6 %collective-permute-start.2 = (bf16[8,16,128]{2,1,0:T(8,128)(2,1)S(1)}, bf16[8,16,128]{2,1,0:T(8,128)(2,1)S(1)}, u32[]{:S(2)}, u32[]{:S(2)}) collective-permute-start(bf16[8,16,128]{2,1,0:T(8,128)(2,1)S(1)} %pad_maximum_fusion.2.mid_ref), channel_id=1, source_target_pairs={{0,384},{64,448},{128,256},{192,320},{256,128},{320,192},{384,0},{... | collective-permute-start | bytes 98312 | tf_op jit(solution)/shard_map/ppermute | solution.py:390
  26.8 4.7 %collective-permute-start.1 = (bf16[8,16,128]{2,1,0:T(8,128)(2,1)S(1)}, bf16[8,16,128]{2,1,0:T(8,128)(2,1)S(1)}, u32[]{:S(2)}, u32[]{:S(2)}) collective-permute-start(bf16[8,16,128]{2,1,0:T(8,128)(2,1)S(1)} %pad_maximum_fusion.2.mid_ref), channel_id=1, source_target_pairs={{0,128},{64,192},{128,0},{192,64},{256,384},{320,448},{384,256},{4... | collective-permute-start | bytes 98312 | tf_op jit(solution)/shard_map/ppermute | solution.py:389
  31.5 4.7 %collective-permute-start.3 = (bf16[24,8,128]{2,1,0:T(8,128)(2,1)S(1)}, bf16[24,8,128]{2,1,0:T(8,128)(2,1)S(1)}, u32[]{:S(2)}, u32[]{:S(2)}) collective-permute-start(bf16[24,8,128]{2,1,0:T(8,128)(2,1)S(1)} %pad_maximum_fusion), channel_id=1, source_target_pairs={{0,8},{8,16},{16,24},{24,32},{32,40},{40,48},{48,56},{56,0},{1,9},... | collective-permute-start | bytes 147464 | tf_op jit(solution)/shard_map/ppermute | solution.py:393
  35.0 3.5 %collective-permute-start.4 = (bf16[24,8,128]{2,1,0:T(8,128)(2,1)S(1)}, bf16[24,8,128]{2,1,0:T(8,128)(2,1)S(1)}, u32[]{:S(2)}, u32[]{:S(2)}) collective-permute-start(bf16[24,8,128]{2,1,0:T(8,128)(2,1)S(1)} %pad_maximum_fusion.1), channel_id=1, source_target_pairs={{0,56},{8,0},{16,8},{24,16},{32,24},{40,32},{48,40},{56,48},{1,57}... | collective-permute-start | bytes 147464 | tf_op jit(solution)/shard_map/ppermute | solution.py:393
  39.3 6.2 %collective-permute-start.5 = (bf16[48,128]{1,0:T(8,128)(2,1)S(1)}, bf16[48,128]{1,0:T(8,128)(2,1)S(1)}, u32[]{:S(2)}, u32[]{:S(2)}) collective-permute-start(bf16[48,128]{1,0:T(8,128)(2,1)S(1)} %get-tuple-element.39), channel_id=1, source_target_pairs={{0,71},{1,2},{2,1},{3,4},{4,3},{5,6},{6,5},{7,64},{64,7},{65,66},{... | collective-permute-start | bytes 36872 | tf_op jit(solution)/shard_map/ppermute | solution.py:396
  43.5 4.4 %collective-permute-start.6 = (bf16[48,128]{1,0:T(8,128)(2,1)S(1)}, bf16[48,128]{1,0:T(8,128)(2,1)S(1)}, u32[]{:S(2)}, u32[]{:S(2)}) collective-permute-start(bf16[48,128]{1,0:T(8,128)(2,1)S(1)} %get-tuple-element.40), channel_id=1, source_target_pairs={{0,1},{1,0},{2,3},{3,2},{4,5},{5,4},{6,7},{7,6},{64,65},{65,64},{6... | collective-permute-start | bytes 36872 | tf_op jit(solution)/shard_map/ppermute | solution.py:397

commit v2 on v1

v2 whole, which is shorter than its diff:
```python
import functools

import jax
import jax.numpy as jnp
from jax import lax
from jax.experimental import pallas as pl
from jax.experimental.pallas import tpu as pltpu
from jax.sharding import PartitionSpec as P

F32 = jnp.float32
BF16 = jnp.bfloat16
ROW = 72
FINE = 1152
COARSE, COARSE_WIDTH = 128, 896
RAISED, RAISED_WIDTH = 200, 768
FINAL, FINAL_WIDTH = 272, 640


def leaky(values):
    return jnp.maximum(values, 0.2 * values)


def iota(shape, dim):
    return lax.broadcasted_iota(jnp.int32, shape, dim)


def spread_bias(bias, rows):
    count = bias.shape[1]
    match = iota((rows, count), 0) % count == iota((rows, count), 1)
    return jnp.broadcast_to(jnp.sum(jnp.where(match, bias, 0.0), axis=1, keepdims=True), (rows, 128))


def weights_kernel(place_ref, first_ref, *refs):
    kernels_ref, vectors_ref = refs[:2]
    (w1_ref, w2_ref, w4_ref, w5_ref, w7_ref, w8_ref, sz_ref, w6_ref, w9_ref, bias_ref, expand_ref, flags_ref) = refs[2:14]
    fine_ref, joint_ref, deeper_base_ref = refs[14:]

    tap = iota((27, 256), 0)
    lane = iota((27, 256), 1)
    place = (tap % 3) * 64 + (tap // 3 % 3) * 16 + tap // 9
    base = lax.dot_general(first_ref[...], (place == lane).astype(BF16), (((0,), (0,)), ((), ())),
                           preferred_element_type=F32)
    base = jnp.where(place_ref[0] == 0, base, pltpu.roll(base, 4, 1))
    old = iota((256, 256), 0)
    new = iota((256, 256), 1)
    order = (old % 16 // 8) * 128 + (old // 16 % 4) * 32 + (old // 64) * 8 + old % 8
    permute = (order == new).astype(BF16)
    for x in range(8):
        rows = jnp.concatenate(
            [pltpu.roll(base, x + 16 * b + 64 * e, 1) if x + b + e else base for b in range(2) for e in range(2)], axis=0)
        w1_ref[64 * x:64 * x + 64] = jnp.dot(rows.astype(BF16), permute, preferred_element_type=F32).astype(BF16)

    row = iota((128, 256), 0)
    sz_ref[...] = (iota((128, 256), 1) == (row % 2) * 128 + row // 2 + 4).astype(BF16)
    row = iota((256, 2 * FINE), 0)
    cell = row % 8 + 136 * (row // 128)
    target = (cell % 2) * FINE + (row % 128 // 8) * ROW + cell // 2
    expand_ref[...] = (iota((256, 2 * FINE), 1) == target).astype(BF16)
    for n in range(2):
        flags_ref[n] = jnp.full((8, 128), place_ref[n + 1].astype(F32))

    for side, target in ((0, w2_ref), (1, w8_ref)):
        fine_ref[...] = jnp.zeros_like(fine_ref)
        for t in range(27):
            at = (t // 3 % 3) * 64 + (t % 3) * 16
            fine_ref[16 * (t // 9):16 * (t // 9) + 16, at:at + 16] = kernels_ref[
                16 * t:16 * t + 16, 16 * side:16 * side + 16].astype(F32)
        for u in range(3):
            block = fine_ref[16 * u:16 * u + 16]
            for n in range(4):
                move = (n // 2) * 64 + (n % 2) * 16
                at = 64 * u + 16 * n
                target[at:at + 16] = (pltpu.roll(block, move, 1) if n else block).astype(BF16)

    joint_ref[...] = jnp.zeros_like(joint_ref)
    for t in range(27):
        piece = kernels_ref[432 + 16 * t:448 + 16 * t].astype(F32)
        for side in range(2):
            at = side * 256 + (t // 3 % 3) * 64 + (t % 3) * 16
            joint_ref[16 * (t // 9):16 * (t // 9) + 16, at:at + 16] = piece[:, 16 * side:16 * side + 16]
    for u in range(3):
        block = joint_ref[16 * u:16 * u + 16]
        for n in range(4):
            move = (n // 2) * 64 + (n % 2) * 16
            at = 64 * u + 16 * n
            w7_ref[at:at + 16] = (pltpu.roll(block, move, 1) if n else block).astype(BF16)

    same = (iota((432, 768), 0) == iota((432, 768), 1)).astype(BF16)
    block = lax.dot_general(kernels_ref[864:1296], same, (((0,), (0,)), ((), ())), preferred_element_type=F32)
    for p in range(3):
        w4_ref[32 * p:32 * p + 32] = (pltpu.roll(block, 144 * p, 1) if p else block).astype(BF16)
    deeper_base_ref[...] = jnp.zeros_like(deeper_base_ref)
    for t in range(27):
        deeper_base_ref[:, 32 * t:32 * t + 32] = kernels_ref[1296 + 32 * t:1328 + 32 * t].astype(F32)
    block = deeper_base_ref[...]
    for p in range(4):
        w5_ref[32 * p:32 * p + 32] = (pltpu.roll(block, 288 * p, 1) if p else block).astype(BF16)

    w6_ref[...] = kernels_ref[2160:2288]
    spread = (iota((16, 64), 0) == iota((16, 64), 1) % 16).astype(BF16)
    row_weights = jnp.dot(vectors_ref[:, 144:160].astype(BF16), spread, preferred_element_type=F32)
    row = iota((8, 64), 0)
    group = iota((8, 64), 1) // 16
    chosen = (row % 2 == group // 2) & (row // 2 == group % 2)
    w9_ref[...] = jnp.where(chosen, row_weights, 0.0)
    for n in range(5):
        bias_ref[n] = spread_bias(vectors_ref[:, 16 * n:16 * n + 16], 64)
    for n in range(2):
        bias_ref[5 + n] = spread_bias(vectors_ref[:, 80 + 32 * n:112 + 32 * n], 64)


def prepare_weights(place, first, kernels, vectors):
    shapes = [(512, 256), (192, 256), (96, 768), (128, 1792), (192, 512), (192, 256), (128, 256), (128, 32)]
    vmem = pl.BlockSpec(memory_space=pltpu.VMEM)
    return pl.pallas_call(
        weights_kernel,
        out_shape=[jax.ShapeDtypeStruct(s, BF16) for s in shapes]
        + [jax.ShapeDtypeStruct((8, 64), F32), jax.ShapeDtypeStruct((7, 64, 128), F32),
           jax.ShapeDtypeStruct((256, 2 * FINE), BF16), jax.ShapeDtypeStruct((2, 8, 128), F32)],
        in_specs=[pl.BlockSpec(memory_space=pltpu.SMEM)] + [vmem] * 3,
        out_specs=[vmem] * 12,
        scratch_shapes=[pltpu.VMEM((48, 256), F32), pltpu.VMEM((48, 512), F32), pltpu.VMEM((32, 1792), F32)],
        compiler_params=pltpu.CompilerParams(vmem_limit_bytes=24 * 2**20),
        cost_estimate=pl.CostEstimate(flops=10**7, bytes_accessed=2 * 10**6, transcendentals=0),
        name="weights",
    )(place, first, kernels, vectors)


def pick(flag, yes, no):
    rows = yes.shape[0] // 8
    return jnp.where((jnp.concatenate([flag] * rows, axis=0) if rows > 1 else flag) > 0.5, yes, no)


def edges_kernel(flags_ref, low_ref, a_ref, mid_ref, b_ref, high_ref, left_ref, right_ref, cells_ref):
    odd_y = flags_ref[0]
    for x in range(8):
        planes = [
            jnp.concatenate([low_ref[8 * g + x], ref[x], high_ref[8 * g + x]], axis=0).astype(F32)
            for g, ref in enumerate((a_ref, mid_ref, b_ref))
        ]
        cells_ref[32 * x:32 * x + 32] = pick(odd_y, planes[0], planes[2])
        cells_ref[32 * (8 + x):32 * (8 + x) + 32] = planes[1]
        cells_ref[32 * (16 + x):32 * (16 + x) + 32] = pick(odd_y, planes[2], planes[0])
    left = [jnp.zeros((24, 128), F32)] * 2
    right = [jnp.zeros((24, 128), F32)] * 2
    lane = iota((24, 128), 1)
    for y in range(32):
        b, at = y % 2, 8 * (y // 2)
        rows = cells_ref[pl.ds(y, 24, stride=32), :]
        inside = (lane >= at) & (lane < at + 8)
        left[b] = jnp.where(inside, pltpu.roll(rows, at, 1) if at else rows, left[b])
        right[b] = jnp.where(inside, pltpu.roll(rows, (at + 8) % 128, 1) if at < 120 else rows, right[b])
    left_ref[...] = jnp.concatenate(left, axis=0).astype(BF16)
    right_ref[...] = jnp.concatenate(right, axis=0).astype(BF16)


def pack_edges(flags, *pieces):
    vmem = pl.BlockSpec(memory_space=pltpu.VMEM)
    return pl.pallas_call(
        edges_kernel,
        out_shape=[jax.ShapeDtypeStruct((48, 128), BF16)] * 2 + [jax.ShapeDtypeStruct((768, 128), F32)],
        in_specs=[vmem] * 6,
        out_specs=[vmem] * 3,
        compiler_params=pltpu.CompilerParams(vmem_limit_bytes=8 * 2**20),
        name="edges",
    )(flags, *pieces)


def sample_kernel(cells_ref, sz_ref, phase_ref, even_ref, odd_ref):
    for at in range(0, 768, 256):
        sampled = jnp.dot(cells_ref[at:at + 256].astype(BF16), sz_ref[...], preferred_element_type=F32)
        even_ref[at:at + 256] = sampled[:, 0:128]
        odd_ref[at:at + 256] = sampled[:, 128:256]
    for y in range(32):
        to = ROW * (y // 2)
        for e, ref in enumerate((even_ref, odd_ref)):
            phase_ref[2 * (y % 2) + e, :, to:to + ROW] = ref[pl.ds(y, 24, stride=32), :][:, 0:ROW]


def sample(cells, sz):
    vmem = pl.BlockSpec(memory_space=pltpu.VMEM)
    return pl.pallas_call(
        sample_kernel,
        out_shape=jax.ShapeDtypeStruct((4, 24, FINE), F32),
        in_specs=[vmem] * 2,
        out_specs=vmem,
        scratch_shapes=[pltpu.VMEM((768, 128), F32), pltpu.VMEM((768, 128), F32)],
        compiler_params=pltpu.CompilerParams(vmem_limit_bytes=8 * 2**20),
        cost_estimate=pl.CostEstimate(flops=10**8, bytes_accessed=10**6, transcendentals=0),
        name="sample",
    )(cells, sz)


def chunks(width):
    return [slice(at, min(at + 256, width)) for at in range(0, width, 256)]


def moved(values, step):
    return pltpu.roll(values, step % values.shape[1], 1) if step else values


def shifted(values, start, width):
    whole = start // 128 * 128
    if start >= 0 and whole + width + 128 <= values.shape[1]:
        values, start = values[:, whole:whole + width + 128], start - whole
    return moved(values, -start)[:, 0:width]


def window(values, start, width):
    rows = []
    for b in range(2):
        even = values[32 * b:32 * b + 16]
        odd = values[32 * b + 16:32 * b + 32]
        rows.append(jnp.concatenate([moved(odd, 1), even, odd, moved(even, -1)], axis=0))
    return jnp.concatenate([shifted(rows[1], start - ROW, width), shifted(rows[0], start, width),
                            shifted(rows[1], start, width), shifted(rows[0], start + ROW, width)], axis=0)


def neighbours(values, start, width):
    rows = jnp.concatenate([moved(values, 1), values, moved(values, -1)], axis=0)
    return jnp.concatenate([shifted(rows, start + ROW * step, width) for step in (-1, 0, 1)], axis=0)


def two_planes(sums_a, sums_b, acc_ref, part):
    done_a = acc_ref[1, :, part] + sums_a[128:192]
    done_b = acc_ref[0, :, part] + sums_a[64:128] + sums_b[128:192]
    acc_ref[1, :, part] = sums_a[0:64] + sums_b[64:128]
    acc_ref[0, :, part] = sums_b[0:64]
    return done_a, done_b


def paired_dots(w_ref, ref_a, ref_b, width):
    whole = width // 256 * 256
    for at in range(0, whole, 256):
        part = slice(at, at + 256)
        yield part, [jnp.dot(w_ref[...], ref[:, part], preferred_element_type=F32) for ref in (ref_a, ref_b)]
    if whole < width:
        part = slice(whole, width)
        both = jnp.dot(w_ref[...], jnp.concatenate([ref_a[:, part], ref_b[:, part]], axis=1), preferred_element_type=F32)
        yield part, [both[:, 0:width - whole], both[:, width - whole:]]


def wide(bias, values):
    rows, columns = values.shape
    bias = jnp.concatenate([bias] * (columns // 128), axis=1) if columns > 128 else bias
    return jnp.concatenate([bias] * (rows // bias.shape[0]), axis=0) if rows > bias.shape[0] else bias


def network_kernel(flags_ref, center_ref, edge_a_ref, edge_b_ref,
                   w1_ref, w2_ref, w4_ref, w5_ref, w7_ref, w8_ref, w6_ref, w9_ref, bias_ref, expand_ref,
                   out_ref,
                   col0_ref, first_ref, slot_a_ref, slot_b_ref, acc_ref,
                   skip_ref, pool_ref, col4_ref, col5_ref, col7_ref, col8_ref, flat_ref, last_ref):
    odd_z = flags_ref[1]
    edge_a = edge_a_ref[...].astype(F32)
    edge_b = edge_b_ref[...].astype(F32)
    edges = jnp.concatenate([pick(odd_z, edge_b, edge_a), pick(odd_z, edge_a, edge_b)], axis=1).astype(BF16)
    rows = []
    for b in range(2):
        even, odd = [
            center_ref[2 * b + e] + jnp.dot(edges[24 * b:24 * b + 24], expand_ref[:, FINE * e:FINE * e + FINE],
                                            preferred_element_type=F32)
            for e in range(2)
        ]
        rows.append([moved(odd, 1), even, odd, moved(even, -1)])
    for g in range(3):
        even, odd = [
            jnp.concatenate([part[8 * g:8 * g + 8] for part in rows[b]], axis=0).astype(BF16) for b in range(2)
        ]
        col0_ref[128 * g:128 * g + 128] = jnp.concatenate([moved(odd, ROW), even, odd, moved(even, -ROW)], axis=0)

    bias = bias_ref[0]
    w1_first_ref = w1_ref.at[0:128, 0:128]
    for part, sums in paired_dots(w1_ref, col0_ref.at[0:256], col0_ref.at[128:384], FINE):
        for g in range(2):
            values = leaky(sums[g] + wide(bias, sums[g])).astype(BF16)
            first_ref[8 * g:8 * g + 8, :, part] = values.reshape(8, 64, values.shape[1])
    for part in chunks(FINE):
        sums = jnp.dot(w1_first_ref[...], col0_ref[256:384, part], preferred_element_type=F32)
        values = leaky(sums + wide(bias, sums)).astype(BF16)
        first_ref[16:18, :, part] = values.reshape(2, 64, values.shape[1])

    bias_second = bias_ref[1]

    def gather_first(j, slot_ref):
        for a in range(2):
            slot_ref[a] = window(first_ref[2 * j + a], 0, FINE)

    def skipped_planes(j, slot_ref):
        for part, sums in paired_dots(w2_ref, slot_ref.at[0], slot_ref.at[1], FINE):
            top = None
            for a, done in enumerate(two_planes(*sums, acc_ref, part)):
                values = leaky(done + wide(bias_second, done))
                skip_ref[j, 64 * a:64 * a + 64, part] = values.astype(BF16)
                highest = jnp.max(values.reshape(4, 16, values.shape[1]), axis=0)
                top = highest if top is None else jnp.maximum(top, highest)
            pool_ref[j, :, part] = top.astype(BF16)

    gather_first(0, slot_a_ref)

    def two_steps(t, carry):
        gather_first(2 * t + 1, slot_b_ref)
        skipped_planes(2 * t, slot_a_ref)
        gather_first(2 * t + 2, slot_a_ref)
        skipped_planes(2 * t + 1, slot_b_ref)
        return carry

    lax.fori_loop(0, 4, two_steps, 0)
    skipped_planes(8, slot_a_ref)

    for s in range(8):
        col4_ref[144 * s:144 * s + 144] = neighbours(pool_ref[s + 1], COARSE, COARSE_WIDTH)
    col4_ref[1152:1200] = jnp.zeros((48, COARSE_WIDTH), BF16)
    for d in range(4):
        for a in range(2):
            col7_ref[2 * d + a, 256:512] = window(skip_ref[d + 3, 64 * a:64 * a + 64], RAISED, RAISED_WIDTH)
    bias_coarse = bias_ref[5, 0:32]
    parts = [[], []]
    for _, sums in paired_dots(w4_ref, col4_ref.at[0:768], col4_ref.at[432:1200], COARSE_WIDTH):
        for m in range(2):
            parts[m].append(leaky(sums[m] + wide(bias_coarse, sums[m])).astype(BF16))
    for m in range(2):
        values = jnp.concatenate(parts[m], axis=1)
        for p in range(3):
            at = 288 * (3 * m + p)
            col5_ref[at:at + 288] = neighbours(values[32 * p:32 * p + 32], RAISED - COARSE, RAISED_WIDTH)
    col5_ref[1728:1792] = jnp.zeros((64, RAISED_WIDTH), BF16)

    bias_deeper = bias_ref[6, 0:32]
    bias_raised = bias_ref[2]
    parts = []
    for part in chunks(RAISED_WIDTH):
        sums = jnp.dot(w5_ref[...], col5_ref[:, part], preferred_element_type=F32)
        parts.append(leaky(sums + wide(bias_deeper, sums)).astype(BF16))
    deeper = jnp.concatenate(parts, axis=1)
    for d in range(4):
        parts = []
        for part in chunks(RAISED_WIDTH):
            sums = jnp.dot(w6_ref[...], deeper[32 * d:32 * d + 32, part], preferred_element_type=F32)
            parts.append(leaky(sums + wide(bias_raised, sums)).astype(BF16))
        values = jnp.concatenate(parts, axis=1)
        for a in range(2):
            col7_ref[2 * d + a, 0:256] = window(values[64 * a:64 * a + 64], 0, RAISED_WIDTH)

    bias_joined = bias_ref[3]
    for j in range(4):
        done = [two_planes(*sums, acc_ref, part)
                for part, sums in paired_dots(w7_ref, col7_ref.at[2 * j], col7_ref.at[2 * j + 1], RAISED_WIDTH)]
        if j > 0:
            for a in range(2):
                values = jnp.concatenate([leaky(pair[a] + wide(bias_joined, pair[a])).astype(BF16) for pair in done], axis=1)
                col8_ref[2 * j + a - 2] = window(values, FINAL - RAISED, FINAL_WIDTH)

    bias_final = bias_ref[4]
    output_matrix = w9_ref[...].astype(BF16)
    for j in range(3):
        for part, sums in paired_dots(w8_ref, col8_ref.at[2 * j], col8_ref.at[2 * j + 1], FINAL_WIDTH):
            done = two_planes(*sums, acc_ref, part)
            if j > 0:
                for a in range(2):
                    values = leaky(done[a] + wide(bias_final, done[a])).astype(BF16)
                    predicted = jnp.dot(output_matrix, values, preferred_element_type=F32)
                    to = 4 * (j - 1) + 2 * a
                    flat_ref[0, to:to + 2, part] = predicted[0:2]
                    flat_ref[1, to:to + 2, part] = predicted[2:4]

    for y in range(8):
        at = ROW * (y + 4) - FINAL + 4
        last_ref[8 * y:8 * y + 8, 0:64] = flat_ref[0, :, at:at + 64]
        last_ref[8 * y:8 * y + 8, 64:128] = flat_ref[1, :, at:at + 64]
    old = iota((128, 128), 0)
    turns = (2 * (old % 64) + old // 64 == iota((128, 128), 1)).astype(F32)
    result = jnp.dot(last_ref[...], turns, preferred_element_type=F32, precision=lax.Precision.HIGHEST)
    for y in range(8):
        for x in range(4):
            at = 8 * y + 2 * x
            out_ref[x, 2 * y:2 * y + 2, :] = result[at:at + 2]


def network(flags, center, edge_a, edge_b, weights):
    vmem = pl.BlockSpec(memory_space=pltpu.VMEM)
    scratch = [
        ((384, FINE), BF16), ((18, 64, FINE), BF16), ((2, 256, FINE), BF16), ((2, 256, FINE), BF16),
        ((2, 64, FINE), F32), ((9, 128, FINE), BF16), ((9, 16, FINE), BF16),
        ((1200, COARSE_WIDTH), BF16), ((1792, RAISED_WIDTH), BF16), ((8, 512, RAISED_WIDTH), BF16), ((6, 256, FINAL_WIDTH), BF16),
        ((2, 8, FINAL_WIDTH), F32), ((64, 128), F32),
    ]
    operands = (flags, center, edge_a, edge_b, *weights)
    return pl.pallas_call(
        network_kernel,
        out_shape=jax.ShapeDtypeStruct((4, 16, 128), F32),
        in_specs=[vmem] * len(operands),
        out_specs=vmem,
        scratch_shapes=[pltpu.VMEM(shape, kind) for shape, kind in scratch],
        compiler_params=pltpu.CompilerParams(vmem_limit_bytes=50 * 2**20),
        cost_estimate=pl.CostEstimate(flops=4 * 10**9, bytes_accessed=4 * 10**6, transcendentals=0),
        name="network",
    )(*operands)


def ring(size, step):
    return [(i, (i + step) % size) for i in range(size)]


def partner(i, size, first):
    return (i + 1 if (i % 2 == 1) == first else i - 1) % size


def swaps_y(first):
    return [(gx, 2 * partner(gx // 2, 4, first) + gx % 2) for gx in range(8)]


def swaps_z(first):
    pairs = []
    for gx in range(8):
        for gz in range(8):
            to = partner(gx % 2 * 8 + gz, 16, first)
            pairs.append((gx * 8 + gz, (gx // 2 * 2 + to // 8) * 8 + to % 8))
    return pairs


def exchange(density, half, pack):
    other = lax.ppermute(density, "gx", [(i, i ^ 1) for i in range(8)])
    other, flags = yield other
    mid = jnp.concatenate([jnp.where(half == 0, density, other), jnp.where(half == 0, other, density)], axis=0)
    a = lax.ppermute(mid, "gx", swaps_y(False))
    b = lax.ppermute(mid, "gx", swaps_y(True))
    high = jnp.concatenate([a[:, 8:], mid[:, 8:], b[:, 8:]], axis=0)
    low = jnp.concatenate([a[:, :8], mid[:, :8], b[:, :8]], axis=0)
    low, high = lax.ppermute(high, "gy", ring(8, 1)), lax.ppermute(low, "gy", ring(8, -1))
    left, right, cells = pack(flags, low, a, mid, b, high)
    odd = lax.axis_index("gz") % 2 == 1
    edge_a = lax.ppermute(jnp.where(odd, right, left), ("gx", "gz"), swaps_z(True))
    edge_b = lax.ppermute(jnp.where(odd, left, right), ("gx", "gz"), swaps_z(False))
    yield edge_a, edge_b, cells


def body(density, first_kernel, first_bias, second_kernel, second_bias, coarse_kernel, coarse_bias, deeper_kernel,
         deeper_bias, upward_kernel, upward_bias, joined_kernel, joined_bias, final_kernel, final_bias, output_weight):
    half = (lax.axis_index("gx") % 2).astype(jnp.int32)
    place = jnp.stack([half, lax.axis_index("gx") // 2 % 2, lax.axis_index("gz") % 2]).astype(jnp.int32)
    steps = exchange(density, half, pack_edges)
    other = next(steps)
    kernels = jnp.concatenate([
        jnp.concatenate([second_kernel, final_kernel], axis=4).reshape(432, 32), joined_kernel.reshape(432, 32),
        jnp.swapaxes(coarse_kernel, 3, 4).reshape(432, 32), deeper_kernel.reshape(864, 32), upward_kernel.reshape(128, 32),
    ], axis=0)
    vectors = jnp.concatenate([first_bias, second_bias, upward_bias, joined_bias, final_bias, coarse_bias, deeper_bias,
                               output_weight.astype(F32)]).reshape(1, 160)
    weights = prepare_weights(place, first_kernel.reshape(27, 16), kernels, vectors)
    other, weights = lax.optimization_barrier((other, weights))
    *weights, flags = weights
    sz = weights.pop(6)
    edge_a, edge_b, cells = steps.send((other, flags))
    return network(flags, sample(cells, sz), edge_a, edge_b, weights)


def solution(mesh):
    placed = (P("gx", "gy", "gz"),) + (P(),) * 15
    return jax.shard_map(body, mesh=mesh, in_specs=placed, out_specs=P("gx", "gy", "gz"), check_vma=False)
```

time: 62.4 us -> 60 us (0.962)
  the two profiles are of different devices: /device:TPU:1 before, /device:TPU:6 now
where the time goes in v2:
time: 60 us; the launch traced here: 59.3 us
  starting transfers between devices  30.6 us (51%)
  Pallas kernels  16.2 us (27%)
  waiting for transfers between devices  8.89 us (15%)
  local copies, waits for them, and re-layouts  2.04 us (3%)
  other arithmetic  1.18 us (2%)
    ppermute x1, starting transfers between devices, exchange(): other = lax.ppermute(density, 'gx', [(i, i ^ 1) for i in range(8)])  15.9 us
    pallas_call x1, Pallas kernels, network(): pl.pallas_call(network_kernel, out_shape=jax.ShapeDtypeStruct((4, 16, 128...  12.9 us
    ppermute x1, starting transfers between devices, exchange(): lax.ppermute(jnp.where(odd, right, left), ('gx', 'gz'), swaps_z(True))  4.77 us
    ppermute x1, starting transfers between devices, exchange(): b = lax.ppermute(mid, 'gx', swaps_y(True))  4.09 us
    ppermute x1, starting transfers between devices, exchange(): a = lax.ppermute(mid, 'gx', swaps_y(False))  3.48 us
    ppermute x1, waiting for transfers between devices, exchange(): lax.ppermute(jnp.where(odd, left, right), ('gx', 'gz'), swaps_z(False))  2.96 us
    ppermute x1, waiting for transfers between devices, exchange(): b = lax.ppermute(mid, 'gx', swaps_y(True))  2.9 us
    pallas_call x1, Pallas kernels, prepare_weights(): pl.pallas_call(weights_kernel, out_shape=[jax.ShapeDtypeStruct(s, BF16) f...  2.32 us
  transfers between devices with their start and end apart: 7, of which 4 were waited for; matrix products, arithmetic and copies ran while one was open for 5% of the time, Pallas kernels for 5%

profile of v2, /device:TPU:6, one launch (start us, length us, event | category | flops | bytes accessed | tf_op | source)
XLA Modules:
  0.0 59.3 jit_solution(7350729775052922044)
XLA Ops:
  0.0 0.0 copy-start.3
  0.0 0.0 copy-start.4
  0.0 0.0 copy-start.5
  0.0 0.0 copy-start.9
  0.0 0.0 copy-start.10
  0.1 0.0 copy-start.6
  0.1 0.0 copy-start.7
  0.1 0.0 copy-start.8
  0.1 0.0 copy-start.11
  0.1 15.9 %collective-permute-start = (bf16[4,16,128]{2,1,0:T(8,128)(2,1)}, bf16[4,16,128]{2,1,0:T(8,128)(2,1)S(1)}, u32[]{:S(2)}, u32[]{:S(2)}) collective-permute-start(bf16[4,16,128]{2,1,0:T(8,128)(2,1)} %param.16), channel_id=1, source_target_pairs={{0,64},{64,0},{128,192},{192,128},{256,320},{320,256},{384,448},{4... | collective-permute-start | bytes 49160 | tf_op jit(solution)/shard_map/ppermute | solution.py:423
  16.0 1.1 %pad_maximum_fusion = bf16[3,3,3,16,32]{4,3,2,1,0:T(8,128)(2,1)S(1)} fusion(bf16[3,3,3,16,16]{4,3,2,1,0:T(8,128)(2,1)} %param.29, bf16[3,3,3,16,16]{4,3,2,1,0:T(8,128)(2,1)} %param.19), kind=kLoop, calls=%fused_computation | loop fusion | flops 55296 | bytes 55296 | tf_op jit(solution)/shard_map/concatenate | solution.py:445
  17.1 0.9 %constant_dynamic-update-slice_fusion.3 = bf16[2288,32]{1,0:T(8,128)(2,1)S(1)} fusion(bf16[2288,32]{1,0:T(8,128)(2,1)S(1)} %constant_dynamic-update-slice_fusion.4, bf16[432,32]{1,0:T(8,128)(2,1)} %bitcast.16), kind=kLoop, calls=%fused_computation.17 | loop fusion | bytes 138240
  18.0 0.9 %constant_dynamic-update-slice_fusion.2 = bf16[2288,32]{1,0:T(8,128)(2,1)S(1)} fusion(bf16[2288,32]{1,0:T(8,128)(2,1)S(1)} %constant_dynamic-update-slice_fusion.3, bf16[432,32]{1,0:T(8,128)(2,1)} %bitcast.17), kind=kLoop, calls=%fused_computation.16 | loop fusion | bytes 138240
  19.0 0.1 pad_add_fusion.place_ref
  19.2 0.1 concatenate.20
  19.3 2.3 %weights.1 = (bf16[512,256]{1,0:T(8,128)(2,1)S(1)}, bf16[192,256]{1,0:T(8,128)(2,1)S(1)}, bf16[96,768]{1,0:T(8,128)(2,1)S(1)}, bf16[128,1792]{1,0:T(8,128)(2,1)S...) custom-call(s32[3]{0:T(128)S(1)} %pad_add_fusion.place_ref, ...), custom_call_target="tpu_custom_call" | custom-call | flops 10000000 | bytes 2000000 | tf_op jit(solution)/shard_map/weights/pallas_call | solution.py:115
  21.6 0.0 collective-permute-done
  21.6 3.5 %collective-permute-start.1 = (bf16[8,16,128]{2,1,0:T(8,128)(2,1)S(1)}, bf16[8,16,128]{2,1,0:T(8,128)(2,1)S(1)}, u32[]{:S(2)}, u32[]{:S(2)}) collective-permute-start(bf16[8,16,128]{2,1,0:T(8,128)(2,1)S(1)} %pad_maximum_fusion.3.mid_ref), channel_id=1, source_target_pairs={{0,128},{64,192},{128,0},{192,64},{256,384},{320,448},{384,256},{4... | collective-permute-start | bytes 98312 | tf_op jit(solution)/shard_map/ppermute | solution.py:426
  25.1 4.1 %collective-permute-start.2 = (bf16[8,16,128]{2,1,0:T(8,128)(2,1)S(1)}, bf16[8,16,128]{2,1,0:T(8,128)(2,1)S(1)}, u32[]{:S(2)}, u32[]{:S(2)}) collective-permute-start(bf16[8,16,128]{2,1,0:T(8,128)(2,1)S(1)} %pad_maximum_fusion.3.mid_ref), channel_id=1, source_target_pairs={{0,384},{64,448},{128,256},{192,320},{256,128},{320,192},{384,0},{... | collective-permute-start | bytes 98312 | tf_op jit(solution)/shard_map/ppermute | solution.py:427
  29.2 0.0 collective-permute-done.1.a_ref
  29.3 2.9 %collective-permute-done.2.b_ref = bf16[8,16,128]{2,1,0:T(8,128)(2,1)S(1)} collective-permute-done((bf16[8,16,128]{2,1,0:T(8,128)(2,1)S(1)}, bf16[8,16,128]{2,1,0:T(8,128)(2,1)S(1)}, u32[]{:S(2)}, u32[]{:S(2)}) %collective-permute-start.2) | collective-permute-done | bytes 32800 | tf_op jit(solution)/shard_map/ppermute | solution.py:427
  32.2 0.0 collective-permute-start.4
  32.2 0.5 collective-permute-start.3
  32.7 1.2 %collective-permute-done.4.high_ref = bf16[24,8,128]{2,1,0:T(8,128)(2,1)S(1)} collective-permute-done((bf16[24,8,128]{2,1,0:T(8,128)(2,1)S(1)}, bf16[24,8,128]{2,1,0:T(8,128)(2,1)S(1)}, u32[]{:S(2)}, u32[]{:S(2)}) %collective-permute-start.4) | collective-permute-done | bytes 49184 | tf_op jit(solution)/shard_map/ppermute | solution.py:430
  33.9 1.8 %collective-permute-done.3.low_ref = bf16[24,8,128]{2,1,0:T(8,128)(2,1)S(1)} collective-permute-done((bf16[24,8,128]{2,1,0:T(8,128)(2,1)S(1)}, bf16[24,8,128]{2,1,0:T(8,128)(2,1)S(1)}, u32[]{:S(2)}, u32[]{:S(2)}) %collective-permute-start.3) | collective-permute-done | bytes 49184 | tf_op jit(solution)/shard_map/ppermute | solution.py:430
  35.7 0.3 edges.1
  36.1 4.8 %collective-permute-start.5 = (bf16[48,128]{1,0:T(8,128)(2,1)S(1)}, bf16[48,128]{1,0:T(8,128)(2,1)S(1)}, u32[]{:S(2)}, u32[]{:S(2)}) collective-permute-start(bf16[48,128]{1,0:T(8,128)(2,1)S(1)} %get-tuple-element.70), channel_id=1, source_target_pairs={{0,71},{1,2},{2,1},{3,4},{4,3},{5,6},{6,5},{7,64},{64,7},{65,66},{... | collective-permute-start | bytes 36872 | tf_op jit(solution)/shard_map/ppermute | solution.py:433
  40.8 1.9 %collective-permute-start.6 = (bf16[48,128]{1,0:T(8,128)(2,1)S(1)}, bf16[48,128]{1,0:T(8,128)(2,1)S(1)}, u32[]{:S(2)}, u32[]{:S(2)}) collective-permute-start(bf16[48,128]{1,0:T(8,128)(2,1)S(1)} %get-tuple-element.69), channel_id=1, source_target_pairs={{0,1},{1,0},{2,3},{3,2},{4,5},{5,4},{6,7},{7,6},{64,65},{65,64},{6... | collective-permute-start | bytes 36872 | tf_op jit(solution)/shard_map/ppermute | solution.py:434
  42.8 0.7 %sample.1.center_ref = f32[4,24,1152]{2,1,0:T(8,128)S(1)} custom-call(f32[768,128]{1,0:T(8,128)S(1)} %get-tuple-element.47.cells_ref, bf16[128,256]{1,0:T(8,128)(2,1)S(1)} %get-tuple-element.48.sz_ref), custom_call_target="tpu_custom_call" | custom-call | flops 100000000 | bytes 1000000 | tf_op jit(solution)/shard_map/sample/pallas_call | solution.py:182
  43.5 0.0 collective-permute-done.5.edge_a_ref
  43.5 3.0 %collective-permute-done.6.edge_b_ref = bf16[48,128]{1,0:T(8,128)(2,1)S(1)} collective-permute-done((bf16[48,128]{1,0:T(8,128)(2,1)S(1)}, bf16[48,128]{1,0:T(8,128)(2,1)S(1)}, u32[]{:S(2)}, u32[]{:S(2)}) %collective-permute-start.6) | collective-permute-done | bytes 12320 | tf_op jit(solution)/shard_map/ppermute | solution.py:434
  46.4 12.9 %network.1 = f32[4,16,128]{2,1,0:T(8,128)} custom-call(f32[2,8,128]{2,1,0:T(8,128)S(1)} %get-tuple-element.45.flags_ref, f32[4,24,1152]{2,1,0:T(8,128)S(1)} %sample.1.center_ref, bf16[48,128]{1,0:T(8,128)(2,1)S(1)} %collective-permute-done.5.edge_a_ref, bf16[48,128]{1,0:T(8,128)(2,1)S(1)} %collective-permute-done.6.edge_b_ref, ...), custom_call_target="tpu_custom_call" | custom-call | flops 4000000000 | bytes 4000000 | tf_op jit(solution)/shard_map/network/pallas_call | solution.py:389
  (27 shorter events, 0.2 us)
Async XLA Ops:
  0.0 21.6 %copy-start.2 = (bf16[4,16,128]{2,1,0:T(8,128)(2,1)S(1)}, bf16[4,16,128]{2,1,0:T(8,128)(2,1)}, u32[]{:S(2)}) copy-start(bf16[4,16,128]{2,1,0:T(8,128)(2,1)} %param.16) | copy-start | bytes 49156
  0.0 18.9 %copy-start = (bf16[3,3,3,32,32]{4,3,2,1,0:T(8,128)(2,1)S(1)}, bf16[3,3,3,32,32]{4,3,2,1,0:T(8,128)(2,1)}, u32[]{:S(2)}) copy-start(bf16[3,3,3,32,32]{4,3,2,1,0:T(8,128)(2,1)} %param.23) | copy-start | bytes 165892
  0.0 19.0 %copy-start.1 = (bf16[2,2,2,16,32]{4,3,2,1,0:T(8,128)(2,1)S(1)}, bf16[2,2,2,16,32]{4,3,2,1,0:T(8,128)(2,1)}, u32[]{:S(2)}) copy-start(bf16[2,2,2,16,32]{4,3,2,1,0:T(8,128)(2,1)} %param.25) | copy-start | bytes 24580
  0.0 19.1 %copy-start.3 = (bf16[3,3,3,16,1]{3,2,4,1,0:T(4,128)(2,1)S(1)}, bf16[3,3,3,16,1]{3,2,4,1,0:T(4,128)(2,1)}, u32[]{:S(2)}) copy-start(bf16[3,3,3,16,1]{3,2,4,1,0:T(4,128)(2,1)} %param.17) | copy-start | bytes 2596
  0.0 19.1 %copy-start.4 = (f32[16]{0:T(128)S(1)}, f32[16]{0:T(128)}, u32[]{:S(2)}) copy-start(f32[16]{0:T(128)} %param.18) | copy-start | bytes 196
  0.0 19.1 %copy-start.5 = (f32[16]{0:T(128)S(1)}, f32[16]{0:T(128)}, u32[]{:S(2)}) copy-start(f32[16]{0:T(128)} %param.20) | copy-start | bytes 196
  0.0 19.1 %copy-start.9 = (f32[32]{0:T(128)S(1)}, f32[32]{0:T(128)}, u32[]{:S(2)}) copy-start(f32[32]{0:T(128)} %param.22) | copy-start | bytes 388
  0.0 19.1 %copy-start.10 = (f32[32]{0:T(128)S(1)}, f32[32]{0:T(128)}, u32[]{:S(2)}) copy-start(f32[32]{0:T(128)} %param.24) | copy-start | bytes 388
  0.1 19.1 %copy-start.6 = (f32[16]{0:T(128)S(1)}, f32[16]{0:T(128)}, u32[]{:S(2)}) copy-start(f32[16]{0:T(128)} %param.26) | copy-start | bytes 196
  0.1 19.1 %copy-start.7 = (f32[16]{0:T(128)S(1)}, f32[16]{0:T(128)}, u32[]{:S(2)}) copy-start(f32[16]{0:T(128)} %param.28) | copy-start | bytes 196
  0.1 19.1 %copy-start.8 = (f32[16]{0:T(128)S(1)}, f32[16]{0:T(128)}, u32[]{:S(2)}) copy-start(f32[16]{0:T(128)} %param.30) | copy-start | bytes 196
  0.1 19.1 %copy-start.11 = (bf16[16]{0:T(256)(128)(2,1)S(1)}, bf16[16]{0:T(256)(128)(2,1)}, u32[]{:S(2)}) copy-start(bf16[16]{0:T(256)(128)(2,1)} %param.31) | copy-start | bytes 100
  0.1 21.5 %collective-permute-start = (bf16[4,16,128]{2,1,0:T(8,128)(2,1)}, bf16[4,16,128]{2,1,0:T(8,128)(2,1)S(1)}, u32[]{:S(2)}, u32[]{:S(2)}) collective-permute-start(bf16[4,16,128]{2,1,0:T(8,128)(2,1)} %param.16), channel_id=1, source_target_pairs={{0,64},{64,0},{128,192},{192,128},{256,320},{320,256},{384,448},{4... | collective-permute-start | bytes 49160 | tf_op jit(solution)/shard_map/ppermute | solution.py:423
  21.6 7.6 %collective-permute-start.1 = (bf16[8,16,128]{2,1,0:T(8,128)(2,1)S(1)}, bf16[8,16,128]{2,1,0:T(8,128)(2,1)S(1)}, u32[]{:S(2)}, u32[]{:S(2)}) collective-permute-start(bf16[8,16,128]{2,1,0:T(8,128)(2,1)S(1)} %pad_maximum_fusion.3.mid_ref), channel_id=1, source_target_pairs={{0,128},{64,192},{128,0},{192,64},{256,384},{320,448},{384,256},{4... | collective-permute-start | bytes 98312 | tf_op jit(solution)/shard_map/ppermute | solution.py:426
  25.1 7.0 %collective-permute-start.2 = (bf16[8,16,128]{2,1,0:T(8,128)(2,1)S(1)}, bf16[8,16,128]{2,1,0:T(8,128)(2,1)S(1)}, u32[]{:S(2)}, u32[]{:S(2)}) collective-permute-start(bf16[8,16,128]{2,1,0:T(8,128)(2,1)S(1)} %pad_maximum_fusion.3.mid_ref), channel_id=1, source_target_pairs={{0,384},{64,448},{128,256},{192,320},{256,128},{320,192},{384,0},{... | collective-permute-start | bytes 98312 | tf_op jit(solution)/shard_map/ppermute | solution.py:427
  32.2 1.8 %collective-permute-start.4 = (bf16[24,8,128]{2,1,0:T(8,128)(2,1)S(1)}, bf16[24,8,128]{2,1,0:T(8,128)(2,1)S(1)}, u32[]{:S(2)}, u32[]{:S(2)}) collective-permute-start(bf16[24,8,128]{2,1,0:T(8,128)(2,1)S(1)} %pad_maximum_fusion.2), channel_id=1, source_target_pairs={{0,56},{8,0},{16,8},{24,16},{32,24},{40,32},{48,40},{56,48},{1,57}... | collective-permute-start | bytes 147464 | tf_op jit(solution)/shard_map/ppermute | solution.py:430
  32.2 3.5 %collective-permute-start.3 = (bf16[24,8,128]{2,1,0:T(8,128)(2,1)S(1)}, bf16[24,8,128]{2,1,0:T(8,128)(2,1)S(1)}, u32[]{:S(2)}, u32[]{:S(2)}) collective-permute-start(bf16[24,8,128]{2,1,0:T(8,128)(2,1)S(1)} %pad_maximum_fusion.1), channel_id=1, source_target_pairs={{0,8},{8,16},{16,24},{24,32},{32,40},{40,48},{48,56},{56,0},{1,9},... | collective-permute-start | bytes 147464 | tf_op jit(solution)/shard_map/ppermute | solution.py:430
  36.1 7.4 %collective-permute-start.5 = (bf16[48,128]{1,0:T(8,128)(2,1)S(1)}, bf16[48,128]{1,0:T(8,128)(2,1)S(1)}, u32[]{:S(2)}, u32[]{:S(2)}) collective-permute-start(bf16[48,128]{1,0:T(8,128)(2,1)S(1)} %get-tuple-element.70), channel_id=1, source_target_pairs={{0,71},{1,2},{2,1},{3,4},{4,3},{5,6},{6,5},{7,64},{64,7},{65,66},{... | collective-permute-start | bytes 36872 | tf_op jit(solution)/shard_map/ppermute | solution.py:433
  40.8 5.6 %collective-permute-start.6 = (bf16[48,128]{1,0:T(8,128)(2,1)S(1)}, bf16[48,128]{1,0:T(8,128)(2,1)S(1)}, u32[]{:S(2)}, u32[]{:S(2)}) collective-permute-start(bf16[48,128]{1,0:T(8,128)(2,1)S(1)} %get-tuple-element.69), channel_id=1, source_target_pairs={{0,1},{1,0},{2,3},{3,2},{4,5},{5,4},{6,7},{7,6},{64,65},{65,64},{6... | collective-permute-start | bytes 36872 | tf_op jit(solution)/shard_map/ppermute | solution.py:434

commit v3 on v2

--- a/solution.py
+++ b/solution.py
@@ -83,7 +83,9 @@
         for n in range(4):
             move = (n // 2) * 64 + (n % 2) * 16
             at = 64 * u + 16 * n
-            w7_ref[at:at + 16] = (pltpu.roll(block, move, 1) if n else block).astype(BF16)
+            rows = (pltpu.roll(block, move, 1) if n else block).astype(BF16)
+            for side in range(2):
+                w7_ref[side, at:at + 16] = rows[:, 256 * side:256 * side + 256]
 
     same = (iota((432, 768), 0) == iota((432, 768), 1)).astype(BF16)
     block = lax.dot_general(kernels_ref[864:1296], same, (((0,), (0,)), ((), ())), preferred_element_type=F32)
@@ -110,7 +112,7 @@
 
 
 def prepare_weights(place, first, kernels, vectors):
-    shapes = [(512, 256), (192, 256), (96, 768), (128, 1792), (192, 512), (192, 256), (128, 256), (128, 32)]
+    shapes = [(512, 256), (192, 256), (96, 768), (128, 1792), (2, 192, 256), (192, 256), (128, 256), (128, 32)]
     vmem = pl.BlockSpec(memory_space=pltpu.VMEM)
     return pl.pallas_call(
         weights_kernel,
@@ -138,9 +140,9 @@
             jnp.concatenate([low_ref[8 * g + x], ref[x], high_ref[8 * g + x]], axis=0).astype(F32)
             for g, ref in enumerate((a_ref, mid_ref, b_ref))
         ]
-        cells_ref[32 * x:32 * x + 32] = pick(odd_y, planes[0], planes[2])
+        cells_ref[32 * x:32 * x + 32] = pick(odd_y, planes[2], planes[0])
         cells_ref[32 * (8 + x):32 * (8 + x) + 32] = planes[1]
-        cells_ref[32 * (16 + x):32 * (16 + x) + 32] = pick(odd_y, planes[2], planes[0])
+        cells_ref[32 * (16 + x):32 * (16 + x) + 32] = pick(odd_y, planes[0], planes[2])
     left = [jnp.zeros((24, 128), F32)] * 2
     right = [jnp.zeros((24, 128), F32)] * 2
     lane = iota((24, 128), 1)
@@ -250,18 +252,15 @@
                    w1_ref, w2_ref, w4_ref, w5_ref, w7_ref, w8_ref, w6_ref, w9_ref, bias_ref, expand_ref,
                    out_ref,
                    col0_ref, first_ref, slot_a_ref, slot_b_ref, acc_ref,
-                   skip_ref, pool_ref, col4_ref, col5_ref, col7_ref, col8_ref, flat_ref, last_ref):
+                   skip_ref, pool_ref, col4_ref, col5_ref, col7_ref, raised_ref, merged_ref, col8_ref, flat_ref, last_ref):
     odd_z = flags_ref[1]
     edge_a = edge_a_ref[...].astype(F32)
     edge_b = edge_b_ref[...].astype(F32)
     edges = jnp.concatenate([pick(odd_z, edge_b, edge_a), pick(odd_z, edge_a, edge_b)], axis=1).astype(BF16)
+    placed = [jnp.dot(edges, expand_ref[:, FINE * e:FINE * e + FINE], preferred_element_type=F32) for e in range(2)]
     rows = []
     for b in range(2):
-        even, odd = [
-            center_ref[2 * b + e] + jnp.dot(edges[24 * b:24 * b + 24], expand_ref[:, FINE * e:FINE * e + FINE],
-                                            preferred_element_type=F32)
-            for e in range(2)
-        ]
+        even, odd = [center_ref[2 * b + e] + placed[e][24 * b:24 * b + 24] for e in range(2)]
         rows.append([moved(odd, 1), even, odd, moved(even, -1)])
     for g in range(3):
         even, odd = [
@@ -313,7 +312,13 @@
     col4_ref[1152:1200] = jnp.zeros((48, COARSE_WIDTH), BF16)
     for d in range(4):
         for a in range(2):
-            col7_ref[2 * d + a, 256:512] = window(skip_ref[d + 3, 64 * a:64 * a + 64], RAISED, RAISED_WIDTH)
+            col7_ref[2 * d + a] = window(skip_ref[d + 3, 64 * a:64 * a + 64], RAISED, RAISED_WIDTH)
+    for j in range(4):
+        for part, sums in paired_dots(w7_ref.at[1], col7_ref.at[2 * j], col7_ref.at[2 * j + 1], RAISED_WIDTH):
+            for a, done in enumerate(two_planes(*sums, acc_ref, part)):
+                if j > 0:
+                    merged_ref[2 * j + a - 2, :, part] = done
+
     bias_coarse = bias_ref[5, 0:32]
     parts = [[], []]
     for _, sums in paired_dots(w4_ref, col4_ref.at[0:768], col4_ref.at[432:1200], COARSE_WIDTH):
@@ -340,15 +345,19 @@
             parts.append(leaky(sums + wide(bias_raised, sums)).astype(BF16))
         values = jnp.concatenate(parts, axis=1)
         for a in range(2):
-            col7_ref[2 * d + a, 0:256] = window(values[64 * a:64 * a + 64], 0, RAISED_WIDTH)
+            raised_ref[2 * d + a] = window(values[64 * a:64 * a + 64], 0, RAISED_WIDTH)
 
     bias_joined = bias_ref[3]
     for j in range(4):
-        done = [two_planes(*sums, acc_ref, part)
-                for part, sums in paired_dots(w7_ref, col7_ref.at[2 * j], col7_ref.at[2 * j + 1], RAISED_WIDTH)]
+        parts = [[], []]
+        for part, sums in paired_dots(w7_ref.at[0], raised_ref.at[2 * j], raised_ref.at[2 * j + 1], RAISED_WIDTH):
+            for a, done in enumerate(two_planes(*sums, acc_ref, part)):
+                if j > 0:
+                    done = done + merged_ref[2 * j + a - 2, :, part]
+                    parts[a].append(leaky(done + wide(bias_joined, done)).astype(BF16))
         if j > 0:
             for a in range(2):
-                values = jnp.concatenate([leaky(pair[a] + wide(bias_joined, pair[a])).astype(BF16) for pair in done], axis=1)
+                values = jnp.concatenate(parts[a], axis=1)
                 col8_ref[2 * j + a - 2] = window(values, FINAL - RAISED, FINAL_WIDTH)
 
     bias_final = bias_ref[4]
@@ -382,7 +391,8 @@
     scratch = [
         ((384, FINE), BF16), ((18, 64, FINE), BF16), ((2, 256, FINE), BF16), ((2, 256, FINE), BF16),
         ((2, 64, FINE), F32), ((9, 128, FINE), BF16), ((9, 16, FINE), BF16),
-        ((1200, COARSE_WIDTH), BF16), ((1792, RAISED_WIDTH), BF16), ((8, 512, RAISED_WIDTH), BF16), ((6, 256, FINAL_WIDTH), BF16),
+        ((1200, COARSE_WIDTH), BF16), ((1792, RAISED_WIDTH), BF16), ((8, 256, RAISED_WIDTH), BF16),
+        ((8, 256, RAISED_WIDTH), BF16), ((6, 64, RAISED_WIDTH), F32), ((6, 256, FINAL_WIDTH), BF16),
         ((2, 8, FINAL_WIDTH), F32), ((64, 128), F32),
     ]
     operands = (flags, center, edge_a, edge_b, *weights)
@@ -423,8 +433,8 @@
     other = lax.ppermute(density, "gx", [(i, i ^ 1) for i in range(8)])
     other, flags = yield other
     mid = jnp.concatenate([jnp.where(half == 0, density, other), jnp.where(half == 0, other, density)], axis=0)
-    a = lax.ppermute(mid, "gx", swaps_y(False))
-    b = lax.ppermute(mid, "gx", swaps_y(True))
+    a = lax.ppermute(mid, "gx", swaps_y(True))
+    b = lax.ppermute(mid, "gx", swaps_y(False))
     high = jnp.concatenate([a[:, 8:], mid[:, 8:], b[:, 8:]], axis=0)
     low = jnp.concatenate([a[:, :8], mid[:, :8], b[:, :8]], axis=0)
     low, high = lax.ppermute(high, "gy", ring(8, 1)), lax.ppermute(low, "gy", ring(8, -1))

time: 60 us -> 60.1 us (level)
  waiting for transfers between devices: 8.89 us -> 9.73 us
    ppermute x2, waiting for transfers between devices: 2.9 us -> 3.75 us  [the longest x1 3.73 us: exchange(): b = lax.ppermute(mid, 'gx', swaps_y(False))]
    ppermute x2, starting transfers between devices: 7.57 us -> 6.97 us  [the longest x1 4.92 us: exchange(): a = lax.ppermute(mid, 'gx', swaps_y(True))]
where the time goes in v3:
time: 60.1 us; the launch traced here: 59.8 us
  starting transfers between devices  30 us (50%)
  Pallas kernels  16.5 us (27%)
  waiting for transfers between devices  9.73 us (16%)
  local copies, waits for them, and re-layouts  2.04 us (3%)
  other arithmetic  1.18 us (2%)
    ppermute x1, starting transfers between devices, exchange(): other = lax.ppermute(density, 'gx', [(i, i ^ 1) for i in range(8)])  15.9 us
    pallas_call x1, Pallas kernels, network(): pl.pallas_call(network_kernel, out_shape=jax.ShapeDtypeStruct((4, 16, 128...  13.1 us
    ppermute x1, starting transfers between devices, exchange(): a = lax.ppermute(mid, 'gx', swaps_y(True))  4.92 us
    ppermute x1, starting transfers between devices, exchange(): lax.ppermute(jnp.where(odd, right, left), ('gx', 'gz'), swaps_z(True))  4.77 us
    ppermute x1, waiting for transfers between devices, exchange(): b = lax.ppermute(mid, 'gx', swaps_y(False))  3.73 us
    ppermute x1, waiting for transfers between devices, exchange(): lax.ppermute(jnp.where(odd, left, right), ('gx', 'gz'), swaps_z(False))  2.96 us
    pallas_call x1, Pallas kernels, prepare_weights(): pl.pallas_call(weights_kernel, out_shape=[jax.ShapeDtypeStruct(s, BF16) f...  2.32 us
    ppermute x1, starting transfers between devices, exchange(): b = lax.ppermute(mid, 'gx', swaps_y(False))  2.05 us
  transfers between devices with their start and end apart: 7, of which 4 were waited for; matrix products, arithmetic and copies ran while one was open for 5% of the time, Pallas kernels for 5%

profile of v3, /device:TPU:6, one launch (start us, length us, event | category | flops | bytes accessed | tf_op | source)
XLA Modules:
  0.0 59.8 jit_solution(6908018827547488695)
XLA Ops:
  0.0 0.0 copy-start.3
  0.0 0.0 copy-start.4
  0.0 0.0 copy-start.5
  0.0 0.0 copy-start.9
  0.0 0.0 copy-start.10
  0.1 0.0 copy-start.6
  0.1 0.0 copy-start.7
  0.1 0.0 copy-start.8
  0.1 0.0 copy-start.11
  0.1 15.9 %collective-permute-start = (bf16[4,16,128]{2,1,0:T(8,128)(2,1)}, bf16[4,16,128]{2,1,0:T(8,128)(2,1)S(1)}, u32[]{:S(2)}, u32[]{:S(2)}) collective-permute-start(bf16[4,16,128]{2,1,0:T(8,128)(2,1)} %param.16), channel_id=1, source_target_pairs={{0,64},{64,0},{128,192},{192,128},{256,320},{320,256},{384,448},{4... | collective-permute-start | bytes 49160 | tf_op jit(solution)/shard_map/ppermute | solution.py:433
  16.0 1.1 %pad_maximum_fusion = bf16[3,3,3,16,32]{4,3,2,1,0:T(8,128)(2,1)S(1)} fusion(bf16[3,3,3,16,16]{4,3,2,1,0:T(8,128)(2,1)} %param.29, bf16[3,3,3,16,16]{4,3,2,1,0:T(8,128)(2,1)} %param.19), kind=kLoop, calls=%fused_computation | loop fusion | flops 55296 | bytes 55296 | tf_op jit(solution)/shard_map/concatenate | solution.py:455
  17.1 0.9 %constant_dynamic-update-slice_fusion.3 = bf16[2288,32]{1,0:T(8,128)(2,1)S(1)} fusion(bf16[2288,32]{1,0:T(8,128)(2,1)S(1)} %constant_dynamic-update-slice_fusion.4, bf16[432,32]{1,0:T(8,128)(2,1)} %bitcast.16), kind=kLoop, calls=%fused_computation.17 | loop fusion | bytes 138240
  18.0 0.9 %constant_dynamic-update-slice_fusion.2 = bf16[2288,32]{1,0:T(8,128)(2,1)S(1)} fusion(bf16[2288,32]{1,0:T(8,128)(2,1)S(1)} %constant_dynamic-update-slice_fusion.3, bf16[432,32]{1,0:T(8,128)(2,1)} %bitcast.17), kind=kLoop, calls=%fused_computation.16 | loop fusion | bytes 138240
  19.0 0.1 pad_add_fusion.place_ref
  19.2 0.1 concatenate.20
  19.3 2.3 %weights.1 = (bf16[512,256]{1,0:T(8,128)(2,1)S(1)}, bf16[192,256]{1,0:T(8,128)(2,1)S(1)}, bf16[96,768]{1,0:T(8,128)(2,1)S(1)}, bf16[128,1792]{1,0:T(8,128)(2,1)S...) custom-call(s32[3]{0:T(128)S(1)} %pad_add_fusion.place_ref, ...), custom_call_target="tpu_custom_call" | custom-call | flops 10000000 | bytes 2000000 | tf_op jit(solution)/shard_map/weights/pallas_call | solution.py:117
  21.6 0.0 collective-permute-done
  21.6 4.9 %collective-permute-start.1 = (bf16[8,16,128]{2,1,0:T(8,128)(2,1)S(1)}, bf16[8,16,128]{2,1,0:T(8,128)(2,1)S(1)}, u32[]{:S(2)}, u32[]{:S(2)}) collective-permute-start(bf16[8,16,128]{2,1,0:T(8,128)(2,1)S(1)} %pad_maximum_fusion.3.mid_ref), channel_id=1, source_target_pairs={{0,384},{64,448},{128,256},{192,320},{256,128},{320,192},{384,0},{... | collective-permute-start | bytes 98312 | tf_op jit(solution)/shard_map/ppermute | solution.py:436
  26.6 2.0 %collective-permute-start.2 = (bf16[8,16,128]{2,1,0:T(8,128)(2,1)S(1)}, bf16[8,16,128]{2,1,0:T(8,128)(2,1)S(1)}, u32[]{:S(2)}, u32[]{:S(2)}) collective-permute-start(bf16[8,16,128]{2,1,0:T(8,128)(2,1)S(1)} %pad_maximum_fusion.3.mid_ref), channel_id=1, source_target_pairs={{0,128},{64,192},{128,0},{192,64},{256,384},{320,448},{384,256},{4... | collective-permute-start | bytes 98312 | tf_op jit(solution)/shard_map/ppermute | solution.py:437
  28.6 0.0 collective-permute-done.1.a_ref
  28.7 3.7 %collective-permute-done.2.b_ref = bf16[8,16,128]{2,1,0:T(8,128)(2,1)S(1)} collective-permute-done((bf16[8,16,128]{2,1,0:T(8,128)(2,1)S(1)}, bf16[8,16,128]{2,1,0:T(8,128)(2,1)S(1)}, u32[]{:S(2)}, u32[]{:S(2)}) %collective-permute-start.2) | collective-permute-done | bytes 32800 | tf_op jit(solution)/shard_map/ppermute | solution.py:437
  32.4 0.0 collective-permute-start.4
  32.4 0.5 collective-permute-start.3
  32.9 1.2 %collective-permute-done.4.high_ref = bf16[24,8,128]{2,1,0:T(8,128)(2,1)S(1)} collective-permute-done((bf16[24,8,128]{2,1,0:T(8,128)(2,1)S(1)}, bf16[24,8,128]{2,1,0:T(8,128)(2,1)S(1)}, u32[]{:S(2)}, u32[]{:S(2)}) %collective-permute-start.4) | collective-permute-done | bytes 49184 | tf_op jit(solution)/shard_map/ppermute | solution.py:440
  34.2 1.8 %collective-permute-done.3.low_ref = bf16[24,8,128]{2,1,0:T(8,128)(2,1)S(1)} collective-permute-done((bf16[24,8,128]{2,1,0:T(8,128)(2,1)S(1)}, bf16[24,8,128]{2,1,0:T(8,128)(2,1)S(1)}, u32[]{:S(2)}, u32[]{:S(2)}) %collective-permute-start.3) | collective-permute-done | bytes 49184 | tf_op jit(solution)/shard_map/ppermute | solution.py:440
  36.0 0.3 edges.1
  36.3 4.8 %collective-permute-start.5 = (bf16[48,128]{1,0:T(8,128)(2,1)S(1)}, bf16[48,128]{1,0:T(8,128)(2,1)S(1)}, u32[]{:S(2)}, u32[]{:S(2)}) collective-permute-start(bf16[48,128]{1,0:T(8,128)(2,1)S(1)} %get-tuple-element.70), channel_id=1, source_target_pairs={{0,71},{1,2},{2,1},{3,4},{4,3},{5,6},{6,5},{7,64},{64,7},{65,66},{... | collective-permute-start | bytes 36872 | tf_op jit(solution)/shard_map/ppermute | solution.py:443
  41.1 1.9 %collective-permute-start.6 = (bf16[48,128]{1,0:T(8,128)(2,1)S(1)}, bf16[48,128]{1,0:T(8,128)(2,1)S(1)}, u32[]{:S(2)}, u32[]{:S(2)}) collective-permute-start(bf16[48,128]{1,0:T(8,128)(2,1)S(1)} %get-tuple-element.69), channel_id=1, source_target_pairs={{0,1},{1,0},{2,3},{3,2},{4,5},{5,4},{6,7},{7,6},{64,65},{65,64},{6... | collective-permute-start | bytes 36872 | tf_op jit(solution)/shard_map/ppermute | solution.py:444
  43.0 0.7 %sample.1.center_ref = f32[4,24,1152]{2,1,0:T(8,128)S(1)} custom-call(f32[768,128]{1,0:T(8,128)S(1)} %get-tuple-element.47.cells_ref, bf16[128,256]{1,0:T(8,128)(2,1)S(1)} %get-tuple-element.48.sz_ref), custom_call_target="tpu_custom_call" | custom-call | flops 100000000 | bytes 1000000 | tf_op jit(solution)/shard_map/sample/pallas_call | solution.py:184
  43.7 0.0 collective-permute-done.5.edge_a_ref
  43.7 3.0 %collective-permute-done.6.edge_b_ref = bf16[48,128]{1,0:T(8,128)(2,1)S(1)} collective-permute-done((bf16[48,128]{1,0:T(8,128)(2,1)S(1)}, bf16[48,128]{1,0:T(8,128)(2,1)S(1)}, u32[]{:S(2)}, u32[]{:S(2)}) %collective-permute-start.6) | collective-permute-done | bytes 12320 | tf_op jit(solution)/shard_map/ppermute | solution.py:444
  46.7 13.1 %network.1 = f32[4,16,128]{2,1,0:T(8,128)} custom-call(f32[2,8,128]{2,1,0:T(8,128)S(1)} %get-tuple-element.45.flags_ref, f32[4,24,1152]{2,1,0:T(8,128)S(1)} %sample.1.center_ref, bf16[48,128]{1,0:T(8,128)(2,1)S(1)} %collective-permute-done.5.edge_a_ref, bf16[48,128]{1,0:T(8,128)(2,1)S(1)} %collective-permute-done.6.edge_b_ref, ...), custom_call_target="tpu_custom_call" | custom-call | flops 4000000000 | bytes 4000000 | tf_op jit(solution)/shard_map/network/pallas_call | solution.py:399
  (27 shorter events, 0.2 us)
Async XLA Ops:
  0.0 21.6 %copy-start.2 = (bf16[4,16,128]{2,1,0:T(8,128)(2,1)S(1)}, bf16[4,16,128]{2,1,0:T(8,128)(2,1)}, u32[]{:S(2)}) copy-start(bf16[4,16,128]{2,1,0:T(8,128)(2,1)} %param.16) | copy-start | bytes 49156
  0.0 18.9 %copy-start = (bf16[3,3,3,32,32]{4,3,2,1,0:T(8,128)(2,1)S(1)}, bf16[3,3,3,32,32]{4,3,2,1,0:T(8,128)(2,1)}, u32[]{:S(2)}) copy-start(bf16[3,3,3,32,32]{4,3,2,1,0:T(8,128)(2,1)} %param.23) | copy-start | bytes 165892
  0.0 19.0 %copy-start.1 = (bf16[2,2,2,16,32]{4,3,2,1,0:T(8,128)(2,1)S(1)}, bf16[2,2,2,16,32]{4,3,2,1,0:T(8,128)(2,1)}, u32[]{:S(2)}) copy-start(bf16[2,2,2,16,32]{4,3,2,1,0:T(8,128)(2,1)} %param.25) | copy-start | bytes 24580
  0.0 19.1 %copy-start.3 = (bf16[3,3,3,16,1]{3,2,4,1,0:T(4,128)(2,1)S(1)}, bf16[3,3,3,16,1]{3,2,4,1,0:T(4,128)(2,1)}, u32[]{:S(2)}) copy-start(bf16[3,3,3,16,1]{3,2,4,1,0:T(4,128)(2,1)} %param.17) | copy-start | bytes 2596
  0.0 19.1 %copy-start.4 = (f32[16]{0:T(128)S(1)}, f32[16]{0:T(128)}, u32[]{:S(2)}) copy-start(f32[16]{0:T(128)} %param.18) | copy-start | bytes 196
  0.0 19.1 %copy-start.5 = (f32[16]{0:T(128)S(1)}, f32[16]{0:T(128)}, u32[]{:S(2)}) copy-start(f32[16]{0:T(128)} %param.20) | copy-start | bytes 196
  0.0 19.1 %copy-start.9 = (f32[32]{0:T(128)S(1)}, f32[32]{0:T(128)}, u32[]{:S(2)}) copy-start(f32[32]{0:T(128)} %param.22) | copy-start | bytes 388
  0.0 19.1 %copy-start.10 = (f32[32]{0:T(128)S(1)}, f32[32]{0:T(128)}, u32[]{:S(2)}) copy-start(f32[32]{0:T(128)} %param.24) | copy-start | bytes 388
  0.1 19.1 %copy-start.6 = (f32[16]{0:T(128)S(1)}, f32[16]{0:T(128)}, u32[]{:S(2)}) copy-start(f32[16]{0:T(128)} %param.26) | copy-start | bytes 196
  0.1 19.1 %copy-start.7 = (f32[16]{0:T(128)S(1)}, f32[16]{0:T(128)}, u32[]{:S(2)}) copy-start(f32[16]{0:T(128)} %param.28) | copy-start | bytes 196
  0.1 19.1 %copy-start.8 = (f32[16]{0:T(128)S(1)}, f32[16]{0:T(128)}, u32[]{:S(2)}) copy-start(f32[16]{0:T(128)} %param.30) | copy-start | bytes 196
  0.1 19.1 %copy-start.11 = (bf16[16]{0:T(256)(128)(2,1)S(1)}, bf16[16]{0:T(256)(128)(2,1)}, u32[]{:S(2)}) copy-start(bf16[16]{0:T(256)(128)(2,1)} %param.31) | copy-start | bytes 100
  0.1 21.5 %collective-permute-start = (bf16[4,16,128]{2,1,0:T(8,128)(2,1)}, bf16[4,16,128]{2,1,0:T(8,128)(2,1)S(1)}, u32[]{:S(2)}, u32[]{:S(2)}) collective-permute-start(bf16[4,16,128]{2,1,0:T(8,128)(2,1)} %param.16), channel_id=1, source_target_pairs={{0,64},{64,0},{128,192},{192,128},{256,320},{320,256},{384,448},{4... | collective-permute-start | bytes 49160 | tf_op jit(solution)/shard_map/ppermute | solution.py:433
  21.6 7.0 %collective-permute-start.1 = (bf16[8,16,128]{2,1,0:T(8,128)(2,1)S(1)}, bf16[8,16,128]{2,1,0:T(8,128)(2,1)S(1)}, u32[]{:S(2)}, u32[]{:S(2)}) collective-permute-start(bf16[8,16,128]{2,1,0:T(8,128)(2,1)S(1)} %pad_maximum_fusion.3.mid_ref), channel_id=1, source_target_pairs={{0,384},{64,448},{128,256},{192,320},{256,128},{320,192},{384,0},{... | collective-permute-start | bytes 98312 | tf_op jit(solution)/shard_map/ppermute | solution.py:436
  26.6 5.8 %collective-permute-start.2 = (bf16[8,16,128]{2,1,0:T(8,128)(2,1)S(1)}, bf16[8,16,128]{2,1,0:T(8,128)(2,1)S(1)}, u32[]{:S(2)}, u32[]{:S(2)}) collective-permute-start(bf16[8,16,128]{2,1,0:T(8,128)(2,1)S(1)} %pad_maximum_fusion.3.mid_ref), channel_id=1, source_target_pairs={{0,128},{64,192},{128,0},{192,64},{256,384},{320,448},{384,256},{4... | collective-permute-start | bytes 98312 | tf_op jit(solution)/shard_map/ppermute | solution.py:437
  32.4 1.8 %collective-permute-start.4 = (bf16[24,8,128]{2,1,0:T(8,128)(2,1)S(1)}, bf16[24,8,128]{2,1,0:T(8,128)(2,1)S(1)}, u32[]{:S(2)}, u32[]{:S(2)}) collective-permute-start(bf16[24,8,128]{2,1,0:T(8,128)(2,1)S(1)} %pad_maximum_fusion.2), channel_id=1, source_target_pairs={{0,56},{8,0},{16,8},{24,16},{32,24},{40,32},{48,40},{56,48},{1,57}... | collective-permute-start | bytes 147464 | tf_op jit(solution)/shard_map/ppermute | solution.py:440
  32.4 3.5 %collective-permute-start.3 = (bf16[24,8,128]{2,1,0:T(8,128)(2,1)S(1)}, bf16[24,8,128]{2,1,0:T(8,128)(2,1)S(1)}, u32[]{:S(2)}, u32[]{:S(2)}) collective-permute-start(bf16[24,8,128]{2,1,0:T(8,128)(2,1)S(1)} %pad_maximum_fusion.1), channel_id=1, source_target_pairs={{0,8},{8,16},{16,24},{24,32},{32,40},{40,48},{48,56},{56,0},{1,9},... | collective-permute-start | bytes 147464 | tf_op jit(solution)/shard_map/ppermute | solution.py:440
  36.3 7.4 %collective-permute-start.5 = (bf16[48,128]{1,0:T(8,128)(2,1)S(1)}, bf16[48,128]{1,0:T(8,128)(2,1)S(1)}, u32[]{:S(2)}, u32[]{:S(2)}) collective-permute-start(bf16[48,128]{1,0:T(8,128)(2,1)S(1)} %get-tuple-element.70), channel_id=1, source_target_pairs={{0,71},{1,2},{2,1},{3,4},{4,3},{5,6},{6,5},{7,64},{64,7},{65,66},{... | collective-permute-start | bytes 36872 | tf_op jit(solution)/shard_map/ppermute | solution.py:443
  41.1 5.6 %collective-permute-start.6 = (bf16[48,128]{1,0:T(8,128)(2,1)S(1)}, bf16[48,128]{1,0:T(8,128)(2,1)S(1)}, u32[]{:S(2)}, u32[]{:S(2)}) collective-permute-start(bf16[48,128]{1,0:T(8,128)(2,1)S(1)} %get-tuple-element.69), channel_id=1, source_target_pairs={{0,1},{1,0},{2,3},{3,2},{4,5},{5,4},{6,7},{7,6},{64,65},{65,64},{6... | collective-permute-start | bytes 36872 | tf_op jit(solution)/shard_map/ppermute | solution.py:444

commit v4 on v3

--- a/solution.py
+++ b/solution.py
@@ -208,14 +208,25 @@
     return moved(values, -start)[:, 0:width]
 
 
-def window(values, start, width):
-    rows = []
+def window_steps(values, start, width, target_ref):
     for b in range(2):
         even = values[32 * b:32 * b + 16]
         odd = values[32 * b + 16:32 * b + 32]
-        rows.append(jnp.concatenate([moved(odd, 1), even, odd, moved(even, -1)], axis=0))
-    return jnp.concatenate([shifted(rows[1], start - ROW, width), shifted(rows[0], start, width),
-                            shifted(rows[1], start, width), shifted(rows[0], start + ROW, width)], axis=0)
+        rows = jnp.concatenate([moved(odd, 1), even, odd, moved(even, -1)], axis=0)
+        at = 64 + 64 * b
+        target_ref[at:at + 64] = shifted(rows, start, width)
+        yield
+        at = 192 - 192 * b
+        target_ref[at:at + 64] = shifted(rows, start + ROW - 2 * ROW * b, width)
+        yield
+
+
+def together(*steps):
+    steps = list(steps)
+    while steps:
+        for work in list(steps):
+            if next(work, work) is work:
+                steps.remove(work)
 
 
 def neighbours(values, start, width):
@@ -251,7 +262,7 @@
 def network_kernel(flags_ref, center_ref, edge_a_ref, edge_b_ref,
                    w1_ref, w2_ref, w4_ref, w5_ref, w7_ref, w8_ref, w6_ref, w9_ref, bias_ref, expand_ref,
                    out_ref,
-                   col0_ref, first_ref, slot_a_ref, slot_b_ref, acc_ref,
+                   col0_ref, first_ref, slot_a_ref, slot_b_ref, acc_ref, last_acc_ref,
                    skip_ref, pool_ref, col4_ref, col5_ref, col7_ref, raised_ref, merged_ref, col8_ref, flat_ref, last_ref):
     odd_z = flags_ref[1]
     edge_a = edge_a_ref[...].astype(F32)
@@ -283,10 +294,11 @@
 
     def gather_first(j, slot_ref):
         for a in range(2):
-            slot_ref[a] = window(first_ref[2 * j + a], 0, FINE)
+            yield from window_steps(first_ref[2 * j + a], 0, FINE, slot_ref.at[a])
 
     def skipped_planes(j, slot_ref):
         for part, sums in paired_dots(w2_ref, slot_ref.at[0], slot_ref.at[1], FINE):
+            yield
             top = None
             for a, done in enumerate(two_planes(*sums, acc_ref, part)):
                 values = leaky(done + wide(bias_second, done))
@@ -294,77 +306,115 @@
                 highest = jnp.max(values.reshape(4, 16, values.shape[1]), axis=0)
                 top = highest if top is None else jnp.maximum(top, highest)
             pool_ref[j, :, part] = top.astype(BF16)
-
-    gather_first(0, slot_a_ref)
+            yield
+
+    def gather_pool(planes):
+        for s in planes:
+            col4_ref[144 * s:144 * s + 144] = neighbours(pool_ref[s + 1], COARSE, COARSE_WIDTH)
+            yield
+
+    together(gather_first(0, slot_a_ref))
 
     def two_steps(t, carry):
-        gather_first(2 * t + 1, slot_b_ref)
-        skipped_planes(2 * t, slot_a_ref)
-        gather_first(2 * t + 2, slot_a_ref)
-        skipped_planes(2 * t + 1, slot_b_ref)
+        together(skipped_planes(2 * t, slot_a_ref), gather_first(2 * t + 1, slot_b_ref))
+        together(skipped_planes(2 * t + 1, slot_b_ref), gather_first(2 * t + 2, slot_a_ref))
         return carry
 
     lax.fori_loop(0, 4, two_steps, 0)
-    skipped_planes(8, slot_a_ref)
-
-    for s in range(8):
-        col4_ref[144 * s:144 * s + 144] = neighbours(pool_ref[s + 1], COARSE, COARSE_WIDTH)
     col4_ref[1152:1200] = jnp.zeros((48, COARSE_WIDTH), BF16)
-    for d in range(4):
-        for a in range(2):
-            col7_ref[2 * d + a] = window(skip_ref[d + 3, 64 * a:64 * a + 64], RAISED, RAISED_WIDTH)
-    for j in range(4):
-        for part, sums in paired_dots(w7_ref.at[1], col7_ref.at[2 * j], col7_ref.at[2 * j + 1], RAISED_WIDTH):
-            for a, done in enumerate(two_planes(*sums, acc_ref, part)):
-                if j > 0:
-                    merged_ref[2 * j + a - 2, :, part] = done
+    col5_ref[1728:1792] = jnp.zeros((64, RAISED_WIDTH), BF16)
+    together(skipped_planes(8, slot_a_ref), gather_pool(range(7)))
+    together(gather_pool([7]))
 
     bias_coarse = bias_ref[5, 0:32]
-    parts = [[], []]
-    for _, sums in paired_dots(w4_ref, col4_ref.at[0:768], col4_ref.at[432:1200], COARSE_WIDTH):
+    coarse_parts = [[], []]
+
+    def coarse_planes():
+        for _, sums in paired_dots(w4_ref, col4_ref.at[0:768], col4_ref.at[432:1200], COARSE_WIDTH):
+            yield
+            for m in range(2):
+                coarse_parts[m].append(leaky(sums[m] + wide(bias_coarse, sums[m])).astype(BF16))
+            yield
+
+    def gather_skipped(planes):
+        for d in planes:
+            for a in range(2):
+                yield from window_steps(skip_ref[d + 3, 64 * a:64 * a + 64], RAISED, RAISED_WIDTH, col7_ref.at[2 * d + a])
+
+    together(coarse_planes(), gather_skipped(range(2)))
+
+    def gather_coarse():
         for m in range(2):
-            parts[m].append(leaky(sums[m] + wide(bias_coarse, sums[m])).astype(BF16))
-    for m in range(2):
-        values = jnp.concatenate(parts[m], axis=1)
-        for p in range(3):
-            at = 288 * (3 * m + p)
-            col5_ref[at:at + 288] = neighbours(values[32 * p:32 * p + 32], RAISED - COARSE, RAISED_WIDTH)
-    col5_ref[1728:1792] = jnp.zeros((64, RAISED_WIDTH), BF16)
+            values = jnp.concatenate(coarse_parts[m], axis=1)
+            for p in range(3):
+                at = 288 * (3 * m + p)
+                col5_ref[at:at + 288] = neighbours(values[32 * p:32 * p + 32], RAISED - COARSE, RAISED_WIDTH)
+                yield
+
+    def merged_skipped(pairs):
+        for j in pairs:
+            for part, sums in paired_dots(w7_ref.at[1], col7_ref.at[2 * j], col7_ref.at[2 * j + 1], RAISED_WIDTH):
+                yield
+                for a, done in enumerate(two_planes(*sums, acc_ref, part)):
+                    if j > 0:
+                        merged_ref[2 * j + a - 2, :, part] = done
+                yield
+
+    together(gather_coarse(), merged_skipped(range(2)))
 
     bias_deeper = bias_ref[6, 0:32]
+    deeper_parts = []
+
+    def deeper_planes():
+        for part in chunks(RAISED_WIDTH):
+            sums = jnp.dot(w5_ref[...], col5_ref[:, part], preferred_element_type=F32)
+            yield
+            deeper_parts.append(leaky(sums + wide(bias_deeper, sums)).astype(BF16))
+            yield
+
+    together(deeper_planes(), gather_skipped(range(2, 4)))
+    deeper = jnp.concatenate(deeper_parts, axis=1)
+
     bias_raised = bias_ref[2]
-    parts = []
-    for part in chunks(RAISED_WIDTH):
-        sums = jnp.dot(w5_ref[...], col5_ref[:, part], preferred_element_type=F32)
-        parts.append(leaky(sums + wide(bias_deeper, sums)).astype(BF16))
-    deeper = jnp.concatenate(parts, axis=1)
-    for d in range(4):
-        parts = []
+    raised_parts = [[], [], [], []]
+
+    def raised_planes(d):
         for part in chunks(RAISED_WIDTH):
             sums = jnp.dot(w6_ref[...], deeper[32 * d:32 * d + 32, part], preferred_element_type=F32)
-            parts.append(leaky(sums + wide(bias_raised, sums)).astype(BF16))
-        values = jnp.concatenate(parts, axis=1)
+            yield
+            raised_parts[d].append(leaky(sums + wide(bias_raised, sums)).astype(BF16))
+            yield
+
+    def gather_raised(d):
+        values = jnp.concatenate(raised_parts[d], axis=1)
         for a in range(2):
-            raised_ref[2 * d + a] = window(values[64 * a:64 * a + 64], 0, RAISED_WIDTH)
+            yield from window_steps(values[64 * a:64 * a + 64], 0, RAISED_WIDTH, raised_ref.at[2 * d + a])
 
     bias_joined = bias_ref[3]
-    for j in range(4):
-        parts = [[], []]
+    merged_parts = {}
+
+    def merged_planes(j):
+        merged_parts[j] = [[], []]
         for part, sums in paired_dots(w7_ref.at[0], raised_ref.at[2 * j], raised_ref.at[2 * j + 1], RAISED_WIDTH):
+            yield
             for a, done in enumerate(two_planes(*sums, acc_ref, part)):
                 if j > 0:
                     done = done + merged_ref[2 * j + a - 2, :, part]
-                    parts[a].append(leaky(done + wide(bias_joined, done)).astype(BF16))
-        if j > 0:
-            for a in range(2):
-                values = jnp.concatenate(parts[a], axis=1)
-                col8_ref[2 * j + a - 2] = window(values, FINAL - RAISED, FINAL_WIDTH)
+                    merged_parts[j][a].append(leaky(done + wide(bias_joined, done)).astype(BF16))
+            yield
+
+    def gather_merged(j):
+        for a in range(2):
+            values = jnp.concatenate(merged_parts[j][a], axis=1)
+            yield from window_steps(values, FINAL - RAISED, FINAL_WIDTH, col8_ref.at[2 * j + a - 2])
 
     bias_final = bias_ref[4]
     output_matrix = w9_ref[...].astype(BF16)
-    for j in range(3):
+
+    def final_planes(j):
         for part, sums in paired_dots(w8_ref, col8_ref.at[2 * j], col8_ref.at[2 * j + 1], FINAL_WIDTH):
-            done = two_planes(*sums, acc_ref, part)
+            yield
+            done = two_planes(*sums, last_acc_ref, part)
             if j > 0:
                 for a in range(2):
                     values = leaky(done[a] + wide(bias_final, done[a])).astype(BF16)
@@ -372,6 +422,16 @@
                     to = 4 * (j - 1) + 2 * a
                     flat_ref[0, to:to + 2, part] = predicted[0:2]
                     flat_ref[1, to:to + 2, part] = predicted[2:4]
+            yield
+
+    together(raised_planes(0), merged_skipped([2]))
+    together(gather_raised(0), raised_planes(1), merged_skipped([3]))
+    together(gather_raised(1), raised_planes(2), merged_planes(0))
+    together(gather_raised(2), raised_planes(3), merged_planes(1))
+    together(gather_raised(3), merged_planes(2), gather_merged(1))
+    together(merged_planes(3), gather_merged(2), final_planes(0))
+    together(gather_merged(3), final_planes(1))
+    together(final_planes(2))
 
     for y in range(8):
         at = ROW * (y + 4) - FINAL + 4
@@ -390,7 +450,7 @@
     vmem = pl.BlockSpec(memory_space=pltpu.VMEM)
     scratch = [
         ((384, FINE), BF16), ((18, 64, FINE), BF16), ((2, 256, FINE), BF16), ((2, 256, FINE), BF16),
-        ((2, 64, FINE), F32), ((9, 128, FINE), BF16), ((9, 16, FINE), BF16),
+        ((2, 64, FINE), F32), ((2, 64, FINAL_WIDTH), F32), ((9, 128, FINE), BF16), ((9, 16, FINE), BF16),
         ((1200, COARSE_WIDTH), BF16), ((1792, RAISED_WIDTH), BF16), ((8, 256, RAISED_WIDTH), BF16),
         ((8, 256, RAISED_WIDTH), BF16), ((6, 64, RAISED_WIDTH), F32), ((6, 256, FINAL_WIDTH), BF16),
         ((2, 8, FINAL_WIDTH), F32), ((64, 128), F32),

time: 60.1 us -> 59.8 us (level)
  no operation moved by 1% of the time
where the time goes in v4:
time: 59.8 us; the launch traced here: 59.5 us
  starting transfers between devices  30 us (50%)
  Pallas kernels  16.2 us (27%)
  waiting for transfers between devices  9.73 us (16%)
  local copies, waits for them, and re-layouts  2.04 us (3%)
  other arithmetic  1.18 us (2%)
    ppermute x1, starting transfers between devices, exchange(): other = lax.ppermute(density, 'gx', [(i, i ^ 1) for i in range(8)])  15.9 us
    pallas_call x1, Pallas kernels, network(): pl.pallas_call(network_kernel, out_shape=jax.ShapeDtypeStruct((4, 16, 128...  12.9 us
    ppermute x1, starting transfers between devices, exchange(): a = lax.ppermute(mid, 'gx', swaps_y(True))  4.92 us
    ppermute x1, starting transfers between devices, exchange(): lax.ppermute(jnp.where(odd, right, left), ('gx', 'gz'), swaps_z(True))  4.77 us
    ppermute x1, waiting for transfers between devices, exchange(): b = lax.ppermute(mid, 'gx', swaps_y(False))  3.73 us
    ppermute x1, waiting for transfers between devices, exchange(): lax.ppermute(jnp.where(odd, left, right), ('gx', 'gz'), swaps_z(False))  2.96 us
    pallas_call x1, Pallas kernels, prepare_weights(): pl.pallas_call(weights_kernel, out_shape=[jax.ShapeDtypeStruct(s, BF16) f...  2.32 us
    ppermute x1, starting transfers between devices, exchange(): b = lax.ppermute(mid, 'gx', swaps_y(False))  2.05 us
  transfers between devices with their start and end apart: 7, of which 4 were waited for; matrix products, arithmetic and copies ran while one was open for 5% of the time, Pallas kernels for 5%

profile of v4, /device:TPU:6, one launch (start us, length us, event | category | flops | bytes accessed | tf_op | source)
XLA Modules:
  0.0 59.5 jit_solution(398242721875969131)
XLA Ops:
  0.0 0.0 copy-start.3
  0.0 0.0 copy-start.4
  0.0 0.0 copy-start.5
  0.0 0.0 copy-start.9
  0.0 0.0 copy-start.10
  0.1 0.0 copy-start.6
  0.1 0.0 copy-start.7
  0.1 0.0 copy-start.8
  0.1 0.0 copy-start.11
  0.1 15.9 %collective-permute-start = (bf16[4,16,128]{2,1,0:T(8,128)(2,1)}, bf16[4,16,128]{2,1,0:T(8,128)(2,1)S(1)}, u32[]{:S(2)}, u32[]{:S(2)}) collective-permute-start(bf16[4,16,128]{2,1,0:T(8,128)(2,1)} %param.16), channel_id=1, source_target_pairs={{0,64},{64,0},{128,192},{192,128},{256,320},{320,256},{384,448},{4... | collective-permute-start | bytes 49160 | tf_op jit(solution)/shard_map/ppermute | solution.py:493
  16.0 1.1 %pad_maximum_fusion = bf16[3,3,3,16,32]{4,3,2,1,0:T(8,128)(2,1)S(1)} fusion(bf16[3,3,3,16,16]{4,3,2,1,0:T(8,128)(2,1)} %param.29, bf16[3,3,3,16,16]{4,3,2,1,0:T(8,128)(2,1)} %param.19), kind=kLoop, calls=%fused_computation | loop fusion | flops 55296 | bytes 55296 | tf_op jit(solution)/shard_map/concatenate | solution.py:515
  17.1 0.9 %constant_dynamic-update-slice_fusion.3 = bf16[2288,32]{1,0:T(8,128)(2,1)S(1)} fusion(bf16[2288,32]{1,0:T(8,128)(2,1)S(1)} %constant_dynamic-update-slice_fusion.4, bf16[432,32]{1,0:T(8,128)(2,1)} %bitcast.16), kind=kLoop, calls=%fused_computation.17 | loop fusion | bytes 138240
  18.0 0.9 %constant_dynamic-update-slice_fusion.2 = bf16[2288,32]{1,0:T(8,128)(2,1)S(1)} fusion(bf16[2288,32]{1,0:T(8,128)(2,1)S(1)} %constant_dynamic-update-slice_fusion.3, bf16[432,32]{1,0:T(8,128)(2,1)} %bitcast.17), kind=kLoop, calls=%fused_computation.16 | loop fusion | bytes 138240
  19.0 0.1 pad_add_fusion.place_ref
  19.2 0.1 concatenate.20
  19.3 2.3 %weights.1 = (bf16[512,256]{1,0:T(8,128)(2,1)S(1)}, bf16[192,256]{1,0:T(8,128)(2,1)S(1)}, bf16[96,768]{1,0:T(8,128)(2,1)S(1)}, bf16[128,1792]{1,0:T(8,128)(2,1)S...) custom-call(s32[3]{0:T(128)S(1)} %pad_add_fusion.place_ref, ...), custom_call_target="tpu_custom_call" | custom-call | flops 10000000 | bytes 2000000 | tf_op jit(solution)/shard_map/weights/pallas_call | solution.py:117
  21.6 0.0 collective-permute-done
  21.6 4.9 %collective-permute-start.1 = (bf16[8,16,128]{2,1,0:T(8,128)(2,1)S(1)}, bf16[8,16,128]{2,1,0:T(8,128)(2,1)S(1)}, u32[]{:S(2)}, u32[]{:S(2)}) collective-permute-start(bf16[8,16,128]{2,1,0:T(8,128)(2,1)S(1)} %pad_maximum_fusion.3.mid_ref), channel_id=1, source_target_pairs={{0,384},{64,448},{128,256},{192,320},{256,128},{320,192},{384,0},{... | collective-permute-start | bytes 98312 | tf_op jit(solution)/shard_map/ppermute | solution.py:496
  26.6 2.0 %collective-permute-start.2 = (bf16[8,16,128]{2,1,0:T(8,128)(2,1)S(1)}, bf16[8,16,128]{2,1,0:T(8,128)(2,1)S(1)}, u32[]{:S(2)}, u32[]{:S(2)}) collective-permute-start(bf16[8,16,128]{2,1,0:T(8,128)(2,1)S(1)} %pad_maximum_fusion.3.mid_ref), channel_id=1, source_target_pairs={{0,128},{64,192},{128,0},{192,64},{256,384},{320,448},{384,256},{4... | collective-permute-start | bytes 98312 | tf_op jit(solution)/shard_map/ppermute | solution.py:497
  28.6 0.0 collective-permute-done.1.a_ref
  28.7 3.7 %collective-permute-done.2.b_ref = bf16[8,16,128]{2,1,0:T(8,128)(2,1)S(1)} collective-permute-done((bf16[8,16,128]{2,1,0:T(8,128)(2,1)S(1)}, bf16[8,16,128]{2,1,0:T(8,128)(2,1)S(1)}, u32[]{:S(2)}, u32[]{:S(2)}) %collective-permute-start.2) | collective-permute-done | bytes 32800 | tf_op jit(solution)/shard_map/ppermute | solution.py:497
  32.4 0.0 collective-permute-start.4
  32.4 0.5 collective-permute-start.3
  32.9 1.2 %collective-permute-done.4.high_ref = bf16[24,8,128]{2,1,0:T(8,128)(2,1)S(1)} collective-permute-done((bf16[24,8,128]{2,1,0:T(8,128)(2,1)S(1)}, bf16[24,8,128]{2,1,0:T(8,128)(2,1)S(1)}, u32[]{:S(2)}, u32[]{:S(2)}) %collective-permute-start.4) | collective-permute-done | bytes 49184 | tf_op jit(solution)/shard_map/ppermute | solution.py:500
  34.2 1.8 %collective-permute-done.3.low_ref = bf16[24,8,128]{2,1,0:T(8,128)(2,1)S(1)} collective-permute-done((bf16[24,8,128]{2,1,0:T(8,128)(2,1)S(1)}, bf16[24,8,128]{2,1,0:T(8,128)(2,1)S(1)}, u32[]{:S(2)}, u32[]{:S(2)}) %collective-permute-start.3) | collective-permute-done | bytes 49184 | tf_op jit(solution)/shard_map/ppermute | solution.py:500
  36.0 0.3 edges.1
  36.3 4.8 %collective-permute-start.5 = (bf16[48,128]{1,0:T(8,128)(2,1)S(1)}, bf16[48,128]{1,0:T(8,128)(2,1)S(1)}, u32[]{:S(2)}, u32[]{:S(2)}) collective-permute-start(bf16[48,128]{1,0:T(8,128)(2,1)S(1)} %get-tuple-element.70), channel_id=1, source_target_pairs={{0,71},{1,2},{2,1},{3,4},{4,3},{5,6},{6,5},{7,64},{64,7},{65,66},{... | collective-permute-start | bytes 36872 | tf_op jit(solution)/shard_map/ppermute | solution.py:503
  41.1 1.9 %collective-permute-start.6 = (bf16[48,128]{1,0:T(8,128)(2,1)S(1)}, bf16[48,128]{1,0:T(8,128)(2,1)S(1)}, u32[]{:S(2)}, u32[]{:S(2)}) collective-permute-start(bf16[48,128]{1,0:T(8,128)(2,1)S(1)} %get-tuple-element.69), channel_id=1, source_target_pairs={{0,1},{1,0},{2,3},{3,2},{4,5},{5,4},{6,7},{7,6},{64,65},{65,64},{6... | collective-permute-start | bytes 36872 | tf_op jit(solution)/shard_map/ppermute | solution.py:504
  43.0 0.7 %sample.1.center_ref = f32[4,24,1152]{2,1,0:T(8,128)S(1)} custom-call(f32[768,128]{1,0:T(8,128)S(1)} %get-tuple-element.47.cells_ref, bf16[128,256]{1,0:T(8,128)(2,1)S(1)} %get-tuple-element.48.sz_ref), custom_call_target="tpu_custom_call" | custom-call | flops 100000000 | bytes 1000000 | tf_op jit(solution)/shard_map/sample/pallas_call | solution.py:184
  43.7 0.0 collective-permute-done.5.edge_a_ref
  43.7 3.0 %collective-permute-done.6.edge_b_ref = bf16[48,128]{1,0:T(8,128)(2,1)S(1)} collective-permute-done((bf16[48,128]{1,0:T(8,128)(2,1)S(1)}, bf16[48,128]{1,0:T(8,128)(2,1)S(1)}, u32[]{:S(2)}, u32[]{:S(2)}) %collective-permute-start.6) | collective-permute-done | bytes 12320 | tf_op jit(solution)/shard_map/ppermute | solution.py:504
  46.7 12.9 %network.1 = f32[4,16,128]{2,1,0:T(8,128)} custom-call(f32[2,8,128]{2,1,0:T(8,128)S(1)} %get-tuple-element.45.flags_ref, f32[4,24,1152]{2,1,0:T(8,128)S(1)} %sample.1.center_ref, bf16[48,128]{1,0:T(8,128)(2,1)S(1)} %collective-permute-done.5.edge_a_ref, bf16[48,128]{1,0:T(8,128)(2,1)S(1)} %collective-permute-done.6.edge_b_ref, ...), custom_call_target="tpu_custom_call" | custom-call | flops 4000000000 | bytes 4000000 | tf_op jit(solution)/shard_map/network/pallas_call | solution.py:459
  (27 shorter events, 0.2 us)
Async XLA Ops:
  0.0 21.6 %copy-start.2 = (bf16[4,16,128]{2,1,0:T(8,128)(2,1)S(1)}, bf16[4,16,128]{2,1,0:T(8,128)(2,1)}, u32[]{:S(2)}) copy-start(bf16[4,16,128]{2,1,0:T(8,128)(2,1)} %param.16) | copy-start | bytes 49156
  0.0 18.9 %copy-start = (bf16[3,3,3,32,32]{4,3,2,1,0:T(8,128)(2,1)S(1)}, bf16[3,3,3,32,32]{4,3,2,1,0:T(8,128)(2,1)}, u32[]{:S(2)}) copy-start(bf16[3,3,3,32,32]{4,3,2,1,0:T(8,128)(2,1)} %param.23) | copy-start | bytes 165892
  0.0 19.0 %copy-start.1 = (bf16[2,2,2,16,32]{4,3,2,1,0:T(8,128)(2,1)S(1)}, bf16[2,2,2,16,32]{4,3,2,1,0:T(8,128)(2,1)}, u32[]{:S(2)}) copy-start(bf16[2,2,2,16,32]{4,3,2,1,0:T(8,128)(2,1)} %param.25) | copy-start | bytes 24580
  0.0 19.1 %copy-start.3 = (bf16[3,3,3,16,1]{3,2,4,1,0:T(4,128)(2,1)S(1)}, bf16[3,3,3,16,1]{3,2,4,1,0:T(4,128)(2,1)}, u32[]{:S(2)}) copy-start(bf16[3,3,3,16,1]{3,2,4,1,0:T(4,128)(2,1)} %param.17) | copy-start | bytes 2596
  0.0 19.1 %copy-start.4 = (f32[16]{0:T(128)S(1)}, f32[16]{0:T(128)}, u32[]{:S(2)}) copy-start(f32[16]{0:T(128)} %param.18) | copy-start | bytes 196
  0.0 19.1 %copy-start.5 = (f32[16]{0:T(128)S(1)}, f32[16]{0:T(128)}, u32[]{:S(2)}) copy-start(f32[16]{0:T(128)} %param.20) | copy-start | bytes 196
  0.0 19.1 %copy-start.9 = (f32[32]{0:T(128)S(1)}, f32[32]{0:T(128)}, u32[]{:S(2)}) copy-start(f32[32]{0:T(128)} %param.22) | copy-start | bytes 388
  0.0 19.1 %copy-start.10 = (f32[32]{0:T(128)S(1)}, f32[32]{0:T(128)}, u32[]{:S(2)}) copy-start(f32[32]{0:T(128)} %param.24) | copy-start | bytes 388
  0.1 19.1 %copy-start.6 = (f32[16]{0:T(128)S(1)}, f32[16]{0:T(128)}, u32[]{:S(2)}) copy-start(f32[16]{0:T(128)} %param.26) | copy-start | bytes 196
  0.1 19.1 %copy-start.7 = (f32[16]{0:T(128)S(1)}, f32[16]{0:T(128)}, u32[]{:S(2)}) copy-start(f32[16]{0:T(128)} %param.28) | copy-start | bytes 196
  0.1 19.1 %copy-start.8 = (f32[16]{0:T(128)S(1)}, f32[16]{0:T(128)}, u32[]{:S(2)}) copy-start(f32[16]{0:T(128)} %param.30) | copy-start | bytes 196
  0.1 19.1 %copy-start.11 = (bf16[16]{0:T(256)(128)(2,1)S(1)}, bf16[16]{0:T(256)(128)(2,1)}, u32[]{:S(2)}) copy-start(bf16[16]{0:T(256)(128)(2,1)} %param.31) | copy-start | bytes 100
  0.1 21.5 %collective-permute-start = (bf16[4,16,128]{2,1,0:T(8,128)(2,1)}, bf16[4,16,128]{2,1,0:T(8,128)(2,1)S(1)}, u32[]{:S(2)}, u32[]{:S(2)}) collective-permute-start(bf16[4,16,128]{2,1,0:T(8,128)(2,1)} %param.16), channel_id=1, source_target_pairs={{0,64},{64,0},{128,192},{192,128},{256,320},{320,256},{384,448},{4... | collective-permute-start | bytes 49160 | tf_op jit(solution)/shard_map/ppermute | solution.py:493
  21.6 7.0 %collective-permute-start.1 = (bf16[8,16,128]{2,1,0:T(8,128)(2,1)S(1)}, bf16[8,16,128]{2,1,0:T(8,128)(2,1)S(1)}, u32[]{:S(2)}, u32[]{:S(2)}) collective-permute-start(bf16[8,16,128]{2,1,0:T(8,128)(2,1)S(1)} %pad_maximum_fusion.3.mid_ref), channel_id=1, source_target_pairs={{0,384},{64,448},{128,256},{192,320},{256,128},{320,192},{384,0},{... | collective-permute-start | bytes 98312 | tf_op jit(solution)/shard_map/ppermute | solution.py:496
  26.6 5.8 %collective-permute-start.2 = (bf16[8,16,128]{2,1,0:T(8,128)(2,1)S(1)}, bf16[8,16,128]{2,1,0:T(8,128)(2,1)S(1)}, u32[]{:S(2)}, u32[]{:S(2)}) collective-permute-start(bf16[8,16,128]{2,1,0:T(8,128)(2,1)S(1)} %pad_maximum_fusion.3.mid_ref), channel_id=1, source_target_pairs={{0,128},{64,192},{128,0},{192,64},{256,384},{320,448},{384,256},{4... | collective-permute-start | bytes 98312 | tf_op jit(solution)/shard_map/ppermute | solution.py:497
  32.4 1.8 %collective-permute-start.4 = (bf16[24,8,128]{2,1,0:T(8,128)(2,1)S(1)}, bf16[24,8,128]{2,1,0:T(8,128)(2,1)S(1)}, u32[]{:S(2)}, u32[]{:S(2)}) collective-permute-start(bf16[24,8,128]{2,1,0:T(8,128)(2,1)S(1)} %pad_maximum_fusion.2), channel_id=1, source_target_pairs={{0,56},{8,0},{16,8},{24,16},{32,24},{40,32},{48,40},{56,48},{1,57}... | collective-permute-start | bytes 147464 | tf_op jit(solution)/shard_map/ppermute | solution.py:500
  32.4 3.5 %collective-permute-start.3 = (bf16[24,8,128]{2,1,0:T(8,128)(2,1)S(1)}, bf16[24,8,128]{2,1,0:T(8,128)(2,1)S(1)}, u32[]{:S(2)}, u32[]{:S(2)}) collective-permute-start(bf16[24,8,128]{2,1,0:T(8,128)(2,1)S(1)} %pad_maximum_fusion.1), channel_id=1, source_target_pairs={{0,8},{8,16},{16,24},{24,32},{32,40},{40,48},{48,56},{56,0},{1,9},... | collective-permute-start | bytes 147464 | tf_op jit(solution)/shard_map/ppermute | solution.py:500
  36.3 7.4 %collective-permute-start.5 = (bf16[48,128]{1,0:T(8,128)(2,1)S(1)}, bf16[48,128]{1,0:T(8,128)(2,1)S(1)}, u32[]{:S(2)}, u32[]{:S(2)}) collective-permute-start(bf16[48,128]{1,0:T(8,128)(2,1)S(1)} %get-tuple-element.70), channel_id=1, source_target_pairs={{0,71},{1,2},{2,1},{3,4},{4,3},{5,6},{6,5},{7,64},{64,7},{65,66},{... | collective-permute-start | bytes 36872 | tf_op jit(solution)/shard_map/ppermute | solution.py:503
  41.1 5.6 %collective-permute-start.6 = (bf16[48,128]{1,0:T(8,128)(2,1)S(1)}, bf16[48,128]{1,0:T(8,128)(2,1)S(1)}, u32[]{:S(2)}, u32[]{:S(2)}) collective-permute-start(bf16[48,128]{1,0:T(8,128)(2,1)S(1)} %get-tuple-element.69), channel_id=1, source_target_pairs={{0,1},{1,0},{2,3},{3,2},{4,5},{5,4},{6,7},{7,6},{64,65},{65,64},{6... | collective-permute-start | bytes 36872 | tf_op jit(solution)/shard_map/ppermute | solution.py:504

commit v5 on v4

--- a/solution.py
+++ b/solution.py
@@ -320,7 +320,7 @@
         together(skipped_planes(2 * t + 1, slot_b_ref), gather_first(2 * t + 2, slot_a_ref))
         return carry
 
-    lax.fori_loop(0, 4, two_steps, 0)
+    lax.fori_loop(0, 4, two_steps, 0, unroll=2)
     col4_ref[1152:1200] = jnp.zeros((48, COARSE_WIDTH), BF16)
     col5_ref[1728:1792] = jnp.zeros((64, RAISED_WIDTH), BF16)
     together(skipped_planes(8, slot_a_ref), gather_pool(range(7)))

time: 59.8 us -> 59.6 us (level)
  no operation moved by 1% of the time
where the time goes in v5:
time: 59.6 us; the launch traced here: 59.3 us
  starting transfers between devices  30 us (50%)
  Pallas kernels  16 us (27%)
  waiting for transfers between devices  9.73 us (16%)
  local copies, waits for them, and re-layouts  2.04 us (3%)
  other arithmetic  1.18 us (2%)
    ppermute x1, starting transfers between devices, exchange(): other = lax.ppermute(density, 'gx', [(i, i ^ 1) for i in range(8)])  15.9 us
    pallas_call x1, Pallas kernels, network(): pl.pallas_call(network_kernel, out_shape=jax.ShapeDtypeStruct((4, 16, 128...  12.6 us
    ppermute x1, starting transfers between devices, exchange(): a = lax.ppermute(mid, 'gx', swaps_y(True))  4.92 us
    ppermute x1, starting transfers between devices, exchange(): lax.ppermute(jnp.where(odd, right, left), ('gx', 'gz'), swaps_z(True))  4.77 us
    ppermute x1, waiting for transfers between devices, exchange(): b = lax.ppermute(mid, 'gx', swaps_y(False))  3.73 us
    ppermute x1, waiting for transfers between devices, exchange(): lax.ppermute(jnp.where(odd, left, right), ('gx', 'gz'), swaps_z(False))  2.96 us
    pallas_call x1, Pallas kernels, prepare_weights(): pl.pallas_call(weights_kernel, out_shape=[jax.ShapeDtypeStruct(s, BF16) f...  2.32 us
    ppermute x1, starting transfers between devices, exchange(): b = lax.ppermute(mid, 'gx', swaps_y(False))  2.05 us
  transfers between devices with their start and end apart: 7, of which 4 were waited for; matrix products, arithmetic and copies ran while one was open for 5% of the time, Pallas kernels for 5%

profile of v5, /device:TPU:6, one launch (start us, length us, event | category | flops | bytes accessed | tf_op | source)
XLA Modules:
  0.0 59.3 jit_solution(5932730394328116126)
XLA Ops:
  0.0 0.0 copy-start.3
  0.0 0.0 copy-start.4
  0.0 0.0 copy-start.5
  0.0 0.0 copy-start.9
  0.0 0.0 copy-start.10
  0.1 0.0 copy-start.6
  0.1 0.0 copy-start.7
  0.1 0.0 copy-start.8
  0.1 15.9 %collective-permute-start = (bf16[4,16,128]{2,1,0:T(8,128)(2,1)}, bf16[4,16,128]{2,1,0:T(8,128)(2,1)S(1)}, u32[]{:S(2)}, u32[]{:S(2)}) collective-permute-start(bf16[4,16,128]{2,1,0:T(8,128)(2,1)} %param.16), channel_id=1, source_target_pairs={{0,64},{64,0},{128,192},{192,128},{256,320},{320,256},{384,448},{4... | collective-permute-start | bytes 49160 | tf_op jit(solution)/shard_map/ppermute | solution.py:493
  16.0 1.1 %pad_maximum_fusion = bf16[3,3,3,16,32]{4,3,2,1,0:T(8,128)(2,1)S(1)} fusion(bf16[3,3,3,16,16]{4,3,2,1,0:T(8,128)(2,1)} %param.29, bf16[3,3,3,16,16]{4,3,2,1,0:T(8,128)(2,1)} %param.19), kind=kLoop, calls=%fused_computation | loop fusion | flops 55296 | bytes 55296 | tf_op jit(solution)/shard_map/concatenate | solution.py:515
  17.1 0.9 %constant_dynamic-update-slice_fusion.3 = bf16[2288,32]{1,0:T(8,128)(2,1)S(1)} fusion(bf16[2288,32]{1,0:T(8,128)(2,1)S(1)} %constant_dynamic-update-slice_fusion.4, bf16[432,32]{1,0:T(8,128)(2,1)} %bitcast.16), kind=kLoop, calls=%fused_computation.17 | loop fusion | bytes 138240
  18.0 0.9 %constant_dynamic-update-slice_fusion.2 = bf16[2288,32]{1,0:T(8,128)(2,1)S(1)} fusion(bf16[2288,32]{1,0:T(8,128)(2,1)S(1)} %constant_dynamic-update-slice_fusion.3, bf16[432,32]{1,0:T(8,128)(2,1)} %bitcast.17), kind=kLoop, calls=%fused_computation.16 | loop fusion | bytes 138240
  18.9 0.0 copy-done
  19.0 0.1 pad_add_fusion.place_ref
  19.2 0.1 concatenate.20
  19.3 2.3 %weights.1 = (bf16[512,256]{1,0:T(8,128)(2,1)S(1)}, bf16[192,256]{1,0:T(8,128)(2,1)S(1)}, bf16[96,768]{1,0:T(8,128)(2,1)S(1)}, bf16[128,1792]{1,0:T(8,128)(2,1)S...) custom-call(s32[3]{0:T(128)S(1)} %pad_add_fusion.place_ref, ...), custom_call_target="tpu_custom_call" | custom-call | flops 10000000 | bytes 2000000 | tf_op jit(solution)/shard_map/weights/pallas_call | solution.py:117
  21.6 0.0 collective-permute-done
  21.6 4.9 %collective-permute-start.1 = (bf16[8,16,128]{2,1,0:T(8,128)(2,1)S(1)}, bf16[8,16,128]{2,1,0:T(8,128)(2,1)S(1)}, u32[]{:S(2)}, u32[]{:S(2)}) collective-permute-start(bf16[8,16,128]{2,1,0:T(8,128)(2,1)S(1)} %pad_maximum_fusion.3.mid_ref), channel_id=1, source_target_pairs={{0,384},{64,448},{128,256},{192,320},{256,128},{320,192},{384,0},{... | collective-permute-start | bytes 98312 | tf_op jit(solution)/shard_map/ppermute | solution.py:496
  26.6 2.0 %collective-permute-start.2 = (bf16[8,16,128]{2,1,0:T(8,128)(2,1)S(1)}, bf16[8,16,128]{2,1,0:T(8,128)(2,1)S(1)}, u32[]{:S(2)}, u32[]{:S(2)}) collective-permute-start(bf16[8,16,128]{2,1,0:T(8,128)(2,1)S(1)} %pad_maximum_fusion.3.mid_ref), channel_id=1, source_target_pairs={{0,128},{64,192},{128,0},{192,64},{256,384},{320,448},{384,256},{4... | collective-permute-start | bytes 98312 | tf_op jit(solution)/shard_map/ppermute | solution.py:497
  28.6 0.0 collective-permute-done.1.a_ref
  28.7 3.7 %collective-permute-done.2.b_ref = bf16[8,16,128]{2,1,0:T(8,128)(2,1)S(1)} collective-permute-done((bf16[8,16,128]{2,1,0:T(8,128)(2,1)S(1)}, bf16[8,16,128]{2,1,0:T(8,128)(2,1)S(1)}, u32[]{:S(2)}, u32[]{:S(2)}) %collective-permute-start.2) | collective-permute-done | bytes 32800 | tf_op jit(solution)/shard_map/ppermute | solution.py:497
  32.4 0.0 collective-permute-start.4
  32.4 0.5 collective-permute-start.3
  32.9 1.2 %collective-permute-done.4.high_ref = bf16[24,8,128]{2,1,0:T(8,128)(2,1)S(1)} collective-permute-done((bf16[24,8,128]{2,1,0:T(8,128)(2,1)S(1)}, bf16[24,8,128]{2,1,0:T(8,128)(2,1)S(1)}, u32[]{:S(2)}, u32[]{:S(2)}) %collective-permute-start.4) | collective-permute-done | bytes 49184 | tf_op jit(solution)/shard_map/ppermute | solution.py:500
  34.2 1.8 %collective-permute-done.3.low_ref = bf16[24,8,128]{2,1,0:T(8,128)(2,1)S(1)} collective-permute-done((bf16[24,8,128]{2,1,0:T(8,128)(2,1)S(1)}, bf16[24,8,128]{2,1,0:T(8,128)(2,1)S(1)}, u32[]{:S(2)}, u32[]{:S(2)}) %collective-permute-start.3) | collective-permute-done | bytes 49184 | tf_op jit(solution)/shard_map/ppermute | solution.py:500
  36.0 0.3 edges.1
  36.3 4.8 %collective-permute-start.5 = (bf16[48,128]{1,0:T(8,128)(2,1)S(1)}, bf16[48,128]{1,0:T(8,128)(2,1)S(1)}, u32[]{:S(2)}, u32[]{:S(2)}) collective-permute-start(bf16[48,128]{1,0:T(8,128)(2,1)S(1)} %get-tuple-element.70), channel_id=1, source_target_pairs={{0,71},{1,2},{2,1},{3,4},{4,3},{5,6},{6,5},{7,64},{64,7},{65,66},{... | collective-permute-start | bytes 36872 | tf_op jit(solution)/shard_map/ppermute | solution.py:503
  41.1 1.9 %collective-permute-start.6 = (bf16[48,128]{1,0:T(8,128)(2,1)S(1)}, bf16[48,128]{1,0:T(8,128)(2,1)S(1)}, u32[]{:S(2)}, u32[]{:S(2)}) collective-permute-start(bf16[48,128]{1,0:T(8,128)(2,1)S(1)} %get-tuple-element.69), channel_id=1, source_target_pairs={{0,1},{1,0},{2,3},{3,2},{4,5},{5,4},{6,7},{7,6},{64,65},{65,64},{6... | collective-permute-start | bytes 36872 | tf_op jit(solution)/shard_map/ppermute | solution.py:504
  43.0 0.7 %sample.1.center_ref = f32[4,24,1152]{2,1,0:T(8,128)S(1)} custom-call(f32[768,128]{1,0:T(8,128)S(1)} %get-tuple-element.47.cells_ref, bf16[128,256]{1,0:T(8,128)(2,1)S(1)} %get-tuple-element.48.sz_ref), custom_call_target="tpu_custom_call" | custom-call | flops 100000000 | bytes 1000000 | tf_op jit(solution)/shard_map/sample/pallas_call | solution.py:184
  43.7 0.0 collective-permute-done.5.edge_a_ref
  43.7 3.0 %collective-permute-done.6.edge_b_ref = bf16[48,128]{1,0:T(8,128)(2,1)S(1)} collective-permute-done((bf16[48,128]{1,0:T(8,128)(2,1)S(1)}, bf16[48,128]{1,0:T(8,128)(2,1)S(1)}, u32[]{:S(2)}, u32[]{:S(2)}) %collective-permute-start.6) | collective-permute-done | bytes 12320 | tf_op jit(solution)/shard_map/ppermute | solution.py:504
  46.7 12.6 %network.1 = f32[4,16,128]{2,1,0:T(8,128)} custom-call(f32[2,8,128]{2,1,0:T(8,128)S(1)} %get-tuple-element.45.flags_ref, f32[4,24,1152]{2,1,0:T(8,128)S(1)} %sample.1.center_ref, bf16[48,128]{1,0:T(8,128)(2,1)S(1)} %collective-permute-done.5.edge_a_ref, bf16[48,128]{1,0:T(8,128)(2,1)S(1)} %collective-permute-done.6.edge_b_ref, ...), custom_call_target="tpu_custom_call" | custom-call | flops 4000000000 | bytes 4000000 | tf_op jit(solution)/shard_map/network/pallas_call | solution.py:459
  (27 shorter events, 0.2 us)
Async XLA Ops:
  0.0 21.6 %copy-start.2 = (bf16[4,16,128]{2,1,0:T(8,128)(2,1)S(1)}, bf16[4,16,128]{2,1,0:T(8,128)(2,1)}, u32[]{:S(2)}) copy-start(bf16[4,16,128]{2,1,0:T(8,128)(2,1)} %param.16) | copy-start | bytes 49156
  0.0 18.9 %copy-start = (bf16[3,3,3,32,32]{4,3,2,1,0:T(8,128)(2,1)S(1)}, bf16[3,3,3,32,32]{4,3,2,1,0:T(8,128)(2,1)}, u32[]{:S(2)}) copy-start(bf16[3,3,3,32,32]{4,3,2,1,0:T(8,128)(2,1)} %param.23) | copy-start | bytes 165892
  0.0 19.0 %copy-start.1 = (bf16[2,2,2,16,32]{4,3,2,1,0:T(8,128)(2,1)S(1)}, bf16[2,2,2,16,32]{4,3,2,1,0:T(8,128)(2,1)}, u32[]{:S(2)}) copy-start(bf16[2,2,2,16,32]{4,3,2,1,0:T(8,128)(2,1)} %param.25) | copy-start | bytes 24580
  0.0 19.1 %copy-start.3 = (bf16[3,3,3,16,1]{3,2,4,1,0:T(4,128)(2,1)S(1)}, bf16[3,3,3,16,1]{3,2,4,1,0:T(4,128)(2,1)}, u32[]{:S(2)}) copy-start(bf16[3,3,3,16,1]{3,2,4,1,0:T(4,128)(2,1)} %param.17) | copy-start | bytes 2596
  0.0 19.1 %copy-start.4 = (f32[16]{0:T(128)S(1)}, f32[16]{0:T(128)}, u32[]{:S(2)}) copy-start(f32[16]{0:T(128)} %param.18) | copy-start | bytes 196
  0.0 19.1 %copy-start.5 = (f32[16]{0:T(128)S(1)}, f32[16]{0:T(128)}, u32[]{:S(2)}) copy-start(f32[16]{0:T(128)} %param.20) | copy-start | bytes 196
  0.0 19.1 %copy-start.9 = (f32[32]{0:T(128)S(1)}, f32[32]{0:T(128)}, u32[]{:S(2)}) copy-start(f32[32]{0:T(128)} %param.22) | copy-start | bytes 388
  0.0 19.1 %copy-start.10 = (f32[32]{0:T(128)S(1)}, f32[32]{0:T(128)}, u32[]{:S(2)}) copy-start(f32[32]{0:T(128)} %param.24) | copy-start | bytes 388
  0.1 19.1 %copy-start.6 = (f32[16]{0:T(128)S(1)}, f32[16]{0:T(128)}, u32[]{:S(2)}) copy-start(f32[16]{0:T(128)} %param.26) | copy-start | bytes 196
  0.1 19.1 %copy-start.7 = (f32[16]{0:T(128)S(1)}, f32[16]{0:T(128)}, u32[]{:S(2)}) copy-start(f32[16]{0:T(128)} %param.28) | copy-start | bytes 196
  0.1 19.1 %copy-start.8 = (f32[16]{0:T(128)S(1)}, f32[16]{0:T(128)}, u32[]{:S(2)}) copy-start(f32[16]{0:T(128)} %param.30) | copy-start | bytes 196
  0.1 19.1 %copy-start.11 = (bf16[16]{0:T(256)(128)(2,1)S(1)}, bf16[16]{0:T(256)(128)(2,1)}, u32[]{:S(2)}) copy-start(bf16[16]{0:T(256)(128)(2,1)} %param.31) | copy-start | bytes 100
  0.1 21.5 %collective-permute-start = (bf16[4,16,128]{2,1,0:T(8,128)(2,1)}, bf16[4,16,128]{2,1,0:T(8,128)(2,1)S(1)}, u32[]{:S(2)}, u32[]{:S(2)}) collective-permute-start(bf16[4,16,128]{2,1,0:T(8,128)(2,1)} %param.16), channel_id=1, source_target_pairs={{0,64},{64,0},{128,192},{192,128},{256,320},{320,256},{384,448},{4... | collective-permute-start | bytes 49160 | tf_op jit(solution)/shard_map/ppermute | solution.py:493
  21.6 7.0 %collective-permute-start.1 = (bf16[8,16,128]{2,1,0:T(8,128)(2,1)S(1)}, bf16[8,16,128]{2,1,0:T(8,128)(2,1)S(1)}, u32[]{:S(2)}, u32[]{:S(2)}) collective-permute-start(bf16[8,16,128]{2,1,0:T(8,128)(2,1)S(1)} %pad_maximum_fusion.3.mid_ref), channel_id=1, source_target_pairs={{0,384},{64,448},{128,256},{192,320},{256,128},{320,192},{384,0},{... | collective-permute-start | bytes 98312 | tf_op jit(solution)/shard_map/ppermute | solution.py:496
  26.6 5.8 %collective-permute-start.2 = (bf16[8,16,128]{2,1,0:T(8,128)(2,1)S(1)}, bf16[8,16,128]{2,1,0:T(8,128)(2,1)S(1)}, u32[]{:S(2)}, u32[]{:S(2)}) collective-permute-start(bf16[8,16,128]{2,1,0:T(8,128)(2,1)S(1)} %pad_maximum_fusion.3.mid_ref), channel_id=1, source_target_pairs={{0,128},{64,192},{128,0},{192,64},{256,384},{320,448},{384,256},{4... | collective-permute-start | bytes 98312 | tf_op jit(solution)/shard_map/ppermute | solution.py:497
  32.4 1.8 %collective-permute-start.4 = (bf16[24,8,128]{2,1,0:T(8,128)(2,1)S(1)}, bf16[24,8,128]{2,1,0:T(8,128)(2,1)S(1)}, u32[]{:S(2)}, u32[]{:S(2)}) collective-permute-start(bf16[24,8,128]{2,1,0:T(8,128)(2,1)S(1)} %pad_maximum_fusion.2), channel_id=1, source_target_pairs={{0,56},{8,0},{16,8},{24,16},{32,24},{40,32},{48,40},{56,48},{1,57}... | collective-permute-start | bytes 147464 | tf_op jit(solution)/shard_map/ppermute | solution.py:500
  32.4 3.5 %collective-permute-start.3 = (bf16[24,8,128]{2,1,0:T(8,128)(2,1)S(1)}, bf16[24,8,128]{2,1,0:T(8,128)(2,1)S(1)}, u32[]{:S(2)}, u32[]{:S(2)}) collective-permute-start(bf16[24,8,128]{2,1,0:T(8,128)(2,1)S(1)} %pad_maximum_fusion.1), channel_id=1, source_target_pairs={{0,8},{8,16},{16,24},{24,32},{32,40},{40,48},{48,56},{56,0},{1,9},... | collective-permute-start | bytes 147464 | tf_op jit(solution)/shard_map/ppermute | solution.py:500
  36.3 7.4 %collective-permute-start.5 = (bf16[48,128]{1,0:T(8,128)(2,1)S(1)}, bf16[48,128]{1,0:T(8,128)(2,1)S(1)}, u32[]{:S(2)}, u32[]{:S(2)}) collective-permute-start(bf16[48,128]{1,0:T(8,128)(2,1)S(1)} %get-tuple-element.70), channel_id=1, source_target_pairs={{0,71},{1,2},{2,1},{3,4},{4,3},{5,6},{6,5},{7,64},{64,7},{65,66},{... | collective-permute-start | bytes 36872 | tf_op jit(solution)/shard_map/ppermute | solution.py:503
  41.1 5.6 %collective-permute-start.6 = (bf16[48,128]{1,0:T(8,128)(2,1)S(1)}, bf16[48,128]{1,0:T(8,128)(2,1)S(1)}, u32[]{:S(2)}, u32[]{:S(2)}) collective-permute-start(bf16[48,128]{1,0:T(8,128)(2,1)S(1)} %get-tuple-element.69), channel_id=1, source_target_pairs={{0,1},{1,0},{2,3},{3,2},{4,5},{5,4},{6,7},{7,6},{64,65},{65,64},{6... | collective-permute-start | bytes 36872 | tf_op jit(solution)/shard_map/ppermute | solution.py:504

commit v6 on v5

--- a/solution.py
+++ b/solution.py
@@ -320,7 +320,7 @@
         together(skipped_planes(2 * t + 1, slot_b_ref), gather_first(2 * t + 2, slot_a_ref))
         return carry
 
-    lax.fori_loop(0, 4, two_steps, 0, unroll=2)
+    lax.fori_loop(0, 4, two_steps, 0, unroll=4)
     col4_ref[1152:1200] = jnp.zeros((48, COARSE_WIDTH), BF16)
     col5_ref[1728:1792] = jnp.zeros((64, RAISED_WIDTH), BF16)
     together(skipped_planes(8, slot_a_ref), gather_pool(range(7)))

time: 59.6 us -> 59.6 us (level)
  no operation moved by 1% of the time
where the time goes in v6:
time: 59.6 us; the launch traced here: 59.2 us
  starting transfers between devices  30.2 us (51%)
  Pallas kernels  15.9 us (27%)
  waiting for transfers between devices  9.55 us (16%)
  local copies, waits for them, and re-layouts  2.04 us (3%)
  other arithmetic  1.18 us (2%)
    ppermute x1, starting transfers between devices, exchange(): other = lax.ppermute(density, 'gx', [(i, i ^ 1) for i in range(8)])  15.9 us
    pallas_call x1, Pallas kernels, network(): pl.pallas_call(network_kernel, out_shape=jax.ShapeDtypeStruct((4, 16, 128...  12.6 us
    ppermute x1, starting transfers between devices, exchange(): a = lax.ppermute(mid, 'gx', swaps_y(True))  4.92 us
    ppermute x1, starting transfers between devices, exchange(): lax.ppermute(jnp.where(odd, right, left), ('gx', 'gz'), swaps_z(True))  4.76 us
    ppermute x1, waiting for transfers between devices, exchange(): b = lax.ppermute(mid, 'gx', swaps_y(False))  3.73 us
    ppermute x1, waiting for transfers between devices, exchange(): lax.ppermute(jnp.where(odd, left, right), ('gx', 'gz'), swaps_z(False))  2.77 us
    pallas_call x1, Pallas kernels, prepare_weights(): pl.pallas_call(weights_kernel, out_shape=[jax.ShapeDtypeStruct(s, BF16) f...  2.32 us
    ppermute x1, starting transfers between devices, exchange(): lax.ppermute(jnp.where(odd, left, right), ('gx', 'gz'), swaps_z(False))  2.1 us
  transfers between devices with their start and end apart: 7, of which 4 were waited for; matrix products, arithmetic and copies ran while one was open for 5% of the time, Pallas kernels for 5%

profile of v6, /device:TPU:6, one launch (start us, length us, event | category | flops | bytes accessed | tf_op | source)
XLA Modules:
  0.0 59.2 jit_solution(1635607258690409542)
XLA Ops:
  0.0 0.0 copy-start.3
  0.0 0.0 copy-start.4
  0.1 15.9 %collective-permute-start = (bf16[4,16,128]{2,1,0:T(8,128)(2,1)}, bf16[4,16,128]{2,1,0:T(8,128)(2,1)S(1)}, u32[]{:S(2)}, u32[]{:S(2)}) collective-permute-start(bf16[4,16,128]{2,1,0:T(8,128)(2,1)} %param.16), channel_id=1, source_target_pairs={{0,64},{64,0},{128,192},{192,128},{256,320},{320,256},{384,448},{4... | collective-permute-start | bytes 49160 | tf_op jit(solution)/shard_map/ppermute | solution.py:493
  16.0 1.1 %pad_maximum_fusion = bf16[3,3,3,16,32]{4,3,2,1,0:T(8,128)(2,1)S(1)} fusion(bf16[3,3,3,16,16]{4,3,2,1,0:T(8,128)(2,1)} %param.29, bf16[3,3,3,16,16]{4,3,2,1,0:T(8,128)(2,1)} %param.19), kind=kLoop, calls=%fused_computation | loop fusion | flops 55296 | bytes 55296 | tf_op jit(solution)/shard_map/concatenate | solution.py:515
  17.1 0.9 %constant_dynamic-update-slice_fusion.3 = bf16[2288,32]{1,0:T(8,128)(2,1)S(1)} fusion(bf16[2288,32]{1,0:T(8,128)(2,1)S(1)} %constant_dynamic-update-slice_fusion.4, bf16[432,32]{1,0:T(8,128)(2,1)} %bitcast.16), kind=kLoop, calls=%fused_computation.17 | loop fusion | bytes 138240
  18.0 0.9 %constant_dynamic-update-slice_fusion.2 = bf16[2288,32]{1,0:T(8,128)(2,1)S(1)} fusion(bf16[2288,32]{1,0:T(8,128)(2,1)S(1)} %constant_dynamic-update-slice_fusion.3, bf16[432,32]{1,0:T(8,128)(2,1)} %bitcast.17), kind=kLoop, calls=%fused_computation.16 | loop fusion | bytes 138240
  19.0 0.1 pad_add_fusion.place_ref
  19.1 0.0 copy-done.5
  19.1 0.0 copy-done.9
  19.1 0.0 copy-done.10
  19.1 0.0 copy-done.6
  19.2 0.0 copy-done.7
  19.2 0.0 copy-done.8
  19.2 0.0 copy-done.11
  19.2 0.1 concatenate.20
  19.3 2.3 %weights.1 = (bf16[512,256]{1,0:T(8,128)(2,1)S(1)}, bf16[192,256]{1,0:T(8,128)(2,1)S(1)}, bf16[96,768]{1,0:T(8,128)(2,1)S(1)}, bf16[128,1792]{1,0:T(8,128)(2,1)S...) custom-call(s32[3]{0:T(128)S(1)} %pad_add_fusion.place_ref, ...), custom_call_target="tpu_custom_call" | custom-call | flops 10000000 | bytes 2000000 | tf_op jit(solution)/shard_map/weights/pallas_call | solution.py:117
  21.6 0.0 collective-permute-done
  21.6 4.9 %collective-permute-start.1 = (bf16[8,16,128]{2,1,0:T(8,128)(2,1)S(1)}, bf16[8,16,128]{2,1,0:T(8,128)(2,1)S(1)}, u32[]{:S(2)}, u32[]{:S(2)}) collective-permute-start(bf16[8,16,128]{2,1,0:T(8,128)(2,1)S(1)} %pad_maximum_fusion.3.mid_ref), channel_id=1, source_target_pairs={{0,384},{64,448},{128,256},{192,320},{256,128},{320,192},{384,0},{... | collective-permute-start | bytes 98312 | tf_op jit(solution)/shard_map/ppermute | solution.py:496
  26.6 2.0 %collective-permute-start.2 = (bf16[8,16,128]{2,1,0:T(8,128)(2,1)S(1)}, bf16[8,16,128]{2,1,0:T(8,128)(2,1)S(1)}, u32[]{:S(2)}, u32[]{:S(2)}) collective-permute-start(bf16[8,16,128]{2,1,0:T(8,128)(2,1)S(1)} %pad_maximum_fusion.3.mid_ref), channel_id=1, source_target_pairs={{0,128},{64,192},{128,0},{192,64},{256,384},{320,448},{384,256},{4... | collective-permute-start | bytes 98312 | tf_op jit(solution)/shard_map/ppermute | solution.py:497
  28.6 0.0 collective-permute-done.1.a_ref
  28.7 3.7 %collective-permute-done.2.b_ref = bf16[8,16,128]{2,1,0:T(8,128)(2,1)S(1)} collective-permute-done((bf16[8,16,128]{2,1,0:T(8,128)(2,1)S(1)}, bf16[8,16,128]{2,1,0:T(8,128)(2,1)S(1)}, u32[]{:S(2)}, u32[]{:S(2)}) %collective-permute-start.2) | collective-permute-done | bytes 32800 | tf_op jit(solution)/shard_map/ppermute | solution.py:497
  32.4 0.0 collective-permute-start.4
  32.4 0.5 collective-permute-start.3
  32.9 1.2 %collective-permute-done.4.high_ref = bf16[24,8,128]{2,1,0:T(8,128)(2,1)S(1)} collective-permute-done((bf16[24,8,128]{2,1,0:T(8,128)(2,1)S(1)}, bf16[24,8,128]{2,1,0:T(8,128)(2,1)S(1)}, u32[]{:S(2)}, u32[]{:S(2)}) %collective-permute-start.4) | collective-permute-done | bytes 49184 | tf_op jit(solution)/shard_map/ppermute | solution.py:500
  34.2 1.8 %collective-permute-done.3.low_ref = bf16[24,8,128]{2,1,0:T(8,128)(2,1)S(1)} collective-permute-done((bf16[24,8,128]{2,1,0:T(8,128)(2,1)S(1)}, bf16[24,8,128]{2,1,0:T(8,128)(2,1)S(1)}, u32[]{:S(2)}, u32[]{:S(2)}) %collective-permute-start.3) | collective-permute-done | bytes 49184 | tf_op jit(solution)/shard_map/ppermute | solution.py:500
  36.0 0.3 edges.1
  36.3 4.8 %collective-permute-start.5 = (bf16[48,128]{1,0:T(8,128)(2,1)S(1)}, bf16[48,128]{1,0:T(8,128)(2,1)S(1)}, u32[]{:S(2)}, u32[]{:S(2)}) collective-permute-start(bf16[48,128]{1,0:T(8,128)(2,1)S(1)} %get-tuple-element.70), channel_id=1, source_target_pairs={{0,71},{1,2},{2,1},{3,4},{4,3},{5,6},{6,5},{7,64},{64,7},{65,66},{... | collective-permute-start | bytes 36872 | tf_op jit(solution)/shard_map/ppermute | solution.py:503
  41.1 2.1 %collective-permute-start.6 = (bf16[48,128]{1,0:T(8,128)(2,1)S(1)}, bf16[48,128]{1,0:T(8,128)(2,1)S(1)}, u32[]{:S(2)}, u32[]{:S(2)}) collective-permute-start(bf16[48,128]{1,0:T(8,128)(2,1)S(1)} %get-tuple-element.69), channel_id=1, source_target_pairs={{0,1},{1,0},{2,3},{3,2},{4,5},{5,4},{6,7},{7,6},{64,65},{65,64},{6... | collective-permute-start | bytes 36872 | tf_op jit(solution)/shard_map/ppermute | solution.py:504
  43.2 0.7 %sample.1.center_ref = f32[4,24,1152]{2,1,0:T(8,128)S(1)} custom-call(f32[768,128]{1,0:T(8,128)S(1)} %get-tuple-element.47.cells_ref, bf16[128,256]{1,0:T(8,128)(2,1)S(1)} %get-tuple-element.48.sz_ref), custom_call_target="tpu_custom_call" | custom-call | flops 100000000 | bytes 1000000 | tf_op jit(solution)/shard_map/sample/pallas_call | solution.py:184
  43.9 0.0 collective-permute-done.5.edge_a_ref
  43.9 2.8 %collective-permute-done.6.edge_b_ref = bf16[48,128]{1,0:T(8,128)(2,1)S(1)} collective-permute-done((bf16[48,128]{1,0:T(8,128)(2,1)S(1)}, bf16[48,128]{1,0:T(8,128)(2,1)S(1)}, u32[]{:S(2)}, u32[]{:S(2)}) %collective-permute-start.6) | collective-permute-done | bytes 12320 | tf_op jit(solution)/shard_map/ppermute | solution.py:504
  46.7 12.6 %network.1 = f32[4,16,128]{2,1,0:T(8,128)} custom-call(f32[2,8,128]{2,1,0:T(8,128)S(1)} %get-tuple-element.45.flags_ref, f32[4,24,1152]{2,1,0:T(8,128)S(1)} %sample.1.center_ref, bf16[48,128]{1,0:T(8,128)(2,1)S(1)} %collective-permute-done.5.edge_a_ref, bf16[48,128]{1,0:T(8,128)(2,1)S(1)} %collective-permute-done.6.edge_b_ref, ...), custom_call_target="tpu_custom_call" | custom-call | flops 4000000000 | bytes 4000000 | tf_op jit(solution)/shard_map/network/pallas_call | solution.py:459
  (27 shorter events, 0.2 us)
Async XLA Ops:
  0.0 21.6 %copy-start.2 = (bf16[4,16,128]{2,1,0:T(8,128)(2,1)S(1)}, bf16[4,16,128]{2,1,0:T(8,128)(2,1)}, u32[]{:S(2)}) copy-start(bf16[4,16,128]{2,1,0:T(8,128)(2,1)} %param.16) | copy-start | bytes 49156
  0.0 18.9 %copy-start = (bf16[3,3,3,32,32]{4,3,2,1,0:T(8,128)(2,1)S(1)}, bf16[3,3,3,32,32]{4,3,2,1,0:T(8,128)(2,1)}, u32[]{:S(2)}) copy-start(bf16[3,3,3,32,32]{4,3,2,1,0:T(8,128)(2,1)} %param.23) | copy-start | bytes 165892
  0.0 19.0 %copy-start.1 = (bf16[2,2,2,16,32]{4,3,2,1,0:T(8,128)(2,1)S(1)}, bf16[2,2,2,16,32]{4,3,2,1,0:T(8,128)(2,1)}, u32[]{:S(2)}) copy-start(bf16[2,2,2,16,32]{4,3,2,1,0:T(8,128)(2,1)} %param.25) | copy-start | bytes 24580
  0.0 19.1 %copy-start.3 = (bf16[3,3,3,16,1]{3,2,4,1,0:T(4,128)(2,1)S(1)}, bf16[3,3,3,16,1]{3,2,4,1,0:T(4,128)(2,1)}, u32[]{:S(2)}) copy-start(bf16[3,3,3,16,1]{3,2,4,1,0:T(4,128)(2,1)} %param.17) | copy-start | bytes 2596
  0.0 19.1 %copy-start.4 = (f32[16]{0:T(128)S(1)}, f32[16]{0:T(128)}, u32[]{:S(2)}) copy-start(f32[16]{0:T(128)} %param.18) | copy-start | bytes 196
  0.0 19.1 %copy-start.5 = (f32[16]{0:T(128)S(1)}, f32[16]{0:T(128)}, u32[]{:S(2)}) copy-start(f32[16]{0:T(128)} %param.20) | copy-start | bytes 196
  0.0 19.1 %copy-start.9 = (f32[32]{0:T(128)S(1)}, f32[32]{0:T(128)}, u32[]{:S(2)}) copy-start(f32[32]{0:T(128)} %param.22) | copy-start | bytes 388
  0.0 19.1 %copy-start.10 = (f32[32]{0:T(128)S(1)}, f32[32]{0:T(128)}, u32[]{:S(2)}) copy-start(f32[32]{0:T(128)} %param.24) | copy-start | bytes 388
  0.1 19.1 %copy-start.6 = (f32[16]{0:T(128)S(1)}, f32[16]{0:T(128)}, u32[]{:S(2)}) copy-start(f32[16]{0:T(128)} %param.26) | copy-start | bytes 196
  0.1 19.1 %copy-start.7 = (f32[16]{0:T(128)S(1)}, f32[16]{0:T(128)}, u32[]{:S(2)}) copy-start(f32[16]{0:T(128)} %param.28) | copy-start | bytes 196
  0.1 19.1 %copy-start.8 = (f32[16]{0:T(128)S(1)}, f32[16]{0:T(128)}, u32[]{:S(2)}) copy-start(f32[16]{0:T(128)} %param.30) | copy-start | bytes 196
  0.1 19.1 %copy-start.11 = (bf16[16]{0:T(256)(128)(2,1)S(1)}, bf16[16]{0:T(256)(128)(2,1)}, u32[]{:S(2)}) copy-start(bf16[16]{0:T(256)(128)(2,1)} %param.31) | copy-start | bytes 100
  0.1 21.5 %collective-permute-start = (bf16[4,16,128]{2,1,0:T(8,128)(2,1)}, bf16[4,16,128]{2,1,0:T(8,128)(2,1)S(1)}, u32[]{:S(2)}, u32[]{:S(2)}) collective-permute-start(bf16[4,16,128]{2,1,0:T(8,128)(2,1)} %param.16), channel_id=1, source_target_pairs={{0,64},{64,0},{128,192},{192,128},{256,320},{320,256},{384,448},{4... | collective-permute-start | bytes 49160 | tf_op jit(solution)/shard_map/ppermute | solution.py:493
  21.6 7.0 %collective-permute-start.1 = (bf16[8,16,128]{2,1,0:T(8,128)(2,1)S(1)}, bf16[8,16,128]{2,1,0:T(8,128)(2,1)S(1)}, u32[]{:S(2)}, u32[]{:S(2)}) collective-permute-start(bf16[8,16,128]{2,1,0:T(8,128)(2,1)S(1)} %pad_maximum_fusion.3.mid_ref), channel_id=1, source_target_pairs={{0,384},{64,448},{128,256},{192,320},{256,128},{320,192},{384,0},{... | collective-permute-start | bytes 98312 | tf_op jit(solution)/shard_map/ppermute | solution.py:496
  26.6 5.8 %collective-permute-start.2 = (bf16[8,16,128]{2,1,0:T(8,128)(2,1)S(1)}, bf16[8,16,128]{2,1,0:T(8,128)(2,1)S(1)}, u32[]{:S(2)}, u32[]{:S(2)}) collective-permute-start(bf16[8,16,128]{2,1,0:T(8,128)(2,1)S(1)} %pad_maximum_fusion.3.mid_ref), channel_id=1, source_target_pairs={{0,128},{64,192},{128,0},{192,64},{256,384},{320,448},{384,256},{4... | collective-permute-start | bytes 98312 | tf_op jit(solution)/shard_map/ppermute | solution.py:497
  32.4 1.8 %collective-permute-start.4 = (bf16[24,8,128]{2,1,0:T(8,128)(2,1)S(1)}, bf16[24,8,128]{2,1,0:T(8,128)(2,1)S(1)}, u32[]{:S(2)}, u32[]{:S(2)}) collective-permute-start(bf16[24,8,128]{2,1,0:T(8,128)(2,1)S(1)} %pad_maximum_fusion.2), channel_id=1, source_target_pairs={{0,56},{8,0},{16,8},{24,16},{32,24},{40,32},{48,40},{56,48},{1,57}... | collective-permute-start | bytes 147464 | tf_op jit(solution)/shard_map/ppermute | solution.py:500
  32.4 3.5 %collective-permute-start.3 = (bf16[24,8,128]{2,1,0:T(8,128)(2,1)S(1)}, bf16[24,8,128]{2,1,0:T(8,128)(2,1)S(1)}, u32[]{:S(2)}, u32[]{:S(2)}) collective-permute-start(bf16[24,8,128]{2,1,0:T(8,128)(2,1)S(1)} %pad_maximum_fusion.1), channel_id=1, source_target_pairs={{0,8},{8,16},{16,24},{24,32},{32,40},{40,48},{48,56},{56,0},{1,9},... | collective-permute-start | bytes 147464 | tf_op jit(solution)/shard_map/ppermute | solution.py:500
  36.3 7.6 %collective-permute-start.5 = (bf16[48,128]{1,0:T(8,128)(2,1)S(1)}, bf16[48,128]{1,0:T(8,128)(2,1)S(1)}, u32[]{:S(2)}, u32[]{:S(2)}) collective-permute-start(bf16[48,128]{1,0:T(8,128)(2,1)S(1)} %get-tuple-element.70), channel_id=1, source_target_pairs={{0,71},{1,2},{2,1},{3,4},{4,3},{5,6},{6,5},{7,64},{64,7},{65,66},{... | collective-permute-start | bytes 36872 | tf_op jit(solution)/shard_map/ppermute | solution.py:503
  41.1 5.6 %collective-permute-start.6 = (bf16[48,128]{1,0:T(8,128)(2,1)S(1)}, bf16[48,128]{1,0:T(8,128)(2,1)S(1)}, u32[]{:S(2)}, u32[]{:S(2)}) collective-permute-start(bf16[48,128]{1,0:T(8,128)(2,1)S(1)} %get-tuple-element.69), channel_id=1, source_target_pairs={{0,1},{1,0},{2,3},{3,2},{4,5},{5,4},{6,7},{7,6},{64,65},{65,64},{6... | collective-permute-start | bytes 36872 | tf_op jit(solution)/shard_map/ppermute | solution.py:504
